TPU v7x, 768 devices: a whole 4x8x12 slice. The times are simulated.
768 devices in a mesh: section: 96 (over z, x, core), ep: 8 (over y).
Axes of the slice: x: 4, y: 8, z: 12, core: 2. Of those that a mesh axis runs over, the one named last changes fastest.
Arguments:
- tokens: bfloat16 [2048, 1440], P('ep', 'section'), may hold values from -6 to 6
- grad_out: bfloat16 [2048, 1440], P('ep', 'section'), may hold values from -6 to 6
- expert_ids: int32 [2048, 4], P('ep'), may hold values from 0 to 7, all different within a row; in each aligned block of 256 rows (0 to 255, 256 to 511, ...) at most 192 rows name the same one
- probs: float32 [2048, 4], P('ep'), may hold values from 0.05 to 1
- w_gate: bfloat16 [8, 1440, 2880], P('ep', None, 'section'), may hold values from -0.15625 to 0.15625
- w_up: bfloat16 [8, 1440, 2880], P('ep', None, 'section'), may hold values from -0.15625 to 0.15625
- w_down: bfloat16 [8, 2880, 1440], P('ep', 'section'), may hold values from -0.109375 to 0.109375
Outputs:
- grad_gate: bfloat16 [8, 1440, 2880], P('ep', None, 'section')
- grad_up: bfloat16 [8, 1440, 2880], P('ep', None, 'section')
- grad_down: bfloat16 [8, 2880, 1440], P('ep', 'section')
Inputs may be any that keep to these rules, and one draw needn't show every extreme that they name: `expert_ids`: among the picks of the 256 tokens of one index of ep, no expert is named more than 192 times, and the 4 experts of a token differ.
All inputs are finite; a program needn't handle non-finite values.
Results may differ from a plain program's by a relative error of at most 0.0065.
Values may be sent and summed in bfloat16 or wider, within the bound.
No kernel may reach another device: no remote copies, remote signals or barrier semaphores. Data moves between devices by JAX's collectives and lax.ppermute only.
A program may use at most 64 MiB of HBM per device.

v0:
```python
import jax
import jax.numpy as jnp
from jax import lax
from jax.sharding import PartitionSpec as P


def rounded(value):
    return lax.optimization_barrier(value.astype(jnp.bfloat16)).astype(jnp.float32)


def slot_grads(inputs, scaled, gate_w, up_w, down_w):
    gate = jnp.einsum("hpscd,sdf->hpscf", inputs, gate_w, preferred_element_type=jnp.float32)
    linear = jnp.einsum("hpscd,sdf->hpscf", inputs, up_w, preferred_element_type=jnp.float32)
    sigma = jax.nn.sigmoid(gate)
    hidden = (gate * sigma * linear).astype(jnp.bfloat16)
    grad_hidden = jnp.einsum("hpscd,sfd->hpscf", scaled, down_w, preferred_element_type=jnp.float32)
    gate_term = (grad_hidden * linear * sigma * (1.0 + gate * (1.0 - sigma))).astype(jnp.bfloat16)
    linear_term = (grad_hidden * gate * sigma).astype(jnp.bfloat16)
    part_gate = rounded(
        jnp.einsum("hpscd,hpscf->hsdf", inputs, gate_term, preferred_element_type=jnp.float32)
    )
    part_up = rounded(
        jnp.einsum("hpscd,hpscf->hsdf", inputs, linear_term, preferred_element_type=jnp.float32)
    )
    part_down = rounded(
        jnp.einsum("hpscf,hpscd->hsfd", hidden, scaled, preferred_element_type=jnp.float32)
    )
    return (part_gate, part_up, part_down)


def shards(tokens, grad_out, expert_ids, probs, w_gate, w_up, w_down):
    n_ep = lax.axis_size("ep")
    half = n_ep // 2
    tok_dev, top = expert_ids.shape
    picks = tok_dev * top
    capacity = max(2, (3 * picks + 2 * n_ep - 1) // (2 * n_ep))
    flat_ids = expert_ids.reshape(picks)
    owners = jnp.arange(n_ep, dtype=jnp.int32)
    slots = 1
    matches = (flat_ids[:, None] == owners[None, :]).astype(jnp.int32)
    rank = jnp.sum(jnp.cumsum(matches, axis=0) * matches, axis=1) - 1
    position = flat_ids * slots * capacity + rank
    width = tokens.shape[1]
    rows = jnp.repeat(tokens, top, axis=0)
    scaled = (
        probs.reshape(picks, 1) * jnp.repeat(grad_out, top, axis=0).astype(jnp.float32)
    ).astype(jnp.bfloat16)
    buffer_rows = n_ep * slots * capacity
    send_rows = jnp.zeros((buffer_rows, width), jnp.bfloat16).at[position].set(rows)
    send_scaled = jnp.zeros((buffer_rows, width), jnp.bfloat16).at[position].set(scaled)
    send_rows = send_rows.reshape(n_ep, slots * capacity, width)
    send_scaled = send_scaled.reshape(n_ep, slots * capacity, width)
    got_rows, got_scaled = (
        lax.all_to_all(send_rows, "ep", split_axis=0, concat_axis=0, tiled=True),
        lax.all_to_all(send_scaled, "ep", split_axis=0, concat_axis=0, tiled=True),
    )
    got_rows = got_rows.reshape(2, half, slots, capacity, width)
    got_scaled = got_scaled.reshape(2, half, slots, capacity, width)
    inputs, scaled_rows = (
        lax.all_gather(got_rows, "section", axis=4, tiled=True),
        lax.all_gather(got_scaled, "section", axis=4, tiled=True),
    )
    part_gate, part_up, part_down = slot_grads(inputs, scaled_rows, w_gate, w_up, w_down)
    grad_gate = (part_gate[0] + part_gate[1]).astype(jnp.bfloat16)
    grad_up = (part_up[0] + part_up[1]).astype(jnp.bfloat16)
    grad_down = (part_down[0] + part_down[1]).astype(jnp.bfloat16)
    return (grad_gate, grad_up, grad_down)


def solution(mesh):
    placed = (
        P("ep", "section"),
        P("ep", "section"),
        P("ep", None),
        P("ep", None),
        P("ep", None, "section"),
        P("ep", None, "section"),
        P("ep", "section", None),
    )
    return jax.shard_map(
        shards,
        mesh=mesh,
        in_specs=placed,
        out_specs=(P("ep", None, "section"), P("ep", None, "section"), P("ep", "section", None)),
        check_vma=False,
    )
```

profile of v0, /device:TPU:1, one launch (start us, length us, event | category | flops | bytes accessed | tf_op | source)
XLA Modules:
  0.0 305.5 jit_solution(7395464064081609958)
XLA Ops:
  7.2 0.0 copy-start
  7.2 0.0 all-gather.3.cloned.1.call-start
  7.2 0.7 broadcast_multiply_fusion
  7.9 0.8 copy.39
  8.7 0.1 eq.29
  8.9 0.1 eq.25
  9.0 0.1 copy.38
  9.1 0.1 mul.55
  9.3 2.3 reduce-window.6
  11.5 0.3 slice_reduce_fusion
  11.8 0.2 reduce-window.9
  12.0 0.1 add_bitcast_fusion
  12.1 0.8 copy.41
  12.9 0.1 broadcast_in_dim.4
  13.0 3.3 %scatter_custom_fusion = bf16[1536,15]{1,0:T(8,128)(2,1)S(1)} fusion(s32[1024]{0:T(1024)S(1)} %bitcast.152, bf16[1024,15]{1,0:T(8,128)(2,1)S(1)} %bitcast.147, bf16[]{:T(256)} %constant.6.clone.1), kind=kCustom, calls=%fused_computation.40 | custom fusion | bytes 46082 | tf_op jit(solution)/shard_map/scatter | solution.py:49
  16.3 0.2 copy.43
  16.5 14.7 %all_to_all.10 = bf16[8,192,15]{1,2,0:T(8,128)(2,1)S(1)} all-to-all(bf16[8,192,15]{1,2,0:T(8,128)(2,1)S(1)} %copy.43), channel_id=1, replica_groups=mesh['section'=96,'ep'=8] {'ep'}, dimensions={0} | all-to-all | bytes 92160 | tf_op jit(solution)/shard_map/all_to_all | solution.py:54
  31.2 0.7 copy.44
  31.9 0.0 all-gather.3.cloned.1.call-update
  31.9 0.0 all-gather.5.cloned.1.call-start
  31.9 0.8 copy.47
  32.8 0.8 copy.46
  33.6 0.1 mul.57
  33.7 0.1 broadcast_in_dim.10
  33.8 3.8 %scatter_custom_fusion.1 = bf16[1536,15]{1,0:T(8,128)(2,1)S(1)} fusion(s32[1024]{0:T(1024)S(1)} %bitcast.153, f32[1024,15]{1,0:T(8,128)S(1)} %bitcast.144, f32[1024]{0:T(1024)S(1)} %mul.57, bf16[]{:T(256)} %constant.6.clone.1), kind=kCustom, calls=%fused_computation.27 | custom fusion | flops 30720 | bytes 574466 | tf_op jit(solution)/shard_map/scatter | solution.py:50
  37.6 0.2 copy.49
  37.8 9.6 %all_to_all.11 = bf16[8,192,15]{1,2,0:T(8,128)(2,1)S(1)} all-to-all(bf16[8,192,15]{1,2,0:T(8,128)(2,1)S(1)} %copy.49), channel_id=1, replica_groups=mesh['section'=96,'ep'=8] {'ep'}, dimensions={0} | all-to-all | bytes 92160 | tf_op jit(solution)/shard_map/all_to_all | solution.py:55
  47.4 0.7 copy.50
  48.1 0.0 all-gather.5.cloned.1.call-update
  48.1 106.9 %all-gather.3.cloned.1.call-done = bf16[2,4,1,192,1440]{3,1,2,0,4:T(4,128)(2,1)} async-done(((bf16[2,4,1,192,15]{3,1,2,0,4:T(4,128)(2,1)}), bf16[2,4,1,192,1440]{3,1,2,0,4:T(4,128)(2,1)}) %all-gather.3.cloned.1.call-update) | async-done | bytes 4423696 | tf_op jit(solution)/shard_map/all_gather | solution.py:60
  155.0 10.2 %copy.45 = bf16[2,4,1,192,1440]{4,3,1,0,2:T(8,128)(2,1)} copy(bf16[2,4,1,192,1440]{3,1,2,0,4:T(4,128)(2,1)} %all-gather.3.cloned.1.call-done) | data formatting | bytes 8847360 | tf_op jit(solution)/shard_map/all_gather | solution.py:60
  165.2 0.0 copy-done
  165.2 0.0 copy-start.1
  165.2 0.0 copy-start.2
  165.2 4.0 %fusion.42 = f32[2,4,1,192,30]{3,4,1,0,2:T(8,128)S(1)} fusion(bf16[2,4,1,192,1440]{4,3,1,0,2:T(8,128)(2,1)} %copy.45, bf16[1,1440,30]{1,2,0:T(8,128)(2,1)S(1)} %copy-done), kind=kOutput, calls=%fused_computation.24 | convolution fusion | flops 132710400 | bytes 4694400 | tf_op jit(solution)/shard_map/hpscd,sdf->hpscf/dot_general | solution.py:12
  169.2 0.0 copy-done.1
  169.2 0.0 copy-done.2
  169.2 1.5 fusion.39
  170.7 0.0 copy-start.3
  170.7 104.5 %all-gather.5.cloned.1.call-done = bf16[2,4,1,192,1440]{3,1,2,0,4:T(4,128)(2,1)} async-done(((bf16[2,4,1,192,15]{3,1,2,0,4:T(4,128)(2,1)}), bf16[2,4,1,192,1440]{3,1,2,0,4:T(4,128)(2,1)}) %all-gather.5.cloned.1.call-update) | async-done | bytes 4423696 | tf_op jit(solution)/shard_map/all_gather | solution.py:61
  275.3 10.2 %copy.51 = bf16[2,4,1,192,1440]{4,3,1,0,2:T(8,128)(2,1)} copy(bf16[2,4,1,192,1440]{3,1,2,0,4:T(4,128)(2,1)} %all-gather.5.cloned.1.call-done) | data formatting | bytes 8847360 | tf_op jit(solution)/shard_map/all_gather | solution.py:61
  285.5 0.0 copy-done.3
  285.5 0.0 slice-start
  285.5 4.0 %fusion.45 = f32[2,4,1,192,30]{3,4,1,0,2:T(8,128)S(1)} fusion(bf16[2,4,1,192,1440]{4,3,1,0,2:T(8,128)(2,1)} %copy.51, bf16[1,30,1440]{2,1,0:T(8,128)(2,1)S(1)} %copy-done.3), kind=kOutput, calls=%fused_computation.25 | convolution fusion | flops 132710400 | bytes 4694400 | tf_op jit(solution)/shard_map/hpscd,sfd->hpscf/dot_general | solution.py:16
  289.5 0.0 slice-start.1
  289.5 3.4 %fusion.33 = bf16[2,1,1440,30]{2,3,0,1:T(8,128)(2,1)S(1)} fusion(bf16[2,4,1,192,1440]{4,3,1,0,2:T(8,128)(2,1)} %copy.45, f32[2,4,1,192,30]{3,4,1,0,2:T(8,128)S(1)} %fusion.45, f32[2,4,1,192,30]{3,4,1,0,2:T(8,128)S(1)} %fusion.42), kind=kOutput, calls=%fused_computation.21 | convolution fusion | flops 133073280 | bytes 4965120 | tf_op jit(solution)/shard_map/hpscd,hpscf->hsdf/dot_general | solution.py:23
  292.9 3.3 %fusion.30 = bf16[2,1,1440,30]{2,3,0,1:T(8,128)(2,1)S(1)} fusion(bf16[2,4,1,192,1440]{4,3,1,0,2:T(8,128)(2,1)} %copy.45, f32[2,4,1,192,30]{3,4,1,0,2:T(8,128)S(1)} %fusion.42, f32[2,4,1,192,30]{3,4,1,0,2:T(8,128)S(1)} %fusion.45, f32[2,4,1,192,30]{3,4,1,0,2:T(8,128)S(1)} %fusion.39), kind=kOutput, calls=%fused_computation.20 | convolution fusion | flops 133257600 | bytes 5149440 | tf_op jit(solution)/shard_map/hpscd,hpscf->hsdf/dot_general | solution.py:20
  296.1 0.0 slice-done
  296.2 0.0 slice-done.1
  296.2 1.0 fusion.36
  297.3 0.7 fusion.61
  297.9 0.7 fusion.59
  (8 shorter events, 0.1 us)
Async XLA Ops:
  7.2 158.0 %copy-start = (bf16[1,1440,30]{1,2,0:T(8,128)(2,1)S(1)}, bf16[1,1440,30]{1,2,0:T(8,128)(2,1)}, u32[]{:S(2)}) copy-start(bf16[1,1440,30]{1,2,0:T(8,128)(2,1)} %param.11) | copy-start | bytes 259204
  7.2 147.8 %all-gather.3.cloned.1.call-start = ((), (), s32[]{:S(2)}) async-start(), calls=%async_computation.2 | async-start | bytes 5959680 | tf_op jit(solution)/shard_map/all_gather | solution.py:60
  31.9 243.4 %all-gather.5.cloned.1.call-start = ((), (), s32[]{:S(2)}) async-start(), calls=%async_computation.3 | async-start | bytes 5959680 | tf_op jit(solution)/shard_map/all_gather | solution.py:61
  165.2 4.0 %copy-start.1 = (bf16[2,4,1,192,1440]{4,3,1,0,2:T(8,128)(2,1)S(1)}, bf16[2,4,1,192,1440]{4,3,1,0,2:T(8,128)(2,1)}, u32[]{:S(2)}) copy-start(bf16[2,4,1,192,1440]{4,3,1,0,2:T(8,128)(2,1)} %copy.45) | copy-start | bytes 13271044
  165.2 4.0 %copy-start.2 = (bf16[1,1440,30]{1,2,0:T(8,128)(2,1)S(1)}, bf16[1,1440,30]{1,2,0:T(8,128)(2,1)}, u32[]{:S(2)}) copy-start(bf16[1,1440,30]{1,2,0:T(8,128)(2,1)} %param.12) | copy-start | bytes 259204
  170.7 114.8 %copy-start.3 = (bf16[1,30,1440]{2,1,0:T(8,128)(2,1)S(1)}, bf16[1,30,1440]{2,1,0:T(8,128)(2,1)}, u32[]{:S(2)}) copy-start(bf16[1,30,1440]{2,1,0:T(8,128)(2,1)} %param.13) | copy-start | bytes 259204
  285.5 10.6 %slice-start = ((s8[4718592]{0:T(1024)(128)(4,1)}), s8[4194304]{0:T(1024)(128)(4,1)S(1)}, s32[]{:S(2)}) async-start(s8[4718592]{0:T(1024)(128)(4,1)} %bitcast.142), calls=%async_computation.4 | async-start | bytes 8388608
  289.5 6.7 %slice-start.1 = ((s8[4718592]{0:T(1024)(128)(4,1)}), s8[524288]{0:T(1024)(128)(4,1)S(1)}, s32[]{:S(2)}) async-start(s8[4718592]{0:T(1024)(128)(4,1)} %bitcast.142), calls=%async_computation.5 | async-start | bytes 1048576
Sparse Core Ops, SparseCore 0:
  32.0 122.8 all-gather.2
  159.2 116.0 all-gather.4
where the time goes:
time: 306 us; the launch traced here: 305 us
  waiting for transfers between devices  211 us (69%)
  local copies, waits for them, and re-layouts  29.9 us (10%)
  blocking collectives  24.3 us (8%)
  matrix products  17.1 us (6%)
  between operations  14.2 us (5%)
  other arithmetic  8.49 us (3%)
    all_gather x1, waiting for transfers between devices, shards(): lax.all_gather(got_rows, 'section', axis=4, tiled=True)  107 us
    all_gather x1, waiting for transfers between devices, shards(): lax.all_gather(got_scaled, 'section', axis=4, tiled=True)  105 us
    all_to_all x1, blocking collectives, shards(): lax.all_to_all(send_rows, 'ep', split_axis=0, concat_axis=0, tiled=True)  14.7 us
    all_gather x1, local copies, waits for them, and re-layouts, shards(): lax.all_gather(got_rows, 'section', axis=4, tiled=True)  10.2 us
    all_gather x1, local copies, waits for them, and re-layouts, shards(): lax.all_gather(got_scaled, 'section', axis=4, tiled=True)  10.2 us
    all_to_all x1, blocking collectives, shards(): lax.all_to_all(send_scaled, 'ep', split_axis=0, concat_axis=0, tiled=True)  9.6 us
  transfers between devices with their start and end apart: 2, of which 2 were waited for; matrix products, arithmetic and copies ran while one was open for 7% of the time, Pallas kernels for 0%

commit v1 on v0

v1 whole, which is shorter than its diff:
```python
import functools

import jax
import jax.numpy as jnp
from jax import lax
from jax.experimental import pallas as pl
from jax.experimental.pallas import tpu as pltpu
from jax.sharding import Mesh, PartitionSpec as P

BF16, F32 = jnp.bfloat16, jnp.float32
CORES = 2
CHIPS_X = 4
PAIR = 2
LANES = 128
SEC = ("z", "x", "core")
EP = ("yo", "yi")


def dot(a, b):
    return jnp.dot(a, b, preferred_element_type=F32)


def dot_t(a, b):
    return lax.dot_general(a, b, (((1,), (1,)), ((), ())), preferred_element_type=F32)


def spread(narrow_lane, wide_lane):
    return (narrow_lane == wide_lane - (wide_lane >> 4)) & ((wide_lane & 15) != 15)


def widen(rows, wide):
    narrow = rows.shape[1]
    pieces = []
    for start in range(0, wide, LANES):
        low = start - start // 16
        low = low // LANES * LANES
        high = min(narrow, low + 2 * LANES)
        source = lax.broadcasted_iota(jnp.int32, (high - low, LANES), 0) + low
        target = lax.broadcasted_iota(jnp.int32, (high - low, LANES), 1) + start
        chosen = spread(source, target).astype(F32).astype(BF16)
        pieces.append(dot(rows[:, low:high], chosen).astype(BF16))
    return jnp.concatenate(pieces, axis=1)


def narrowed(rows, narrow):
    wide = rows.shape[1]
    pieces = []
    for start in range(0, narrow, LANES):
        width = min(LANES, narrow - start)
        low = start // 15 * 16 // LANES * LANES
        last = start + width - 1
        high = min(wide, -(-(last // 15 * 16 + last % 15 + 1) // LANES) * LANES)
        source = lax.broadcasted_iota(jnp.int32, (high - low, width), 0) + low
        target = lax.broadcasted_iota(jnp.int32, (high - low, width), 1) + start
        chosen = spread(target, source).astype(F32).astype(BF16)
        pieces.append(dot(rows[:, low:high], chosen).astype(BF16))
    return jnp.concatenate(pieces, axis=1)


def pack_kernel(place, tokens, cotangent, ids, probs, out):
    width, count = tokens.shape
    mine = ids[...] == place[0]
    weight = jnp.sum(jnp.where(mine, probs[...], 0.0), axis=0, keepdims=True)
    high = weight.astype(BF16).astype(F32)
    low = weight - high
    left = jnp.concatenate([tokens[...].astype(F32), high], axis=0)
    right = jnp.concatenate([cotangent[...].astype(F32), low], axis=0)
    out[:, :count] = left.astype(BF16)
    out[:, count:] = right.astype(BF16)


def weights_kernel(gate_w, up_w, down_w, out):
    hidden, wide = out.shape[0] // 3, out.shape[1]
    units = gate_w.shape[0]
    filler = jnp.zeros((hidden - units, gate_w.shape[1]), F32)
    rows = []
    for ref in (gate_w, up_w, down_w):
        rows += [ref[...].astype(F32), filler]
    out[...] = widen(jnp.concatenate(rows, axis=0).astype(BF16), wide)


def grads_kernel(place, own, other, weights, out, inputs, cotangents, sems):
    chips_x, chips_z, pair, depth, both = own.shape
    count = both // 2
    groups, stacked, wide = weights.shape
    hidden = stacked // 3
    core, yi = place[0], place[1]
    copies = []
    for s, ref in enumerate((own, other)):
        slot = core if s == 0 else 1 - core
        for x in range(chips_x):
            for y in range(pair):
                for k, held in enumerate((inputs, cotangents)):
                    copies.append(
                        pltpu.make_async_copy(
                            ref.at[x, :, y, :, pl.ds(k * count, count)],
                            held.at[:, x * CORES + slot, :, pl.ds(y * count, count)],
                            sems.at[s, x, y, k],
                        )
                    )
    for copy in copies:
        copy.start()
    for copy in copies:
        copy.wait()
    total = pair * count
    rows = inputs[...].reshape(wide, total)
    backs = cotangents[...].reshape(wide, total)

    def part(k):
        return weights[:, k * hidden : (k + 1) * hidden, :].reshape(groups * hidden, wide)

    gate = dot(part(0), rows)
    linear = dot(part(1), rows)
    back = dot(part(2), backs)
    shares = []
    for j in range(groups):
        high = inputs[j * PAIR + yi, 0].astype(F32)[depth - 1 : depth]
        low = cotangents[j * PAIR + yi, 0].astype(F32)[depth - 1 : depth]
        shares.append(jnp.broadcast_to(high + low, (hidden, total)))
    share = jnp.concatenate(shares, axis=0)
    back = back * share
    sigma = jax.nn.sigmoid(gate)
    lifted = (gate * sigma * linear * share).astype(BF16)
    gate_term = (back * linear * sigma * (1.0 + gate * (1.0 - sigma))).astype(BF16)
    linear_term = (back * gate * sigma).astype(BF16)
    for k, (left, right) in enumerate(((gate_term, rows), (linear_term, rows), (lifted, backs))):
        grad = dot_t(left, right).astype(BF16)
        out[:, k * hidden : (k + 1) * hidden, :] = grad.reshape(groups, hidden, wide)


def total_kernel(parts, gate_g, up_g, down_g):
    hidden = parts.shape[1] // 3
    total = parts[0].astype(F32)
    for j in range(1, parts.shape[0]):
        total = total + parts[j].astype(F32)
    units, narrow = gate_g.shape
    slim = narrowed(total.astype(BF16), narrow).astype(F32)
    for k, ref in enumerate((gate_g, up_g, down_g)):
        ref[...] = slim[k * hidden : k * hidden + units].astype(BF16)


VMEM = pl.BlockSpec(memory_space=pltpu.VMEM)
SMEM = pl.BlockSpec(memory_space=pltpu.SMEM)
ANY = pl.BlockSpec(memory_space=pl.ANY)
PARAMS = pltpu.CompilerParams(vmem_limit_bytes=40 * 1024 * 1024)


def swap(value, axis):
    return lax.ppermute(value, axis, [(0, 1), (1, 0)])


def shards(tokens, grad_out, expert_ids, probs, w_gate, w_up, w_down):
    chips_z, chips_x, groups = lax.axis_size("z"), lax.axis_size("x"), lax.axis_size("yo")
    count, width = tokens.shape
    features, units = w_gate.shape[1:]
    depth = width + 1
    wide = chips_z * chips_x * CORES * depth
    hidden = -(-units // 16) * 16
    core, yi = lax.axis_index("core"), lax.axis_index("yi")

    packed = pl.pallas_call(
        pack_kernel,
        out_shape=jax.ShapeDtypeStruct((depth, 2 * count), BF16),
        in_specs=[SMEM, VMEM, VMEM, VMEM, VMEM],
        out_specs=VMEM,
        name="pack",
    )(lax.axis_index("z").reshape(1), tokens.T, grad_out.T, expert_ids.T, probs.T)
    paired = jnp.stack([packed, swap(packed, "yi")])
    along_z = lax.all_gather(paired, "z")
    along_x = lax.all_to_all(
        jnp.broadcast_to(along_z[None], (chips_x,) + along_z.shape), "x", split_axis=0, concat_axis=0, tiled=True
    )
    crossed = swap(along_x, "core")

    stacked = pl.pallas_call(
        weights_kernel,
        out_shape=jax.ShapeDtypeStruct((3 * hidden, wide), BF16),
        in_specs=[VMEM] * 3,
        out_specs=VMEM,
        name="widen_weights",
    )(w_gate[0].T, w_up[0].T, w_down[0])
    weights = lax.all_gather(stacked, "yo")

    parts = pl.pallas_call(
        grads_kernel,
        out_shape=jax.ShapeDtypeStruct((groups, 3 * hidden, wide), BF16),
        in_specs=[SMEM, ANY, ANY, VMEM],
        out_specs=VMEM,
        scratch_shapes=[
            pltpu.VMEM((chips_z, chips_x * CORES, depth, PAIR * count), BF16),
            pltpu.VMEM((chips_z, chips_x * CORES, depth, PAIR * count), BF16),
            pltpu.SemaphoreType.DMA((2, chips_x, PAIR, 2)),
        ],
        compiler_params=PARAMS,
        name="grads",
    )(jnp.stack([core, yi]), along_x, crossed, weights)
    met = lax.all_to_all(parts, "yo", split_axis=0, concat_axis=0, tiled=True)
    grad_gate, grad_up, grad_down = pl.pallas_call(
        total_kernel,
        out_shape=[jax.ShapeDtypeStruct((units, features), BF16)] * 3,
        in_specs=[VMEM],
        out_specs=[VMEM] * 3,
        name="total",
    )(met)
    return grad_gate.T[None], grad_up.T[None], grad_down[None]


def solution(mesh, chips_x=CHIPS_X):
    section, ep = mesh.devices.shape
    shape = (section // (chips_x * CORES), chips_x, CORES, ep // PAIR, PAIR)
    fine = Mesh(mesh.devices.reshape(shape), SEC + EP)
    placed = (
        P(EP, SEC),
        P(EP, SEC),
        P(EP, None),
        P(EP, None),
        P(EP, None, SEC),
        P(EP, None, SEC),
        P(EP, SEC, None),
    )
    return jax.shard_map(
        shards,
        mesh=fine,
        in_specs=placed,
        out_specs=(P(EP, None, SEC), P(EP, None, SEC), P(EP, SEC, None)),
        check_vma=False,
    )
```

time: 306 us -> 144 us (0.47)
  waiting for transfers between devices: 211 us -> 35.9 us
  blocking collectives: 24.3 us -> 61.6 us
  local copies, waits for them, and re-layouts: 29.9 us -> 2.62 us
  starting transfers between devices: 0.08 us -> 18.4 us
  matrix products: 17.1 us -> 0 us
  Pallas kernels: 0 us -> 9.42 us
  other arithmetic: 8.49 us -> 0.8 us
    all_gather x2 -> x1, waiting for transfers between devices: 211 us -> 23.4 us  [shards(): weights = lax.all_gather(stacked, 'yo')]
    all_gather x0 -> x1, blocking collectives: none -> 29.3 us  [shards(): along_z = lax.all_gather(paired, 'z')]
    all_gather x2 -> x0, local copies, waits for them, and re-layouts: 20.5 us -> none  [the longest x1 10.2 us: shards(): lax.all_gather(got_rows, 'section', axis=4, tiled=True)]
    dot_general x6 -> x0, matrix products: 17.1 us -> none  [the longest x1 3.99 us: slot_grads(): jnp.einsum('hpscd,sdf->hpscf', inputs, gate_w, preferred_element_type=jnp...]
    ppermute x0 -> x2, starting transfers between devices: none -> 14.4 us  [swap(): return lax.ppermute(value, axis, [(0, 1), (1, 0)])]
    all_to_all x0 -> x1, waiting for transfers between devices: none -> 11.1 us  [shards(): lax.all_to_all(jnp.broadcast_to(along_z[None], (chips_x,) + along_z.shape...]
    pallas_call x0 -> x4, Pallas kernels: none -> 9.42 us  [the longest x1 3.47 us: shards(): pl.pallas_call(grads_kernel, out_shape=jax.ShapeDtypeStruct((groups, 3 *...]
    all_to_all x2 -> x1, blocking collectives: 24.3 us -> 32.3 us  [shards(): met = lax.all_to_all(parts, 'yo', split_axis=0, concat_axis=0, tiled=True)]
  transfers between devices with their start and end apart: 2 -> 4, of which waited for: 2 -> 3; matrix products, arithmetic and copies ran while one was open for 7% -> 0% of each run, Pallas kernels for 0% -> 1%
where the time goes in v1:
time: 144 us; the launch traced here: 143 us
  blocking collectives  61.6 us (43%)
  waiting for transfers between devices  35.9 us (25%)
  starting transfers between devices  18.4 us (13%)
  between operations  14.1 us (10%)
  Pallas kernels  9.42 us (7%)
  local copies, waits for them, and re-layouts  2.62 us (2%)
    all_to_all x1, blocking collectives, shards(): met = lax.all_to_all(parts, 'yo', split_axis=0, concat_axis=0, tiled=True)  32.3 us
    all_gather x1, blocking collectives, shards(): along_z = lax.all_gather(paired, 'z')  29.3 us
    all_gather x1, waiting for transfers between devices, shards(): weights = lax.all_gather(stacked, 'yo')  23.4 us
    ppermute x2, starting transfers between devices, swap(): return lax.ppermute(value, axis, [(0, 1), (1, 0)])  14.4 us
    all_to_all x1, waiting for transfers between devices, shards(): lax.all_to_all(jnp.broadcast_to(along_z[None], (chips_x,) + along_z.shape...  11.1 us
    all_to_all x1, starting transfers between devices, shards(): lax.all_to_all(jnp.broadcast_to(along_z[None], (chips_x,) + along_z.shape...  4.01 us
    pallas_call x1, Pallas kernels, shards(): pl.pallas_call(grads_kernel, out_shape=jax.ShapeDtypeStruct((groups, 3 *...  3.47 us
  transfers between devices with their start and end apart: 4, of which 3 were waited for; matrix products, arithmetic and copies ran while one was open for 0% of the time, Pallas kernels for 1%

profile of v1, /device:TPU:1, one launch (start us, length us, event | category | flops | bytes accessed | tf_op | source)
XLA Modules:
  0.0 142.8 jit_solution(3599778642017999084)
XLA Ops:
  7.2 1.4 pack.1
  8.5 4.0 %collective-permute-start = (bf16[16,512]{1,0:T(8,128)(2,1)}, bf16[16,512]{1,0:T(8,128)(2,1)S(1)}, u32[]{:S(2)}, u32[]{:S(2)}) collective-permute-start(bf16[16,512]{1,0:T(8,128)(2,1)} %pack.1), channel_id=1, source_target_pairs={{0,1},{1,0},{2,3},{3,2},{4,5},{5,4},{6,7},{7,6},{8,9},{9,8},{10,11... | collective-permute-start | bytes 49160 | tf_op jit(solution)/shard_map/ppermute | solution.py:149
  12.6 1.3 collective-permute-done
  13.9 0.7 pad_maximum_fusion
  14.6 29.3 %all-gather = bf16[24,16,512]{2,1,0:T(8,128)(2,1)S(1)} all-gather(bf16[2,16,512]{2,1,0:T(8,128)(2,1)S(1)} %pad_maximum_fusion), channel_id=2, replica_groups=mesh['z'=12,'x'=4,'core'=2,'yo'=4,'yi'=2] {'z'}, dimensions={0}, use_global_device_ids=true | all-gather | bytes 425984 | tf_op jit(solution)/shard_map/all_gather | solution.py:169
  43.9 1.3 broadcast_in_dim.15
  45.3 4.0 %all-to-all-start = ((bf16[4,12,2,16,512]{4,3,2,1,0:T(8,128)(2,1)}), bf16[4,12,2,16,512]{4,3,2,1,0:T(8,128)(2,1)S(1)}, u32[]{:S(2)}, u32[]{:S(2)}) async-start(bf16[4,12,2,16,512]{4,3,2,1,0:T(8,128)(2,1)} %broadcast_in_dim.15), calls=%async_computation | async-start | bytes 3145728 | tf_op jit(solution)/shard_map/all_to_all | solution.py:170
  49.3 0.0 all-gather.4.cloned.1.call-start
  49.3 2.0 %widen_weights.1 = bf16[96,1536]{1,0:T(8,128)(2,1)} custom-call(bf16[30,1440]{1,0:T(8,128)(2,1)} %bitcast.27, bf16[30,1440]{1,0:T(8,128)(2,1)} %bitcast.28, bf16[30,1440]{1,0:T(8,128)(2,1)} %bitcast.29), custom_call_target="tpu_custom_call" | custom-call | tf_op jit(solution)/shard_map/widen_weights/pallas_call | solution.py:175
  51.3 0.0 all-gather.4.cloned.1.call-update
  51.4 11.1 %all-to-all-done.own = bf16[4,12,2,16,512]{4,3,2,1,0:T(8,128)(2,1)S(1)} async-done(((bf16[4,12,2,16,512]{4,3,2,1,0:T(8,128)(2,1)}), bf16[4,12,2,16,512]{4,3,2,1,0:T(8,128)(2,1)S(1)}, u32[]{:S(2)}, u32[]{:S(2)}) %all-to-all-start) | async-done | bytes 1572896 | tf_op jit(solution)/shard_map/all_to_all | solution.py:170
  62.5 10.4 %collective-permute-start.1 = (bf16[4,12,2,16,512]{4,3,2,1,0:T(8,128)(2,1)S(1)}, bf16[4,12,2,16,512]{4,3,2,1,0:T(8,128)(2,1)S(1)}, u32[]{:S(2)}, u32[]{:S(2)}) collective-permute-start(bf16[4,12,2,16,512]{4,3,2,1,0:T(8,128)(2,1)S(1)} %all-to-all-done.own), channel_id=1, source_target_pairs={{0,8},{8,0},{1,9},{9,1},{2,10},{10,2},{3,11},{11,3},{4,12},{12,4},... | collective-permute-start | bytes 4718600 | tf_op jit(solution)/shard_map/ppermute | solution.py:149
  72.9 0.1 pad_add_fusion.place
  73.0 23.4 %all-gather.4.cloned.1.call-done = bf16[384,1536]{1,0:T(8,128)(2,1)} async-done(((bf16[96,1536]{1,0:T(8,128)(2,1)}), bf16[384,1536]{1,0:T(8,128)(2,1)}) %all-gather.4.cloned.1.call-update) | async-done | bytes 1179664 | tf_op jit(solution)/shard_map/all_gather | solution.py:182
  96.4 0.0 collective-permute-done.1.other
  96.4 0.0 copy-start
  96.4 1.3 copy-done
  97.7 3.5 %grads.1 = bf16[4,96,1536]{2,1,0:T(8,128)(2,1)S(1)} custom-call(s32[2]{0:T(128)S(1)} %pad_add_fusion.place, bf16[4,12,2,16,512]{4,3,2,1,0:T(8,128)(2,1)S(1)} %all-to-all-done.own, bf16[4,12,2,16,512]{4,3,2,1,0:T(8,128)(2,1)S(1)} %collective-permute-done.1.other, bf16[4,96,1536]{2,1,0:T(8,128)(2,1)S(1)} %bitcast.25), custom_call_target="tpu_custom_call" | custom-call | tf_op jit(solution)/shard_map/grads/pallas_call | solution.py:184
  101.2 32.3 %all_to_all.10.parts = bf16[4,96,1536]{2,1,0:T(8,128)(2,1)} all-to-all(bf16[4,96,1536]{2,1,0:T(8,128)(2,1)S(1)} %grads.1), channel_id=1, replica_groups=mesh['z'=12,'x'=4,'core'=2,'yo'=4,'yi'=2] {'yo'}, dimensions={0} | all-to-all | bytes 2359296 | tf_op jit(solution)/shard_map/all_to_all | solution.py:197
  133.4 2.6 %total.1 = (bf16[30,1440]{1,0:T(8,128)(2,1)}, bf16[30,1440]{1,0:T(8,128)(2,1)}, bf16[30,1440]{1,0:T(8,128)(2,1)}) custom-call(bf16[4,96,1536]{2,1,0:T(8,128)(2,1)} %all_to_all.10.parts), custom_call_target="tpu_custom_call" | custom-call | tf_op jit(solution)/shard_map/total/pallas_call | solution.py:198
Async XLA Ops:
  8.5 5.4 %collective-permute-start = (bf16[16,512]{1,0:T(8,128)(2,1)}, bf16[16,512]{1,0:T(8,128)(2,1)S(1)}, u32[]{:S(2)}, u32[]{:S(2)}) collective-permute-start(bf16[16,512]{1,0:T(8,128)(2,1)} %pack.1), channel_id=1, source_target_pairs={{0,1},{1,0},{2,3},{3,2},{4,5},{5,4},{6,7},{7,6},{8,9},{9,8},{10,11... | collective-permute-start | bytes 49160 | tf_op jit(solution)/shard_map/ppermute | solution.py:149
  45.3 17.2 %all-to-all-start = ((bf16[4,12,2,16,512]{4,3,2,1,0:T(8,128)(2,1)}), bf16[4,12,2,16,512]{4,3,2,1,0:T(8,128)(2,1)S(1)}, u32[]{:S(2)}, u32[]{:S(2)}) async-start(bf16[4,12,2,16,512]{4,3,2,1,0:T(8,128)(2,1)} %broadcast_in_dim.15), calls=%async_computation | async-start | bytes 3145728 | tf_op jit(solution)/shard_map/all_to_all | solution.py:170
  49.3 47.1 %all-gather.4.cloned.1.call-start = ((), (), s32[]{:S(2)}) async-start(), calls=%async_computation.2 | async-start | bytes 1474560 | tf_op jit(solution)/shard_map/all_gather | solution.py:182
  62.5 33.9 %collective-permute-start.1 = (bf16[4,12,2,16,512]{4,3,2,1,0:T(8,128)(2,1)S(1)}, bf16[4,12,2,16,512]{4,3,2,1,0:T(8,128)(2,1)S(1)}, u32[]{:S(2)}, u32[]{:S(2)}) collective-permute-start(bf16[4,12,2,16,512]{4,3,2,1,0:T(8,128)(2,1)S(1)} %all-to-all-done.own), channel_id=1, source_target_pairs={{0,8},{8,0},{1,9},{9,1},{2,10},{10,2},{3,11},{11,3},{4,12},{12,4},... | collective-permute-start | bytes 4718600 | tf_op jit(solution)/shard_map/ppermute | solution.py:149
  96.4 1.3 copy-start
Sparse Core Ops, SparseCore 0:
  52.5 43.8 all-gather.3

commit v2 on v1

--- a/solution.py
+++ b/solution.py
@@ -12,8 +12,9 @@
 CHIPS_X = 4
 PAIR = 2
 LANES = 128
-SEC = ("z", "x", "core")
+SEC = ("zo", "zi", "x", "core")
 EP = ("yo", "yi")
+GROUP = ("zi", "yi")
 
 
 def dot(a, b):
@@ -57,16 +58,32 @@
     return jnp.concatenate(pieces, axis=1)
 
 
+def half_turn(tile):
+    return pltpu.roll(tile, LANES // 2, 1)
+
+
+def turned(rows):
+    tiles = [half_turn(rows[:, k : k + LANES]) for k in range(0, rows.shape[1], LANES)]
+    return jnp.concatenate(tiles, axis=1)
+
+
 def pack_kernel(place, tokens, cotangent, ids, probs, out):
-    width, count = tokens.shape
+    count = tokens.shape[1]
     mine = ids[...] == place[0]
     weight = jnp.sum(jnp.where(mine, probs[...], 0.0), axis=0, keepdims=True)
     high = weight.astype(BF16).astype(F32)
-    low = weight - high
     left = jnp.concatenate([tokens[...].astype(F32), high], axis=0)
-    right = jnp.concatenate([cotangent[...].astype(F32), low], axis=0)
-    out[:, :count] = left.astype(BF16)
-    out[:, count:] = right.astype(BF16)
+    right = jnp.concatenate([cotangent[...].astype(F32), weight - high], axis=0)
+    odd = place[1] == 1
+    first, second = jnp.where(odd, right, left), jnp.where(odd, left, right)
+    lower = lax.broadcasted_iota(jnp.int32, (first.shape[0], LANES), 1) < LANES // 2
+    for tile in range(count // LANES):
+        a, b = first[:, tile * LANES : (tile + 1) * LANES], second[:, tile * LANES : (tile + 1) * LANES]
+        quarters = (jnp.where(lower, a, half_turn(b)), jnp.where(lower, half_turn(a), b))
+        for k, quarter in enumerate(quarters):
+            zi, yi = divmod(2 * tile + k, PAIR)
+            for yo in range(out.shape[1]):
+                out[zi, yo, yi] = quarter.astype(BF16)
 
 
 def weights_kernel(gate_w, up_w, down_w, out):
@@ -79,30 +96,25 @@
     out[...] = widen(jnp.concatenate(rows, axis=0).astype(BF16), wide)
 
 
-def grads_kernel(place, own, other, weights, out, inputs, cotangents, sems):
-    chips_x, chips_z, pair, depth, both = own.shape
-    count = both // 2
+def grads_kernel(place, own, other, weights, out, inputs, cotangents, near, sems):
+    chips_x, chips_z, blocks, depth, lanes = own.shape
     groups, stacked, wide = weights.shape
     hidden = stacked // 3
-    core, yi = place[0], place[1]
-    copies = []
-    for s, ref in enumerate((own, other)):
-        slot = core if s == 0 else 1 - core
-        for x in range(chips_x):
-            for y in range(pair):
-                for k, held in enumerate((inputs, cotangents)):
-                    copies.append(
-                        pltpu.make_async_copy(
-                            ref.at[x, :, y, :, pl.ds(k * count, count)],
-                            held.at[:, x * CORES + slot, :, pl.ds(y * count, count)],
-                            sems.at[s, x, y, k],
-                        )
-                    )
+    core, yo = place[0], place[1]
+    lower = lax.broadcasted_iota(jnp.int32, (chips_z, depth, lanes), 2) < lanes // 2
+    copies = [pltpu.make_async_copy(own.at[x], near.at[x], sems.at[x]) for x in range(chips_x)]
     for copy in copies:
         copy.start()
-    for copy in copies:
-        copy.wait()
-    total = pair * count
+    for ref, slot in ((other, 1 - core), (near, core)):
+        for x in range(chips_x):
+            if ref is near:
+                copies[x].wait()
+            for pair in range(blocks // 2):
+                even, odd = ref[x, :, 2 * pair], ref[x, :, 2 * pair + 1]
+                at = slice(pair * lanes, (pair + 1) * lanes)
+                inputs[:, x * CORES + slot, :, at] = jnp.where(lower, even, odd)
+                cotangents[:, x * CORES + slot, :, at] = jnp.where(lower, odd, even)
+    total = blocks // 2 * lanes
     rows = inputs[...].reshape(wide, total)
     backs = cotangents[...].reshape(wide, total)
 
@@ -111,16 +123,17 @@
 
     gate = dot(part(0), rows)
     linear = dot(part(1), rows)
-    back = dot(part(2), backs)
+    back = turned(dot(part(2), backs))
     shares = []
     for j in range(groups):
-        high = inputs[j * PAIR + yi, 0].astype(F32)[depth - 1 : depth]
-        low = cotangents[j * PAIR + yi, 0].astype(F32)[depth - 1 : depth]
+        expert = yo * PAIR + j % PAIR
+        high = inputs[expert, 0].astype(F32)[depth - 1 : depth]
+        low = turned(cotangents[expert, 0].astype(F32))[depth - 1 : depth]
         shares.append(jnp.broadcast_to(high + low, (hidden, total)))
     share = jnp.concatenate(shares, axis=0)
     back = back * share
     sigma = jax.nn.sigmoid(gate)
-    lifted = (gate * sigma * linear * share).astype(BF16)
+    lifted = turned(gate * sigma * linear * share).astype(BF16)
     gate_term = (back * linear * sigma * (1.0 + gate * (1.0 - sigma))).astype(BF16)
     linear_term = (back * gate * sigma).astype(BF16)
     for k, (left, right) in enumerate(((gate_term, rows), (linear_term, rows), (lifted, backs))):
@@ -145,33 +158,38 @@
 PARAMS = pltpu.CompilerParams(vmem_limit_bytes=40 * 1024 * 1024)
 
 
+def after(value, earlier):
+    return pl.pallas_call(
+        lambda value_ref, earlier_ref, out_ref: None,
+        out_shape=jax.ShapeDtypeStruct(value.shape, value.dtype),
+        in_specs=[ANY, ANY],
+        out_specs=ANY,
+        input_output_aliases={0: 0},
+        name="after",
+    )(value, earlier)
+
+
 def swap(value, axis):
     return lax.ppermute(value, axis, [(0, 1), (1, 0)])
 
 
 def shards(tokens, grad_out, expert_ids, probs, w_gate, w_up, w_down):
-    chips_z, chips_x, groups = lax.axis_size("z"), lax.axis_size("x"), lax.axis_size("yo")
+    pairs_z, chips_x, pairs_y = lax.axis_size("zo"), lax.axis_size("x"), lax.axis_size("yo")
+    chips_z, groups = pairs_z * PAIR, PAIR * PAIR
     count, width = tokens.shape
     features, units = w_gate.shape[1:]
     depth = width + 1
     wide = chips_z * chips_x * CORES * depth
     hidden = -(-units // 16) * 16
-    core, yi = lax.axis_index("core"), lax.axis_index("yi")
+    zone = lax.axis_index(("zo", "zi"))
 
     packed = pl.pallas_call(
         pack_kernel,
-        out_shape=jax.ShapeDtypeStruct((depth, 2 * count), BF16),
+        out_shape=jax.ShapeDtypeStruct((PAIR, pairs_y, PAIR, depth, LANES), BF16),
         in_specs=[SMEM, VMEM, VMEM, VMEM, VMEM],
         out_specs=VMEM,
         name="pack",
-    )(lax.axis_index("z").reshape(1), tokens.T, grad_out.T, expert_ids.T, probs.T)
-    paired = jnp.stack([packed, swap(packed, "yi")])
-    along_z = lax.all_gather(paired, "z")
-    along_x = lax.all_to_all(
-        jnp.broadcast_to(along_z[None], (chips_x,) + along_z.shape), "x", split_axis=0, concat_axis=0, tiled=True
-    )
-    crossed = swap(along_x, "core")
-
+    )(jnp.stack([zone, lax.axis_index("yi")]), tokens.T, grad_out.T, expert_ids.T, probs.T)
     stacked = pl.pallas_call(
         weights_kernel,
         out_shape=jax.ShapeDtypeStruct((3 * hidden, wide), BF16),
@@ -179,22 +197,29 @@
         out_specs=VMEM,
         name="widen_weights",
     )(w_gate[0].T, w_up[0].T, w_down[0])
-    weights = lax.all_gather(stacked, "yo")
-
+    sent = packed.reshape(PAIR * pairs_y * PAIR, depth, LANES)
+    quarter = lax.all_to_all(sent, ("zi",) + EP, split_axis=0, concat_axis=0, tiled=True)
+    quarter, stacked = lax.optimization_barrier((quarter, stacked))
+    weights = lax.all_gather(stacked, GROUP)
+    along_z = lax.all_gather(quarter, "zo").reshape(chips_z, pairs_y * PAIR, depth, LANES)
+    along_x = lax.all_to_all(
+        jnp.broadcast_to(along_z[None], (chips_x,) + along_z.shape), "x", split_axis=0, concat_axis=0, tiled=True
+    )
+    along_x = after(along_x, weights)
+    crossed = swap(along_x, "core")
+
+    tokens_held = pairs_y * LANES
     parts = pl.pallas_call(
         grads_kernel,
         out_shape=jax.ShapeDtypeStruct((groups, 3 * hidden, wide), BF16),
-        in_specs=[SMEM, ANY, ANY, VMEM],
+        in_specs=[SMEM, ANY, VMEM, VMEM],
         out_specs=VMEM,
-        scratch_shapes=[
-            pltpu.VMEM((chips_z, chips_x * CORES, depth, PAIR * count), BF16),
-            pltpu.VMEM((chips_z, chips_x * CORES, depth, PAIR * count), BF16),
-            pltpu.SemaphoreType.DMA((2, chips_x, PAIR, 2)),
-        ],
+        scratch_shapes=[pltpu.VMEM((chips_z, chips_x * CORES, depth, tokens_held), BF16)] * 2
+        + [pltpu.VMEM(along_x.shape, BF16), pltpu.SemaphoreType.DMA((chips_x,))],
         compiler_params=PARAMS,
         name="grads",
-    )(jnp.stack([core, yi]), along_x, crossed, weights)
-    met = lax.all_to_all(parts, "yo", split_axis=0, concat_axis=0, tiled=True)
+    )(jnp.stack([lax.axis_index("core"), lax.axis_index("yo")]), along_x, crossed, weights)
+    met = lax.all_to_all(parts, GROUP, split_axis=0, concat_axis=0, tiled=True)
     grad_gate, grad_up, grad_down = pl.pallas_call(
         total_kernel,
         out_shape=[jax.ShapeDtypeStruct((units, features), BF16)] * 3,
@@ -207,7 +232,7 @@
 
 def solution(mesh, chips_x=CHIPS_X):
     section, ep = mesh.devices.shape
-    shape = (section // (chips_x * CORES), chips_x, CORES, ep // PAIR, PAIR)
+    shape = (section // (chips_x * CORES * PAIR), PAIR, chips_x, CORES, ep // PAIR, PAIR)
     fine = Mesh(mesh.devices.reshape(shape), SEC + EP)
     placed = (
         P(EP, SEC),

time: 144 us -> 118 us (0.82)
  waiting for transfers between devices: 35.9 us -> 8.45 us
    all_gather x1, waiting for transfers between devices: 23.4 us -> 0.01 us  [shards(): weights = lax.all_gather(stacked, GROUP)]
    all_to_all x1, waiting for transfers between devices: 11.1 us -> 5.29 us  [shards(): lax.all_to_all(sent, ('zi',) + EP, split_axis=0, concat_axis=0, tiled=True)]
    all_to_all x1, starting transfers between devices: 4.01 us -> 9.56 us  [shards(): lax.all_to_all(sent, ('zi',) + EP, split_axis=0, concat_axis=0, tiled=True)]
    ppermute x2 -> x1, starting transfers between devices: 14.4 us -> 9.59 us  [swap(): return lax.ppermute(value, axis, [(0, 1), (1, 0)])]
    all_to_all x1 -> x2, blocking collectives: 32.3 us -> 36.1 us  [the longest x1 18.1 us: shards(): met = lax.all_to_all(parts, GROUP, split_axis=0, concat_axis=0, tiled=True)]
    all_gather x1, blocking collectives: 29.3 us -> 26.6 us  [shards(): lax.all_gather(quarter, 'zo').reshape(chips_z, pairs_y * PAIR, depth, LANES)]
    ppermute x2 -> x1, waiting for transfers between devices: 1.33 us -> 3.14 us  [swap(): return lax.ppermute(value, axis, [(0, 1), (1, 0)])]
  transfers between devices with their start and end apart: 4 -> 3, of which waited for: 3 -> 2; matrix products, arithmetic and copies ran while one was open for 0% -> 0% of each run, Pallas kernels for 1% -> 2%
where the time goes in v2:
time: 118 us; the launch traced here: 117 us
  blocking collectives  62.7 us (53%)
  starting transfers between devices  19.2 us (16%)
  between operations  14.1 us (12%)
  Pallas kernels  10.5 us (9%)
  waiting for transfers between devices  8.45 us (7%)
  local copies, waits for them, and re-layouts  1.77 us (2%)
    all_gather x1, blocking collectives, shards(): lax.all_gather(quarter, 'zo').reshape(chips_z, pairs_y * PAIR, depth, LANES)  26.6 us
    all_to_all x1, blocking collectives, shards(): met = lax.all_to_all(parts, GROUP, split_axis=0, concat_axis=0, tiled=True)  18.1 us
    all_to_all x1, blocking collectives, shards(): lax.all_to_all(jnp.broadcast_to(along_z[None], (chips_x,) + along_z.shape...  18 us
    ppermute x1, starting transfers between devices, swap(): return lax.ppermute(value, axis, [(0, 1), (1, 0)])  9.59 us
    all_to_all x1, starting transfers between devices, shards(): lax.all_to_all(sent, ('zi',) + EP, split_axis=0, concat_axis=0, tiled=True)  9.56 us
    all_to_all x1, waiting for transfers between devices, shards(): lax.all_to_all(sent, ('zi',) + EP, split_axis=0, concat_axis=0, tiled=True)  5.29 us
    pallas_call x1, Pallas kernels, shards(): pl.pallas_call(grads_kernel, out_shape=jax.ShapeDtypeStruct((groups, 3 *...  4.37 us
    ppermute x1, waiting for transfers between devices, swap(): return lax.ppermute(value, axis, [(0, 1), (1, 0)])  3.14 us
  transfers between devices with their start and end apart: 3, of which 2 were waited for; matrix products, arithmetic and copies ran while one was open for 0% of the time, Pallas kernels for 2%

profile of v2, /device:TPU:1, one launch (start us, length us, event | category | flops | bytes accessed | tf_op | source)
XLA Modules:
  0.0 117.4 jit_solution(17246955078451392721)
XLA Ops:
  7.2 0.6 pad_add_fusion.1.place
  7.8 1.5 %pack.1 = bf16[2,4,2,16,128]{4,3,2,1,0:T(8,128)(2,1)} custom-call(s32[2]{0:T(128)} %pad_add_fusion.1.place, bf16[15,256]{1,0:T(8,128)(2,1)} %bitcast.32, bf16[15,256]{1,0:T(8,128)(2,1)} %bitcast.33, s32[4,256]{1,0:T(4,128)} %bitcast.34, f32[4,256]{1,0:T(4,128)} %bitcast.35), custom_call_target="tpu_custom_call" | custom-call | tf_op jit(solution)/shard_map/pack/pallas_call | solution.py:186
  9.3 9.6 %all-to-all-start = ((bf16[16,16,128]{2,1,0:T(8,128)(2,1)}), bf16[16,16,128]{2,1,0:T(8,128)(2,1)S(1)}, u32[]{:S(2)}, u32[]{:S(2)}) async-start(bf16[16,16,128]{2,1,0:T(8,128)(2,1)} %bitcast.28), calls=%async_computation | async-start | bytes 131072 | tf_op jit(solution)/shard_map/all_to_all | solution.py:201
  18.9 0.0 all-gather.4.cloned.1.call-start
  18.9 2.0 %widen_weights.1 = bf16[96,1536]{1,0:T(8,128)(2,1)} custom-call(bf16[30,1440]{1,0:T(8,128)(2,1)} %bitcast.29, bf16[30,1440]{1,0:T(8,128)(2,1)} %bitcast.30, bf16[30,1440]{1,0:T(8,128)(2,1)} %bitcast.31), custom_call_target="tpu_custom_call" | custom-call | tf_op jit(solution)/shard_map/widen_weights/pallas_call | solution.py:193
  20.9 5.3 %all-to-all-done = bf16[16,16,128]{2,1,0:T(8,128)(2,1)S(1)} async-done(((bf16[16,16,128]{2,1,0:T(8,128)(2,1)}), bf16[16,16,128]{2,1,0:T(8,128)(2,1)S(1)}, u32[]{:S(2)}, u32[]{:S(2)}) %all-to-all-start) | async-done | bytes 65568 | tf_op jit(solution)/shard_map/all_to_all | solution.py:201
  26.2 0.0 all-gather.4.cloned.1.call-update
  26.3 26.6 %all-gather = bf16[96,16,128]{2,1,0:T(8,128)(2,1)S(1)} all-gather(bf16[16,16,128]{2,1,0:T(8,128)(2,1)S(1)} %all-to-all-done), channel_id=2, replica_groups=mesh['zo'=6,'zi'=2,'x'=4,'core'=2,'yo'=4,'yi'=2] {'zo'}, dimensions={0}, use_global_device_ids=true | all-gather | bytes 458752 | tf_op jit(solution)/shard_map/all_gather | solution.py:204
  52.8 0.4 broadcast_in_dim.17
  53.2 18.0 %all_to_all.15.value_ref = bf16[4,12,8,16,128]{4,3,2,1,0:T(8,128)(2,1)} all-to-all(bf16[4,12,8,16,128]{4,3,2,1,0:T(8,128)(2,1)S(1)} %broadcast_in_dim.17), channel_id=1, replica_groups=mesh['zo'=6,'zi'=2,'x'=4,'core'=2,'yo'=4,'yi'=2] {'x'}, dimensions={0} | all-to-all | bytes 3145728 | tf_op jit(solution)/shard_map/all_to_all | solution.py:205
  71.2 0.0 all-gather.4.cloned.1.call-done
  71.2 0.0 copy-start.1
  71.3 9.6 %collective-permute-start = (bf16[4,12,8,16,128]{4,3,2,1,0:T(8,128)(2,1)}, bf16[4,12,8,16,128]{4,3,2,1,0:T(8,128)(2,1)S(1)}, u32[]{:S(2)}, u32[]{:S(2)}) collective-permute-start(bf16[4,12,8,16,128]{4,3,2,1,0:T(8,128)(2,1)} %after.1.own), channel_id=1, source_target_pairs={{0,8},{8,0},{1,9},{9,1},{2,10},{10,2},{3,11},{11,3},{4,12},{12,4},... | collective-permute-start | bytes 4718600 | tf_op jit(solution)/shard_map/ppermute | solution.py:173
  80.9 0.1 pad_add_fusion.place
  80.9 3.1 %collective-permute-done.other = bf16[4,12,8,16,128]{4,3,2,1,0:T(8,128)(2,1)S(1)} collective-permute-done((bf16[4,12,8,16,128]{4,3,2,1,0:T(8,128)(2,1)}, bf16[4,12,8,16,128]{4,3,2,1,0:T(8,128)(2,1)S(1)}, u32[]{:S(2)}, u32[]{:S(2)}) %collective-permute-start) | collective-permute-done | bytes 1572896 | tf_op jit(solution)/shard_map/ppermute | solution.py:173
  84.1 0.0 copy-done.1
  84.1 0.0 copy-start
  84.1 1.4 %copy-done = bf16[4,12,8,16,128]{4,3,2,1,0:T(8,128)(2,1)S(1)} copy-done((bf16[4,12,8,16,128]{4,3,2,1,0:T(8,128)(2,1)S(1)}, bf16[4,12,8,16,128]{4,3,2,1,0:T(8,128)(2,1)}, u32[]{:S(2)}) %copy-start) | copy-done | bytes 1572888
  85.5 4.4 %grads.1 = bf16[4,96,1536]{2,1,0:T(8,128)(2,1)S(1)} custom-call(s32[2]{0:T(128)S(1)} %pad_add_fusion.place, bf16[4,12,8,16,128]{4,3,2,1,0:T(8,128)(2,1)S(1)} %copy-done, bf16[4,12,8,16,128]{4,3,2,1,0:T(8,128)(2,1)S(1)} %collective-permute-done.other, bf16[4,96,1536]{2,1,0:T(8,128)(2,1)S(1)} %bitcast.26), custom_call_target="tpu_custom_call" | custom-call | tf_op jit(solution)/shard_map/grads/pallas_call | solution.py:212
  89.9 18.1 %all_to_all.16.parts = bf16[4,96,1536]{2,1,0:T(8,128)(2,1)} all-to-all(bf16[4,96,1536]{2,1,0:T(8,128)(2,1)S(1)} %grads.1), channel_id=1, replica_groups=mesh['zo'=6,'zi'=2,'x'=4,'core'=2,'yo'=4,'yi'=2] {'zi','yi'}, dimensions={0} | all-to-all | bytes 2359296 | tf_op jit(solution)/shard_map/all_to_all | solution.py:222
  108.0 2.6 %total.1 = (bf16[30,1440]{1,0:T(8,128)(2,1)}, bf16[30,1440]{1,0:T(8,128)(2,1)}, bf16[30,1440]{1,0:T(8,128)(2,1)}) custom-call(bf16[4,96,1536]{2,1,0:T(8,128)(2,1)} %all_to_all.16.parts), custom_call_target="tpu_custom_call" | custom-call | tf_op jit(solution)/shard_map/total/pallas_call | solution.py:223
  (1 shorter events, 0.0 us)
Async XLA Ops:
  9.3 16.9 %all-to-all-start = ((bf16[16,16,128]{2,1,0:T(8,128)(2,1)}), bf16[16,16,128]{2,1,0:T(8,128)(2,1)S(1)}, u32[]{:S(2)}, u32[]{:S(2)}) async-start(bf16[16,16,128]{2,1,0:T(8,128)(2,1)} %bitcast.28), calls=%async_computation | async-start | bytes 131072 | tf_op jit(solution)/shard_map/all_to_all | solution.py:201
  18.9 52.4 %all-gather.4.cloned.1.call-start = ((), (), s32[]{:S(2)}) async-start(), calls=%async_computation.3 | async-start | bytes 1474560 | tf_op jit(solution)/shard_map/all_gather | solution.py:203
  71.2 12.8 %copy-start.1 = (bf16[384,1536]{1,0:T(8,128)(2,1)S(1)}, bf16[384,1536]{1,0:T(8,128)(2,1)}, u32[]{:S(2)}) copy-start(bf16[384,1536]{1,0:T(8,128)(2,1)} %all-gather.4.cloned.1.call-done) | copy-start | bytes 3538948
  71.3 12.8 %collective-permute-start = (bf16[4,12,8,16,128]{4,3,2,1,0:T(8,128)(2,1)}, bf16[4,12,8,16,128]{4,3,2,1,0:T(8,128)(2,1)S(1)}, u32[]{:S(2)}, u32[]{:S(2)}) collective-permute-start(bf16[4,12,8,16,128]{4,3,2,1,0:T(8,128)(2,1)} %after.1.own), channel_id=1, source_target_pairs={{0,8},{8,0},{1,9},{9,1},{2,10},{10,2},{3,11},{11,3},{4,12},{12,4},... | collective-permute-start | bytes 4718600 | tf_op jit(solution)/shard_map/ppermute | solution.py:173
  84.1 1.4 %copy-start = (bf16[4,12,8,16,128]{4,3,2,1,0:T(8,128)(2,1)S(1)}, bf16[4,12,8,16,128]{4,3,2,1,0:T(8,128)(2,1)}, u32[]{:S(2)}) copy-start(bf16[4,12,8,16,128]{4,3,2,1,0:T(8,128)(2,1)} %after.1.own) | copy-start | bytes 4718596
Sparse Core Ops, SparseCore 0:
  26.4 42.1 all-gather.3

commit v3 on v2

--- a/solution.py
+++ b/solution.py
@@ -67,14 +67,14 @@
     return jnp.concatenate(tiles, axis=1)
 
 
-def pack_kernel(place, tokens, cotangent, ids, probs, out):
+def pack_kernel(zone, yi, tokens, cotangent, ids, probs, out):
     count = tokens.shape[1]
-    mine = ids[...] == place[0]
+    mine = ids[...] == zone[0]
     weight = jnp.sum(jnp.where(mine, probs[...], 0.0), axis=0, keepdims=True)
     high = weight.astype(BF16).astype(F32)
     left = jnp.concatenate([tokens[...].astype(F32), high], axis=0)
     right = jnp.concatenate([cotangent[...].astype(F32), weight - high], axis=0)
-    odd = place[1] == 1
+    odd = yi[0] == 1
     first, second = jnp.where(odd, right, left), jnp.where(odd, left, right)
     lower = lax.broadcasted_iota(jnp.int32, (first.shape[0], LANES), 1) < LANES // 2
     for tile in range(count // LANES):
@@ -96,24 +96,28 @@
     out[...] = widen(jnp.concatenate(rows, axis=0).astype(BF16), wide)
 
 
-def grads_kernel(place, own, other, weights, out, inputs, cotangents, near, sems):
+def grads_kernel(core_at, yo_at, own, other, gathered, out, inputs, cotangents, held, weights, sems, weights_sem):
     chips_x, chips_z, blocks, depth, lanes = own.shape
     groups, stacked, wide = weights.shape
     hidden = stacked // 3
-    core, yo = place[0], place[1]
+    core, yo = core_at[0], yo_at[0]
     lower = lax.broadcasted_iota(jnp.int32, (chips_z, depth, lanes), 2) < lanes // 2
-    copies = [pltpu.make_async_copy(own.at[x], near.at[x], sems.at[x]) for x in range(chips_x)]
-    for copy in copies:
+    copies = [
+        [pltpu.make_async_copy(ref.at[x], held.at[s, x], sems.at[s, x]) for x in range(chips_x)]
+        for s, ref in enumerate((own, other))
+    ]
+    weights_copy = pltpu.make_async_copy(gathered, weights, weights_sem)
+    for copy in copies[0] + copies[1] + [weights_copy]:
         copy.start()
-    for ref, slot in ((other, 1 - core), (near, core)):
+    for s, slot in ((0, core), (1, 1 - core)):
         for x in range(chips_x):
-            if ref is near:
-                copies[x].wait()
+            copies[s][x].wait()
             for pair in range(blocks // 2):
-                even, odd = ref[x, :, 2 * pair], ref[x, :, 2 * pair + 1]
+                even, odd = held[s, x, :, 2 * pair], held[s, x, :, 2 * pair + 1]
                 at = slice(pair * lanes, (pair + 1) * lanes)
                 inputs[:, x * CORES + slot, :, at] = jnp.where(lower, even, odd)
                 cotangents[:, x * CORES + slot, :, at] = jnp.where(lower, odd, even)
+    weights_copy.wait()
     total = blocks // 2 * lanes
     rows = inputs[...].reshape(wide, total)
     backs = cotangents[...].reshape(wide, total)
@@ -155,7 +159,11 @@
 VMEM = pl.BlockSpec(memory_space=pltpu.VMEM)
 SMEM = pl.BlockSpec(memory_space=pltpu.SMEM)
 ANY = pl.BlockSpec(memory_space=pl.ANY)
-PARAMS = pltpu.CompilerParams(vmem_limit_bytes=40 * 1024 * 1024)
+HBM = pl.BlockSpec(memory_space=pltpu.HBM)
+
+
+def room(mib):
+    return pltpu.CompilerParams(vmem_limit_bytes=mib * 1024 * 1024)
 
 
 def after(value, earlier):
@@ -165,6 +173,7 @@
         in_specs=[ANY, ANY],
         out_specs=ANY,
         input_output_aliases={0: 0},
+        compiler_params=room(1),
         name="after",
     )(value, earlier)
 
@@ -186,10 +195,10 @@
     packed = pl.pallas_call(
         pack_kernel,
         out_shape=jax.ShapeDtypeStruct((PAIR, pairs_y, PAIR, depth, LANES), BF16),
-        in_specs=[SMEM, VMEM, VMEM, VMEM, VMEM],
+        in_specs=[SMEM, SMEM, VMEM, VMEM, VMEM, VMEM],
         out_specs=VMEM,
         name="pack",
-    )(jnp.stack([zone, lax.axis_index("yi")]), tokens.T, grad_out.T, expert_ids.T, probs.T)
+    )(zone.reshape(1), lax.axis_index("yi").reshape(1), tokens.T, grad_out.T, expert_ids.T, probs.T)
     stacked = pl.pallas_call(
         weights_kernel,
         out_shape=jax.ShapeDtypeStruct((3 * hidden, wide), BF16),
@@ -205,26 +214,28 @@
     along_x = lax.all_to_all(
         jnp.broadcast_to(along_z[None], (chips_x,) + along_z.shape), "x", split_axis=0, concat_axis=0, tiled=True
     )
-    along_x = after(along_x, weights)
+    along_x = after(along_x, weights[0, :16, :LANES])
     crossed = swap(along_x, "core")
 
     tokens_held = pairs_y * LANES
     parts = pl.pallas_call(
         grads_kernel,
         out_shape=jax.ShapeDtypeStruct((groups, 3 * hidden, wide), BF16),
-        in_specs=[SMEM, ANY, VMEM, VMEM],
+        in_specs=[SMEM, SMEM, ANY, ANY, HBM],
         out_specs=VMEM,
         scratch_shapes=[pltpu.VMEM((chips_z, chips_x * CORES, depth, tokens_held), BF16)] * 2
-        + [pltpu.VMEM(along_x.shape, BF16), pltpu.SemaphoreType.DMA((chips_x,))],
-        compiler_params=PARAMS,
+        + [pltpu.VMEM((2,) + along_x.shape, BF16), pltpu.VMEM(weights.shape, BF16)]
+        + [pltpu.SemaphoreType.DMA((2, chips_x)), pltpu.SemaphoreType.DMA],
+        compiler_params=room(20),
         name="grads",
-    )(jnp.stack([lax.axis_index("core"), lax.axis_index("yo")]), along_x, crossed, weights)
+    )(lax.axis_index("core").reshape(1), lax.axis_index("yo").reshape(1), along_x, crossed, weights)
     met = lax.all_to_all(parts, GROUP, split_axis=0, concat_axis=0, tiled=True)
     grad_gate, grad_up, grad_down = pl.pallas_call(
         total_kernel,
         out_shape=[jax.ShapeDtypeStruct((units, features), BF16)] * 3,
         in_specs=[VMEM],
         out_specs=[VMEM] * 3,
+        compiler_params=room(8),
         name="total",
     )(met)
     return grad_gate.T[None], grad_up.T[None], grad_down[None]

time: 118 us -> 116 us (0.983)
  blocking collectives: 62.7 us -> 44 us
  waiting for transfers between devices: 8.45 us -> 21.7 us
  starting transfers between devices: 19.2 us -> 23.1 us
  local copies, waits for them, and re-layouts: 1.77 us -> 3.48 us
    all_to_all x1 -> x0, blocking collectives: 18 us -> none  [shards(): lax.all_to_all(jnp.broadcast_to(along_z[None], (chips_x,) + along_z.shape...]
    all_gather x1, waiting for transfers between devices: 0.01 us -> 10.2 us  [shards(): weights = lax.all_gather(stacked, GROUP)]
    all_to_all x0 -> x1, starting transfers between devices: none -> 4.01 us  [shards(): lax.all_to_all(jnp.broadcast_to(along_z[None], (chips_x,) + along_z.shape...]
    all_to_all x0 -> x1, waiting for transfers between devices: none -> 3.25 us  [shards(): lax.all_to_all(jnp.broadcast_to(along_z[None], (chips_x,) + along_z.shape...]
    pallas_call x1, Pallas kernels: 2.56 us -> 1.3 us  [shards(): pl.pallas_call(total_kernel, out_shape=[jax.ShapeDtypeStruct((units, feat...]
  transfers between devices with their start and end apart: 3 -> 4, of which waited for: 2 -> 4; matrix products, arithmetic and copies ran while one was open for 0% -> 2% of each run, Pallas kernels for 2% -> 2%
where the time goes in v3:
time: 116 us
  blocking collectives  44 us (38%)
  starting transfers between devices  23.1 us (20%)
  waiting for transfers between devices  21.7 us (19%)
  between operations  14.1 us (12%)
  Pallas kernels  9.62 us (8%)
  local copies, waits for them, and re-layouts  3.48 us (3%)
    all_gather x1, blocking collectives, shards(): lax.all_gather(quarter, 'zo').reshape(chips_z, pairs_y * PAIR, depth, LANES)  26.6 us
    all_to_all x1, blocking collectives, shards(): met = lax.all_to_all(parts, GROUP, split_axis=0, concat_axis=0, tiled=True)  17.4 us
    all_gather x1, waiting for transfers between devices, shards(): weights = lax.all_gather(stacked, GROUP)  10.2 us
    all_to_all x1, starting transfers between devices, shards(): lax.all_to_all(sent, ('zi',) + EP, split_axis=0, concat_axis=0, tiled=True)  9.56 us
    ppermute x1, starting transfers between devices, swap(): return lax.ppermute(value, axis, [(0, 1), (1, 0)])  9.47 us
    all_to_all x1, waiting for transfers between devices, shards(): lax.all_to_all(sent, ('zi',) + EP, split_axis=0, concat_axis=0, tiled=True)  5.28 us
    pallas_call x1, Pallas kernels, shards(): pl.pallas_call(grads_kernel, out_shape=jax.ShapeDtypeStruct((groups, 3 *...  4.83 us
    all_to_all x1, starting transfers between devices, shards(): lax.all_to_all(jnp.broadcast_to(along_z[None], (chips_x,) + along_z.shape...  4.01 us
  transfers between devices with their start and end apart: 4, of which 4 were waited for; matrix products, arithmetic and copies ran while one was open for 2% of the time, Pallas kernels for 2%

profile of v3, /device:TPU:1, one launch (start us, length us, event | category | flops | bytes accessed | tf_op | source)
XLA Modules:
  0.0 115.9 jit_solution(6949673801447798547)
XLA Ops:
  7.2 1.5 %pack.1 = bf16[2,4,2,16,128]{4,3,2,1,0:T(8,128)(2,1)} custom-call(s32[1]{0:T(128)} %bitcast.2.zone, s32[1]{0:T(128)} %bitcast.3.yi, bf16[15,256]{1,0:T(8,128)(2,1)} %bitcast.34, bf16[15,256]{1,0:T(8,128)(2,1)} %bitcast.35, s32[4,256]{1,0:T(4,128)} %bitcast.36, f32[4,256]{1,0:T(4,128)} %bitcast.37), custom_call_target="tpu_custom_call" | custom-call | tf_op jit(solution)/shard_map/pack/pallas_call | solution.py:195
  8.6 9.6 %all-to-all-start = ((bf16[16,16,128]{2,1,0:T(8,128)(2,1)}), bf16[16,16,128]{2,1,0:T(8,128)(2,1)S(1)}, u32[]{:S(2)}, u32[]{:S(2)}) async-start(bf16[16,16,128]{2,1,0:T(8,128)(2,1)} %bitcast.30), calls=%async_computation | async-start | bytes 131072 | tf_op jit(solution)/shard_map/all_to_all | solution.py:210
  18.2 0.0 all-gather.4.cloned.1.call-start
  18.3 2.0 %widen_weights.1 = bf16[96,1536]{1,0:T(8,128)(2,1)} custom-call(bf16[30,1440]{1,0:T(8,128)(2,1)} %bitcast.31, bf16[30,1440]{1,0:T(8,128)(2,1)} %bitcast.32, bf16[30,1440]{1,0:T(8,128)(2,1)} %bitcast.33), custom_call_target="tpu_custom_call" | custom-call | tf_op jit(solution)/shard_map/widen_weights/pallas_call | solution.py:202
  20.3 5.3 %all-to-all-done = bf16[16,16,128]{2,1,0:T(8,128)(2,1)S(1)} async-done(((bf16[16,16,128]{2,1,0:T(8,128)(2,1)}), bf16[16,16,128]{2,1,0:T(8,128)(2,1)S(1)}, u32[]{:S(2)}, u32[]{:S(2)}) %all-to-all-start) | async-done | bytes 65568 | tf_op jit(solution)/shard_map/all_to_all | solution.py:210
  25.6 0.0 all-gather.4.cloned.1.call-update
  25.6 26.6 %all-gather = bf16[96,16,128]{2,1,0:T(8,128)(2,1)S(1)} all-gather(bf16[16,16,128]{2,1,0:T(8,128)(2,1)S(1)} %all-to-all-done), channel_id=2, replica_groups=mesh['zo'=6,'zi'=2,'x'=4,'core'=2,'yo'=4,'yi'=2] {'zo'}, dimensions={0}, use_global_device_ids=true | all-gather | bytes 458752 | tf_op jit(solution)/shard_map/all_gather | solution.py:213
  52.2 1.5 %broadcast_in_dim.17 = bf16[4,12,8,16,128]{4,3,2,1,0:T(8,128)(2,1)} broadcast(bf16[12,8,16,128]{3,2,1,0:T(8,128)(2,1)S(1)} %bitcast.29), dimensions={1,2,3,4} | broadcast | bytes 1966080 | tf_op jit(solution)/shard_map/broadcast_in_dim | solution.py:215
  53.7 4.0 %all-to-all-start.1 = ((bf16[4,12,8,16,128]{4,3,2,1,0:T(8,128)(2,1)}), bf16[4,12,8,16,128]{4,3,2,1,0:T(8,128)(2,1)S(1)}, u32[]{:S(2)}, u32[]{:S(2)}) async-start(bf16[4,12,8,16,128]{4,3,2,1,0:T(8,128)(2,1)} %broadcast_in_dim.17), calls=%async_computation.1 | async-start | bytes 3145728 | tf_op jit(solution)/shard_map/all_to_all | solution.py:214
  57.7 10.2 %all-gather.4.cloned.1.call-done = bf16[384,1536]{1,0:T(8,128)(2,1)} async-done(((bf16[96,1536]{1,0:T(8,128)(2,1)}), bf16[384,1536]{1,0:T(8,128)(2,1)}) %all-gather.4.cloned.1.call-update) | async-done | bytes 1179664 | tf_op jit(solution)/shard_map/all_gather | solution.py:212
  67.9 0.7 slice_bitcast_fusion.earlier_ref
  68.6 3.2 %all-to-all-done.1.value_ref = bf16[4,12,8,16,128]{4,3,2,1,0:T(8,128)(2,1)S(1)} async-done(((bf16[4,12,8,16,128]{4,3,2,1,0:T(8,128)(2,1)}), bf16[4,12,8,16,128]{4,3,2,1,0:T(8,128)(2,1)S(1)}, u32[]{:S(2)}, u32[]{:S(2)}) %all-to-all-start.1) | async-done | bytes 1572896 | tf_op jit(solution)/shard_map/all_to_all | solution.py:214
  71.8 9.5 %collective-permute-start = (bf16[4,12,8,16,128]{4,3,2,1,0:T(8,128)(2,1)S(1)}, bf16[4,12,8,16,128]{4,3,2,1,0:T(8,128)(2,1)S(1)}, u32[]{:S(2)}, u32[]{:S(2)}) collective-permute-start(bf16[4,12,8,16,128]{4,3,2,1,0:T(8,128)(2,1)S(1)} %after.1.own), channel_id=1, source_target_pairs={{0,8},{8,0},{1,9},{9,1},{2,10},{10,2},{3,11},{11,3},{4,12},{12,4},... | collective-permute-start | bytes 4718600 | tf_op jit(solution)/shard_map/ppermute | solution.py:182
  81.3 3.0 %collective-permute-done.other = bf16[4,12,8,16,128]{4,3,2,1,0:T(8,128)(2,1)S(1)} collective-permute-done((bf16[4,12,8,16,128]{4,3,2,1,0:T(8,128)(2,1)S(1)}, bf16[4,12,8,16,128]{4,3,2,1,0:T(8,128)(2,1)S(1)}, u32[]{:S(2)}, u32[]{:S(2)}) %collective-permute-start) | collective-permute-done | bytes 1572896 | tf_op jit(solution)/shard_map/ppermute | solution.py:182
  84.3 0.0 copy-start
  84.3 1.3 %copy-done = bf16[384,1536]{1,0:T(8,128)(2,1)S(1)} copy-done((bf16[384,1536]{1,0:T(8,128)(2,1)S(1)}, bf16[384,1536]{1,0:T(8,128)(2,1)}, u32[]{:S(2)}) %copy-start) | copy-done | bytes 1179672
  85.6 4.8 %grads.1 = bf16[4,96,1536]{2,1,0:T(8,128)(2,1)S(1)} custom-call(s32[1]{0:T(128)} %bitcast.core_at, s32[1]{0:T(128)} %bitcast.1.yo_at, bf16[4,12,8,16,128]{4,3,2,1,0:T(8,128)(2,1)S(1)} %after.1.own, bf16[4,12,8,16,128]{4,3,2,1,0:T(8,128)(2,1)S(1)} %collective-permute-done.other, bf16[4,96,1536]{2,1,0:T(8,128)(2,1)S(1)} %bitcast.28), custom_call_target="tpu_custom_call" | custom-call | tf_op jit(solution)/shard_map/grads/pallas_call | solution.py:221
  90.4 17.4 %all_to_all.15.parts = bf16[4,96,1536]{2,1,0:T(8,128)(2,1)S(1)} all-to-all(bf16[4,96,1536]{2,1,0:T(8,128)(2,1)S(1)} %grads.1), channel_id=1, replica_groups=mesh['zo'=6,'zi'=2,'x'=4,'core'=2,'yo'=4,'yi'=2] {'zi','yi'}, dimensions={0} | all-to-all | bytes 2359296 | tf_op jit(solution)/shard_map/all_to_all | solution.py:232
  107.8 1.3 %total.1 = (bf16[30,1440]{1,0:T(8,128)(2,1)}, bf16[30,1440]{1,0:T(8,128)(2,1)}, bf16[30,1440]{1,0:T(8,128)(2,1)}) custom-call(bf16[4,96,1536]{2,1,0:T(8,128)(2,1)S(1)} %all_to_all.15.parts), custom_call_target="tpu_custom_call" | custom-call | tf_op jit(solution)/shard_map/total/pallas_call | solution.py:233
  (1 shorter events, 0.0 us)
Async XLA Ops:
  8.6 16.9 %all-to-all-start = ((bf16[16,16,128]{2,1,0:T(8,128)(2,1)}), bf16[16,16,128]{2,1,0:T(8,128)(2,1)S(1)}, u32[]{:S(2)}, u32[]{:S(2)}) async-start(bf16[16,16,128]{2,1,0:T(8,128)(2,1)} %bitcast.30), calls=%async_computation | async-start | bytes 131072 | tf_op jit(solution)/shard_map/all_to_all | solution.py:210
  18.2 49.7 %all-gather.4.cloned.1.call-start = ((), (), s32[]{:S(2)}) async-start(), calls=%async_computation.3 | async-start | bytes 1474560 | tf_op jit(solution)/shard_map/all_gather | solution.py:212
  53.7 18.1 %all-to-all-start.1 = ((bf16[4,12,8,16,128]{4,3,2,1,0:T(8,128)(2,1)}), bf16[4,12,8,16,128]{4,3,2,1,0:T(8,128)(2,1)S(1)}, u32[]{:S(2)}, u32[]{:S(2)}) async-start(bf16[4,12,8,16,128]{4,3,2,1,0:T(8,128)(2,1)} %broadcast_in_dim.17), calls=%async_computation.1 | async-start | bytes 3145728 | tf_op jit(solution)/shard_map/all_to_all | solution.py:214
  71.8 12.5 %collective-permute-start = (bf16[4,12,8,16,128]{4,3,2,1,0:T(8,128)(2,1)S(1)}, bf16[4,12,8,16,128]{4,3,2,1,0:T(8,128)(2,1)S(1)}, u32[]{:S(2)}, u32[]{:S(2)}) collective-permute-start(bf16[4,12,8,16,128]{4,3,2,1,0:T(8,128)(2,1)S(1)} %after.1.own), channel_id=1, source_target_pairs={{0,8},{8,0},{1,9},{9,1},{2,10},{10,2},{3,11},{11,3},{4,12},{12,4},... | collective-permute-start | bytes 4718600 | tf_op jit(solution)/shard_map/ppermute | solution.py:182
  84.3 1.3 %copy-start = (bf16[384,1536]{1,0:T(8,128)(2,1)S(1)}, bf16[384,1536]{1,0:T(8,128)(2,1)}, u32[]{:S(2)}) copy-start(bf16[384,1536]{1,0:T(8,128)(2,1)} %all-gather.4.cloned.1.call-done) | copy-start | bytes 3538948
Sparse Core Ops, SparseCore 0:
  25.7 42.1 all-gather.3

commit v4 on v3

--- a/solution.py
+++ b/solution.py
@@ -96,29 +96,23 @@
     out[...] = widen(jnp.concatenate(rows, axis=0).astype(BF16), wide)
 
 
-def grads_kernel(core_at, yo_at, own, other, gathered, out, inputs, cotangents, held, weights, sems, weights_sem):
-    chips_x, chips_z, blocks, depth, lanes = own.shape
+def grads_kernel(core_at, x_at, yo_at, *refs):
+    blocks, (weights, out, inputs, cotangents) = refs[:-4], refs[-4:]
+    chips_x = len(blocks) // CORES
+    chips_z, tokens_y, depth, lanes = blocks[0].shape
     groups, stacked, wide = weights.shape
     hidden = stacked // 3
-    core, yo = core_at[0], yo_at[0]
+    core, x, yo = core_at[0], x_at[0], yo_at[0]
     lower = lax.broadcasted_iota(jnp.int32, (chips_z, depth, lanes), 2) < lanes // 2
-    copies = [
-        [pltpu.make_async_copy(ref.at[x], held.at[s, x], sems.at[s, x]) for x in range(chips_x)]
-        for s, ref in enumerate((own, other))
-    ]
-    weights_copy = pltpu.make_async_copy(gathered, weights, weights_sem)
-    for copy in copies[0] + copies[1] + [weights_copy]:
-        copy.start()
-    for s, slot in ((0, core), (1, 1 - core)):
-        for x in range(chips_x):
-            copies[s][x].wait()
-            for pair in range(blocks // 2):
-                even, odd = held[s, x, :, 2 * pair], held[s, x, :, 2 * pair + 1]
-                at = slice(pair * lanes, (pair + 1) * lanes)
-                inputs[:, x * CORES + slot, :, at] = jnp.where(lower, even, odd)
-                cotangents[:, x * CORES + slot, :, at] = jnp.where(lower, odd, even)
-    weights_copy.wait()
-    total = blocks // 2 * lanes
+    for k, ref in enumerate(blocks):
+        steps, crossed = divmod(k, CORES)
+        slot = lax.rem(x + chips_x - steps, chips_x) * CORES + (1 - core if crossed else core)
+        for pair in range(tokens_y // 2):
+            even, odd = ref[:, 2 * pair], ref[:, 2 * pair + 1]
+            at = slice(pair * lanes, (pair + 1) * lanes)
+            inputs[:, slot, :, at] = jnp.where(lower, even, odd)
+            cotangents[:, slot, :, at] = jnp.where(lower, odd, even)
+    total = tokens_y // 2 * lanes
     rows = inputs[...].reshape(wide, total)
     backs = cotangents[...].reshape(wide, total)
 
@@ -158,24 +152,10 @@
 
 VMEM = pl.BlockSpec(memory_space=pltpu.VMEM)
 SMEM = pl.BlockSpec(memory_space=pltpu.SMEM)
-ANY = pl.BlockSpec(memory_space=pl.ANY)
-HBM = pl.BlockSpec(memory_space=pltpu.HBM)
 
 
 def room(mib):
     return pltpu.CompilerParams(vmem_limit_bytes=mib * 1024 * 1024)
-
-
-def after(value, earlier):
-    return pl.pallas_call(
-        lambda value_ref, earlier_ref, out_ref: None,
-        out_shape=jax.ShapeDtypeStruct(value.shape, value.dtype),
-        in_specs=[ANY, ANY],
-        out_specs=ANY,
-        input_output_aliases={0: 0},
-        compiler_params=room(1),
-        name="after",
-    )(value, earlier)
 
 
 def swap(value, axis):
@@ -211,24 +191,21 @@
     quarter, stacked = lax.optimization_barrier((quarter, stacked))
     weights = lax.all_gather(stacked, GROUP)
     along_z = lax.all_gather(quarter, "zo").reshape(chips_z, pairs_y * PAIR, depth, LANES)
-    along_x = lax.all_to_all(
-        jnp.broadcast_to(along_z[None], (chips_x,) + along_z.shape), "x", split_axis=0, concat_axis=0, tiled=True
-    )
-    along_x = after(along_x, weights[0, :16, :LANES])
-    crossed = swap(along_x, "core")
-
-    tokens_held = pairs_y * LANES
+    blocks = []
+    for steps in range(chips_x):
+        along = [(i, (i + steps) % chips_x) for i in range(chips_x)]
+        block = lax.ppermute(along_z, "x", along) if steps else along_z
+        blocks += [block, swap(block, "core")]
+
     parts = pl.pallas_call(
         grads_kernel,
         out_shape=jax.ShapeDtypeStruct((groups, 3 * hidden, wide), BF16),
-        in_specs=[SMEM, SMEM, ANY, ANY, HBM],
+        in_specs=[SMEM] * 3 + [VMEM] * (len(blocks) + 1),
         out_specs=VMEM,
-        scratch_shapes=[pltpu.VMEM((chips_z, chips_x * CORES, depth, tokens_held), BF16)] * 2
-        + [pltpu.VMEM((2,) + along_x.shape, BF16), pltpu.VMEM(weights.shape, BF16)]
-        + [pltpu.SemaphoreType.DMA((2, chips_x)), pltpu.SemaphoreType.DMA],
+        scratch_shapes=[pltpu.VMEM((chips_z, chips_x * CORES, depth, pairs_y * LANES), BF16)] * 2,
         compiler_params=room(20),
         name="grads",
-    )(lax.axis_index("core").reshape(1), lax.axis_index("yo").reshape(1), along_x, crossed, weights)
+    )(*(lax.axis_index(axis).reshape(1) for axis in ("core", "x", "yo")), *blocks, weights)
     met = lax.all_to_all(parts, GROUP, split_axis=0, concat_axis=0, tiled=True)
     grad_gate, grad_up, grad_down = pl.pallas_call(
         total_kernel,

time: 116 us -> 114 us (0.983)
  starting transfers between devices: 23.1 us -> 39.2 us
  waiting for transfers between devices: 21.7 us -> 6.64 us
  local copies, waits for them, and re-layouts: 3.48 us -> 1.27 us
  Pallas kernels: 9.62 us -> 8.01 us
    ppermute x1 -> x4, starting transfers between devices: 9.47 us -> 20.2 us  [swap(): return lax.ppermute(value, axis, [(0, 1), (1, 0)])]
    all_gather x1, waiting for transfers between devices: 10.2 us -> 0.01 us  [shards(): weights = lax.all_gather(stacked, GROUP)]
    ppermute x0 -> x3, starting transfers between devices: none -> 9.32 us  [shards(): block = lax.ppermute(along_z, 'x', along) if steps else along_z]
    all_to_all x1 -> x0, starting transfers between devices: 4.01 us -> none  [shards(): lax.all_to_all(jnp.broadcast_to(along_z[None], (chips_x,) + along_z.shape...]
    all_to_all x1 -> x0, waiting for transfers between devices: 3.25 us -> none  [shards(): lax.all_to_all(jnp.broadcast_to(along_z[None], (chips_x,) + along_z.shape...]
    ppermute x1 -> x4, waiting for transfers between devices: 3.01 us -> 1.3 us  [swap(): return lax.ppermute(value, axis, [(0, 1), (1, 0)])]
    pallas_call x1, Pallas kernels: 4.83 us -> 3.25 us  [shards(): pl.pallas_call(grads_kernel, out_shape=jax.ShapeDtypeStruct((groups, 3 *...]
    broadcast_in_dim x1 -> x0, local copies, waits for them, and re-layouts: 1.53 us -> none  [shards(): jnp.broadcast_to(along_z[None], (chips_x,) + along_z.shape)]
  transfers between devices with their start and end apart: 4 -> 9, of which waited for: 4 -> 2; matrix products, arithmetic and copies ran while one was open for 2% -> 0% of each run, Pallas kernels for 2% -> 2%
where the time goes in v4:
time: 114 us; the launch traced here: 113 us
  blocking collectives  44 us (39%)
  starting transfers between devices  39.2 us (34%)
  between operations  14.2 us (12%)
  Pallas kernels  8.01 us (7%)
  waiting for transfers between devices  6.64 us (6%)
  local copies, waits for them, and re-layouts  1.27 us (1%)
    all_gather x1, blocking collectives, shards(): lax.all_gather(quarter, 'zo').reshape(chips_z, pairs_y * PAIR, depth, LANES)  26.6 us
    ppermute x4, starting transfers between devices, swap(): return lax.ppermute(value, axis, [(0, 1), (1, 0)])  20.2 us
    all_to_all x1, blocking collectives, shards(): met = lax.all_to_all(parts, GROUP, split_axis=0, concat_axis=0, tiled=True)  17.4 us
    all_to_all x1, starting transfers between devices, shards(): lax.all_to_all(sent, ('zi',) + EP, split_axis=0, concat_axis=0, tiled=True)  9.56 us
    ppermute x3, starting transfers between devices, shards(): block = lax.ppermute(along_z, 'x', along) if steps else along_z  9.32 us
    all_to_all x1, waiting for transfers between devices, shards(): lax.all_to_all(sent, ('zi',) + EP, split_axis=0, concat_axis=0, tiled=True)  5.32 us
    pallas_call x1, Pallas kernels, shards(): pl.pallas_call(grads_kernel, out_shape=jax.ShapeDtypeStruct((groups, 3 *...  3.25 us
  transfers between devices with their start and end apart: 9, of which 2 were waited for; matrix products, arithmetic and copies ran while one was open for 0% of the time, Pallas kernels for 2%

profile of v4, /device:TPU:1, one launch (start us, length us, event | category | flops | bytes accessed | tf_op | source)
XLA Modules:
  0.0 113.2 jit_solution(11059231661387090661)
XLA Ops:
  7.2 1.5 %pack.1 = bf16[2,4,2,16,128]{4,3,2,1,0:T(8,128)(2,1)} custom-call(s32[1]{0:T(128)} %bitcast.3.zone, s32[1]{0:T(128)} %bitcast.4.yi, bf16[15,256]{1,0:T(8,128)(2,1)} %bitcast.36, bf16[15,256]{1,0:T(8,128)(2,1)} %bitcast.37, s32[4,256]{1,0:T(4,128)} %bitcast.38, f32[4,256]{1,0:T(4,128)} %bitcast.39), custom_call_target="tpu_custom_call" | custom-call | tf_op jit(solution)/shard_map/pack/pallas_call | solution.py:175
  8.6 9.6 %all-to-all-start = ((bf16[16,16,128]{2,1,0:T(8,128)(2,1)}), bf16[16,16,128]{2,1,0:T(8,128)(2,1)S(1)}, u32[]{:S(2)}, u32[]{:S(2)}) async-start(bf16[16,16,128]{2,1,0:T(8,128)(2,1)} %bitcast.32), calls=%async_computation | async-start | bytes 131072 | tf_op jit(solution)/shard_map/all_to_all | solution.py:190
  18.2 0.0 all-gather.4.cloned.1.call-start
  18.3 2.0 %widen_weights.1 = bf16[96,1536]{1,0:T(8,128)(2,1)} custom-call(bf16[30,1440]{1,0:T(8,128)(2,1)} %bitcast.33, bf16[30,1440]{1,0:T(8,128)(2,1)} %bitcast.34, bf16[30,1440]{1,0:T(8,128)(2,1)} %bitcast.35), custom_call_target="tpu_custom_call" | custom-call | tf_op jit(solution)/shard_map/widen_weights/pallas_call | solution.py:182
  20.3 5.3 %all-to-all-done = bf16[16,16,128]{2,1,0:T(8,128)(2,1)S(1)} async-done(((bf16[16,16,128]{2,1,0:T(8,128)(2,1)}), bf16[16,16,128]{2,1,0:T(8,128)(2,1)S(1)}, u32[]{:S(2)}, u32[]{:S(2)}) %all-to-all-start) | async-done | bytes 65568 | tf_op jit(solution)/shard_map/all_to_all | solution.py:190
  25.6 0.0 all-gather.4.cloned.1.call-update
  25.6 26.6 %all-gather = bf16[96,16,128]{2,1,0:T(8,128)(2,1)S(1)} all-gather(bf16[16,16,128]{2,1,0:T(8,128)(2,1)S(1)} %all-to-all-done), channel_id=2, replica_groups=mesh['zo'=6,'zi'=2,'x'=4,'core'=2,'yo'=4,'yi'=2] {'zo'}, dimensions={0}, use_global_device_ids=true | all-gather | bytes 458752 | tf_op jit(solution)/shard_map/all_gather | solution.py:193
  52.2 4.4 %collective-permute-start.5 = (bf16[12,8,16,128]{3,2,1,0:T(8,128)(2,1)S(1)}, bf16[12,8,16,128]{3,2,1,0:T(8,128)(2,1)S(1)}, u32[]{:S(2)}, u32[]{:S(2)}) collective-permute-start(bf16[12,8,16,128]{3,2,1,0:T(8,128)(2,1)S(1)} %bitcast.26), channel_id=1, source_target_pairs={{0,48},{16,0},{32,16},{48,32},{1,49},{17,1},{33,17},{49,33},{2,50}... | collective-permute-start | bytes 1179656 | tf_op jit(solution)/shard_map/ppermute | solution.py:197
  56.6 2.4 %collective-permute-start.3 = (bf16[12,8,16,128]{3,2,1,0:T(8,128)(2,1)S(1)}, bf16[12,8,16,128]{3,2,1,0:T(8,128)(2,1)S(1)}, u32[]{:S(2)}, u32[]{:S(2)}) collective-permute-start(bf16[12,8,16,128]{3,2,1,0:T(8,128)(2,1)S(1)} %bitcast.27), channel_id=1, source_target_pairs={{0,32},{16,48},{32,0},{48,16},{1,33},{17,49},{33,1},{49,17},{2,34}... | collective-permute-start | bytes 1179656 | tf_op jit(solution)/shard_map/ppermute | solution.py:197
  59.0 2.5 %collective-permute-start.1 = (bf16[12,8,16,128]{3,2,1,0:T(8,128)(2,1)S(1)}, bf16[12,8,16,128]{3,2,1,0:T(8,128)(2,1)S(1)}, u32[]{:S(2)}, u32[]{:S(2)}) collective-permute-start(bf16[12,8,16,128]{3,2,1,0:T(8,128)(2,1)S(1)} %bitcast.28), channel_id=1, source_target_pairs={{0,16},{16,32},{32,48},{48,0},{1,17},{17,33},{33,49},{49,1},{2,18}... | collective-permute-start | bytes 1179656 | tf_op jit(solution)/shard_map/ppermute | solution.py:197
  61.5 8.8 %collective-permute-start = (bf16[12,8,16,128]{3,2,1,0:T(8,128)(2,1)S(1)}, bf16[12,8,16,128]{3,2,1,0:T(8,128)(2,1)S(1)}, u32[]{:S(2)}, u32[]{:S(2)}) collective-permute-start(bf16[12,8,16,128]{3,2,1,0:T(8,128)(2,1)S(1)} %bitcast.29), channel_id=1, source_target_pairs={{0,8},{8,0},{1,9},{9,1},{2,10},{10,2},{3,11},{11,3},{4,12},{12,4},... | collective-permute-start | bytes 1179656 | tf_op jit(solution)/shard_map/ppermute | solution.py:162
  70.4 0.0 collective-permute-done.5.refs_6_
  70.4 5.9 %collective-permute-start.6 = (bf16[12,8,16,128]{3,2,1,0:T(8,128)(2,1)S(1)}, bf16[12,8,16,128]{3,2,1,0:T(8,128)(2,1)S(1)}, u32[]{:S(2)}, u32[]{:S(2)}) collective-permute-start(bf16[12,8,16,128]{3,2,1,0:T(8,128)(2,1)S(1)} %collective-permute-done.5.refs_6_), channel_id=1, source_target_pairs={{0,8},{8,0},{1,9},{9,1},{2,10},{10,2},{3,11},{11,3},{4,12},{12,4},... | collective-permute-start | bytes 1179656 | tf_op jit(solution)/shard_map/ppermute | solution.py:162
  76.3 0.0 collective-permute-done.3.refs_4_
  76.3 1.9 %collective-permute-start.4 = (bf16[12,8,16,128]{3,2,1,0:T(8,128)(2,1)S(1)}, bf16[12,8,16,128]{3,2,1,0:T(8,128)(2,1)S(1)}, u32[]{:S(2)}, u32[]{:S(2)}) collective-permute-start(bf16[12,8,16,128]{3,2,1,0:T(8,128)(2,1)S(1)} %collective-permute-done.3.refs_4_), channel_id=1, source_target_pairs={{0,8},{8,0},{1,9},{9,1},{2,10},{10,2},{3,11},{11,3},{4,12},{12,4},... | collective-permute-start | bytes 1179656 | tf_op jit(solution)/shard_map/ppermute | solution.py:162
  78.2 0.0 collective-permute-done.1.refs_2_
  78.2 3.6 %collective-permute-start.2 = (bf16[12,8,16,128]{3,2,1,0:T(8,128)(2,1)S(1)}, bf16[12,8,16,128]{3,2,1,0:T(8,128)(2,1)S(1)}, u32[]{:S(2)}, u32[]{:S(2)}) collective-permute-start(bf16[12,8,16,128]{3,2,1,0:T(8,128)(2,1)S(1)} %collective-permute-done.1.refs_2_), channel_id=1, source_target_pairs={{0,8},{8,0},{1,9},{9,1},{2,10},{10,2},{3,11},{11,3},{4,12},{12,4},... | collective-permute-start | bytes 1179656 | tf_op jit(solution)/shard_map/ppermute | solution.py:162
  81.8 0.0 collective-permute-done.refs_1_
  81.9 0.0 collective-permute-done.6.refs_7_
  81.9 0.0 collective-permute-done.4.refs_5_
  81.9 1.3 %collective-permute-done.2.refs_3_ = bf16[12,8,16,128]{3,2,1,0:T(8,128)(2,1)S(1)} collective-permute-done((bf16[12,8,16,128]{3,2,1,0:T(8,128)(2,1)S(1)}, bf16[12,8,16,128]{3,2,1,0:T(8,128)(2,1)S(1)}, u32[]{:S(2)}, u32[]{:S(2)}) %collective-permute-start.2) | collective-permute-done | bytes 393248 | tf_op jit(solution)/shard_map/ppermute | solution.py:162
  83.2 0.0 all-gather.4.cloned.1.call-done
  83.2 0.0 copy-start
  83.2 1.3 %copy-done = bf16[384,1536]{1,0:T(8,128)(2,1)S(1)} copy-done((bf16[384,1536]{1,0:T(8,128)(2,1)S(1)}, bf16[384,1536]{1,0:T(8,128)(2,1)}, u32[]{:S(2)}) %copy-start) | copy-done | bytes 1179672
  84.4 3.2 %grads.1 = bf16[4,96,1536]{2,1,0:T(8,128)(2,1)S(1)} custom-call(s32[1]{0:T(128)} %bitcast.core_at, s32[1]{0:T(128)} %bitcast.1.x_at, s32[1]{0:T(128)} %bitcast.2.yo_at, bf16[12,8,16,128]{3,2,1,0:T(8,128)(2,1)S(1)} %bitcast.30, bf16[12,8,16,128]{3,2,1,0:T(8,128)(2,1)S(1)} %collective-permute-done.refs_1_, ...), custom_call_target="tpu_custom_call" | custom-call | tf_op jit(solution)/shard_map/grads/pallas_call | solution.py:200
  87.7 17.4 %all_to_all.10.parts = bf16[4,96,1536]{2,1,0:T(8,128)(2,1)S(1)} all-to-all(bf16[4,96,1536]{2,1,0:T(8,128)(2,1)S(1)} %grads.1), channel_id=1, replica_groups=mesh['zo'=6,'zi'=2,'x'=4,'core'=2,'yo'=4,'yi'=2] {'zi','yi'}, dimensions={0} | all-to-all | bytes 2359296 | tf_op jit(solution)/shard_map/all_to_all | solution.py:209
  105.1 1.3 %total.1 = (bf16[30,1440]{1,0:T(8,128)(2,1)}, bf16[30,1440]{1,0:T(8,128)(2,1)}, bf16[30,1440]{1,0:T(8,128)(2,1)}) custom-call(bf16[4,96,1536]{2,1,0:T(8,128)(2,1)S(1)} %all_to_all.10.parts), custom_call_target="tpu_custom_call" | custom-call | tf_op jit(solution)/shard_map/total/pallas_call | solution.py:210
Async XLA Ops:
  8.6 16.9 %all-to-all-start = ((bf16[16,16,128]{2,1,0:T(8,128)(2,1)}), bf16[16,16,128]{2,1,0:T(8,128)(2,1)S(1)}, u32[]{:S(2)}, u32[]{:S(2)}) async-start(bf16[16,16,128]{2,1,0:T(8,128)(2,1)} %bitcast.32), calls=%async_computation | async-start | bytes 131072 | tf_op jit(solution)/shard_map/all_to_all | solution.py:190
  18.2 65.0 %all-gather.4.cloned.1.call-start = ((), (), s32[]{:S(2)}) async-start(), calls=%async_computation.2 | async-start | bytes 1474560 | tf_op jit(solution)/shard_map/all_gather | solution.py:192
  52.2 18.2 %collective-permute-start.5 = (bf16[12,8,16,128]{3,2,1,0:T(8,128)(2,1)S(1)}, bf16[12,8,16,128]{3,2,1,0:T(8,128)(2,1)S(1)}, u32[]{:S(2)}, u32[]{:S(2)}) collective-permute-start(bf16[12,8,16,128]{3,2,1,0:T(8,128)(2,1)S(1)} %bitcast.26), channel_id=1, source_target_pairs={{0,48},{16,0},{32,16},{48,32},{1,49},{17,1},{33,17},{49,33},{2,50}... | collective-permute-start | bytes 1179656 | tf_op jit(solution)/shard_map/ppermute | solution.py:197
  56.6 19.7 %collective-permute-start.3 = (bf16[12,8,16,128]{3,2,1,0:T(8,128)(2,1)S(1)}, bf16[12,8,16,128]{3,2,1,0:T(8,128)(2,1)S(1)}, u32[]{:S(2)}, u32[]{:S(2)}) collective-permute-start(bf16[12,8,16,128]{3,2,1,0:T(8,128)(2,1)S(1)} %bitcast.27), channel_id=1, source_target_pairs={{0,32},{16,48},{32,0},{48,16},{1,33},{17,49},{33,1},{49,17},{2,34}... | collective-permute-start | bytes 1179656 | tf_op jit(solution)/shard_map/ppermute | solution.py:197
  59.0 19.2 %collective-permute-start.1 = (bf16[12,8,16,128]{3,2,1,0:T(8,128)(2,1)S(1)}, bf16[12,8,16,128]{3,2,1,0:T(8,128)(2,1)S(1)}, u32[]{:S(2)}, u32[]{:S(2)}) collective-permute-start(bf16[12,8,16,128]{3,2,1,0:T(8,128)(2,1)S(1)} %bitcast.28), channel_id=1, source_target_pairs={{0,16},{16,32},{32,48},{48,0},{1,17},{17,33},{33,49},{49,1},{2,18}... | collective-permute-start | bytes 1179656 | tf_op jit(solution)/shard_map/ppermute | solution.py:197
  61.5 20.3 %collective-permute-start = (bf16[12,8,16,128]{3,2,1,0:T(8,128)(2,1)S(1)}, bf16[12,8,16,128]{3,2,1,0:T(8,128)(2,1)S(1)}, u32[]{:S(2)}, u32[]{:S(2)}) collective-permute-start(bf16[12,8,16,128]{3,2,1,0:T(8,128)(2,1)S(1)} %bitcast.29), channel_id=1, source_target_pairs={{0,8},{8,0},{1,9},{9,1},{2,10},{10,2},{3,11},{11,3},{4,12},{12,4},... | collective-permute-start | bytes 1179656 | tf_op jit(solution)/shard_map/ppermute | solution.py:162
  70.4 11.5 %collective-permute-start.6 = (bf16[12,8,16,128]{3,2,1,0:T(8,128)(2,1)S(1)}, bf16[12,8,16,128]{3,2,1,0:T(8,128)(2,1)S(1)}, u32[]{:S(2)}, u32[]{:S(2)}) collective-permute-start(bf16[12,8,16,128]{3,2,1,0:T(8,128)(2,1)S(1)} %collective-permute-done.5.refs_6_), channel_id=1, source_target_pairs={{0,8},{8,0},{1,9},{9,1},{2,10},{10,2},{3,11},{11,3},{4,12},{12,4},... | collective-permute-start | bytes 1179656 | tf_op jit(solution)/shard_map/ppermute | solution.py:162
  76.3 5.6 %collective-permute-start.4 = (bf16[12,8,16,128]{3,2,1,0:T(8,128)(2,1)S(1)}, bf16[12,8,16,128]{3,2,1,0:T(8,128)(2,1)S(1)}, u32[]{:S(2)}, u32[]{:S(2)}) collective-permute-start(bf16[12,8,16,128]{3,2,1,0:T(8,128)(2,1)S(1)} %collective-permute-done.3.refs_4_), channel_id=1, source_target_pairs={{0,8},{8,0},{1,9},{9,1},{2,10},{10,2},{3,11},{11,3},{4,12},{12,4},... | collective-permute-start | bytes 1179656 | tf_op jit(solution)/shard_map/ppermute | solution.py:162
  78.2 5.0 %collective-permute-start.2 = (bf16[12,8,16,128]{3,2,1,0:T(8,128)(2,1)S(1)}, bf16[12,8,16,128]{3,2,1,0:T(8,128)(2,1)S(1)}, u32[]{:S(2)}, u32[]{:S(2)}) collective-permute-start(bf16[12,8,16,128]{3,2,1,0:T(8,128)(2,1)S(1)} %collective-permute-done.1.refs_2_), channel_id=1, source_target_pairs={{0,8},{8,0},{1,9},{9,1},{2,10},{10,2},{3,11},{11,3},{4,12},{12,4},... | collective-permute-start | bytes 1179656 | tf_op jit(solution)/shard_map/ppermute | solution.py:162
  83.2 1.3 %copy-start = (bf16[384,1536]{1,0:T(8,128)(2,1)S(1)}, bf16[384,1536]{1,0:T(8,128)(2,1)}, u32[]{:S(2)}) copy-start(bf16[384,1536]{1,0:T(8,128)(2,1)} %all-gather.4.cloned.1.call-done) | copy-start | bytes 3538948
Sparse Core Ops, SparseCore 0:
  25.7 42.1 all-gather.3

commit v5 on v4

--- a/solution.py
+++ b/solution.py
@@ -96,22 +96,26 @@
     out[...] = widen(jnp.concatenate(rows, axis=0).astype(BF16), wide)
 
 
-def grads_kernel(core_at, x_at, yo_at, *refs):
+def grads_kernel(core_at, x_at, yo_at, zo_at, *refs):
     blocks, (weights, out, inputs, cotangents) = refs[:-4], refs[-4:]
     chips_x = len(blocks) // CORES
     chips_z, tokens_y, depth, lanes = blocks[0].shape
     groups, stacked, wide = weights.shape
     hidden = stacked // 3
-    core, x, yo = core_at[0], x_at[0], yo_at[0]
-    lower = lax.broadcasted_iota(jnp.int32, (chips_z, depth, lanes), 2) < lanes // 2
+    core, x, yo, zo = core_at[0], x_at[0], yo_at[0], zo_at[0]
+    pairs_z = chips_z // PAIR
+    lower = lax.broadcasted_iota(jnp.int32, (PAIR, depth, lanes), 2) < lanes // 2
     for k, ref in enumerate(blocks):
         steps, crossed = divmod(k, CORES)
         slot = lax.rem(x + chips_x - steps, chips_x) * CORES + (1 - core if crossed else core)
-        for pair in range(tokens_y // 2):
-            even, odd = ref[:, 2 * pair], ref[:, 2 * pair + 1]
-            at = slice(pair * lanes, (pair + 1) * lanes)
-            inputs[:, slot, :, at] = jnp.where(lower, even, odd)
-            cotangents[:, slot, :, at] = jnp.where(lower, odd, even)
+        for back in range(pairs_z):
+            source = pl.ds(back * PAIR, PAIR)
+            target = pl.ds(lax.rem(zo + pairs_z - back, pairs_z) * PAIR, PAIR)
+            for pair in range(tokens_y // 2):
+                even, odd = ref[source, 2 * pair], ref[source, 2 * pair + 1]
+                at = slice(pair * lanes, (pair + 1) * lanes)
+                inputs[target, slot, :, at] = jnp.where(lower, even, odd)
+                cotangents[target, slot, :, at] = jnp.where(lower, odd, even)
     total = tokens_y // 2 * lanes
     rows = inputs[...].reshape(wide, total)
     backs = cotangents[...].reshape(wide, total)
@@ -162,6 +166,21 @@
     return lax.ppermute(value, axis, [(0, 1), (1, 0)])
 
 
+def ring(block, axis):
+    size = lax.axis_size(axis)
+    up = [(i, (i + 1) % size) for i in range(size)]
+    down = [(j, i) for i, j in up]
+    found = [block] + [None] * (size - 1)
+    ahead = behind = block
+    for step in range(1, size // 2 + 1):
+        ahead = lax.ppermute(ahead, axis, up)
+        found[step] = ahead
+        if step < size - step:
+            behind = lax.ppermute(behind, axis, down)
+            found[size - step] = behind
+    return found
+
+
 def shards(tokens, grad_out, expert_ids, probs, w_gate, w_up, w_down):
     pairs_z, chips_x, pairs_y = lax.axis_size("zo"), lax.axis_size("x"), lax.axis_size("yo")
     chips_z, groups = pairs_z * PAIR, PAIR * PAIR
@@ -190,7 +209,8 @@
     quarter = lax.all_to_all(sent, ("zi",) + EP, split_axis=0, concat_axis=0, tiled=True)
     quarter, stacked = lax.optimization_barrier((quarter, stacked))
     weights = lax.all_gather(stacked, GROUP)
-    along_z = lax.all_gather(quarter, "zo").reshape(chips_z, pairs_y * PAIR, depth, LANES)
+    along_z = jnp.stack(ring(quarter, "zo"))
+    along_z = along_z.reshape(chips_z, pairs_y * PAIR, depth, LANES)
     blocks = []
     for steps in range(chips_x):
         along = [(i, (i + steps) % chips_x) for i in range(chips_x)]
@@ -200,12 +220,12 @@
     parts = pl.pallas_call(
         grads_kernel,
         out_shape=jax.ShapeDtypeStruct((groups, 3 * hidden, wide), BF16),
-        in_specs=[SMEM] * 3 + [VMEM] * (len(blocks) + 1),
+        in_specs=[SMEM] * 4 + [VMEM] * (len(blocks) + 1),
         out_specs=VMEM,
         scratch_shapes=[pltpu.VMEM((chips_z, chips_x * CORES, depth, pairs_y * LANES), BF16)] * 2,
         compiler_params=room(20),
         name="grads",
-    )(*(lax.axis_index(axis).reshape(1) for axis in ("core", "x", "yo")), *blocks, weights)
+    )(*(lax.axis_index(axis).reshape(1) for axis in ("core", "x", "yo", "zo")), *blocks, weights)
     met = lax.all_to_all(parts, GROUP, split_axis=0, concat_axis=0, tiled=True)
     grad_gate, grad_up, grad_down = pl.pallas_call(
         total_kernel,

time: 114 us -> 125 us (1.096)
  blocking collectives: 44 us -> 17.4 us
  starting transfers between devices: 39.2 us -> 64.3 us
  waiting for transfers between devices: 6.64 us -> 18.8 us
    all_gather x1 -> x0, blocking collectives: 26.6 us -> none  [shards(): lax.all_gather(quarter, 'zo').reshape(chips_z, pairs_y * PAIR, depth, LANES)]
    ppermute x0 -> x5, starting transfers between devices: none -> 25 us  [the longest x2 19.2 us: ring(): behind = lax.ppermute(behind, axis, down)]
    ppermute x0 -> x5, waiting for transfers between devices: none -> 12.2 us  [the longest x3 12.2 us: ring(): ahead = lax.ppermute(ahead, axis, up)]
  transfers between devices with their start and end apart: 9 -> 14, of which waited for: 2 -> 4; matrix products, arithmetic and copies ran while one was open for 0% -> 0% of each run, Pallas kernels for 2% -> 2%
where the time goes in v5:
time: 125 us; the launch traced here: 124 us
  starting transfers between devices  64.3 us (51%)
  waiting for transfers between devices  18.8 us (15%)
  blocking collectives  17.4 us (14%)
  between operations  14.3 us (11%)
  Pallas kernels  7.97 us (6%)
  local copies, waits for them, and re-layouts  1.35 us (1%)
    ppermute x4, starting transfers between devices, swap(): return lax.ppermute(value, axis, [(0, 1), (1, 0)])  20.3 us
    ppermute x2, starting transfers between devices, ring(): behind = lax.ppermute(behind, axis, down)  19.2 us
    all_to_all x1, blocking collectives, shards(): met = lax.all_to_all(parts, GROUP, split_axis=0, concat_axis=0, tiled=True)  17.4 us
    ppermute x3, waiting for transfers between devices, ring(): ahead = lax.ppermute(ahead, axis, up)  12.2 us
    all_to_all x1, starting transfers between devices, shards(): lax.all_to_all(sent, ('zi',) + EP, split_axis=0, concat_axis=0, tiled=True)  9.56 us
    ppermute x3, starting transfers between devices, shards(): block = lax.ppermute(along_z, 'x', along) if steps else along_z  9.42 us
    ppermute x3, starting transfers between devices, ring(): ahead = lax.ppermute(ahead, axis, up)  5.75 us
    all_to_all x1, waiting for transfers between devices, shards(): lax.all_to_all(sent, ('zi',) + EP, split_axis=0, concat_axis=0, tiled=True)  5.3 us
  transfers between devices with their start and end apart: 14, of which 4 were waited for; matrix products, arithmetic and copies ran while one was open for 0% of the time, Pallas kernels for 2%

profile of v5, /device:TPU:1, one launch (start us, length us, event | category | flops | bytes accessed | tf_op | source)
XLA Modules:
  0.0 124.1 jit_solution(17041539437015030916)
XLA Ops:
  7.2 1.5 %pack.1 = bf16[2,4,2,16,128]{4,3,2,1,0:T(8,128)(2,1)} custom-call(s32[1]{0:T(128)} %bitcast.4.zone, s32[1]{0:T(128)} %bitcast.5.yi, bf16[15,256]{1,0:T(8,128)(2,1)} %bitcast.49, bf16[15,256]{1,0:T(8,128)(2,1)} %bitcast.50, s32[4,256]{1,0:T(4,128)} %bitcast.51, f32[4,256]{1,0:T(4,128)} %bitcast.52), custom_call_target="tpu_custom_call" | custom-call | tf_op jit(solution)/shard_map/pack/pallas_call | solution.py:194
  8.6 9.6 %all-to-all-start = ((bf16[16,16,128]{2,1,0:T(8,128)(2,1)}), bf16[16,16,128]{2,1,0:T(8,128)(2,1)S(1)}, u32[]{:S(2)}, u32[]{:S(2)}) async-start(bf16[16,16,128]{2,1,0:T(8,128)(2,1)} %bitcast.45), calls=%async_computation | async-start | bytes 131072 | tf_op jit(solution)/shard_map/all_to_all | solution.py:209
  18.2 0.0 all-gather.3.cloned.1.call-start
  18.3 2.0 %widen_weights.1 = bf16[96,1536]{1,0:T(8,128)(2,1)} custom-call(bf16[30,1440]{1,0:T(8,128)(2,1)} %bitcast.46, bf16[30,1440]{1,0:T(8,128)(2,1)} %bitcast.47, bf16[30,1440]{1,0:T(8,128)(2,1)} %bitcast.48), custom_call_target="tpu_custom_call" | custom-call | tf_op jit(solution)/shard_map/widen_weights/pallas_call | solution.py:201
  20.3 5.3 %all-to-all-done = bf16[16,16,128]{2,1,0:T(8,128)(2,1)S(1)} async-done(((bf16[16,16,128]{2,1,0:T(8,128)(2,1)}), bf16[16,16,128]{2,1,0:T(8,128)(2,1)S(1)}, u32[]{:S(2)}, u32[]{:S(2)}) %all-to-all-start) | async-done | bytes 65568 | tf_op jit(solution)/shard_map/all_to_all | solution.py:209
  25.6 13.4 %collective-permute-start.3 = (bf16[16,16,128]{2,1,0:T(8,128)(2,1)S(1)}, bf16[16,16,128]{2,1,0:T(8,128)(2,1)S(1)}, u32[]{:S(2)}, u32[]{:S(2)}) collective-permute-start(bf16[16,16,128]{2,1,0:T(8,128)(2,1)S(1)} %all-to-all-done), channel_id=1, source_target_pairs={{128,0},{256,128},{384,256},{512,384},{640,512},{0,640},{129,1},{2... | collective-permute-start | bytes 196616 | tf_op jit(solution)/shard_map/ppermute | solution.py:179
  39.0 1.9 %collective-permute-start = (bf16[16,16,128]{2,1,0:T(8,128)(2,1)S(1)}, bf16[16,16,128]{2,1,0:T(8,128)(2,1)S(1)}, u32[]{:S(2)}, u32[]{:S(2)}) collective-permute-start(bf16[16,16,128]{2,1,0:T(8,128)(2,1)S(1)} %all-to-all-done), channel_id=1, source_target_pairs={{0,128},{128,256},{256,384},{384,512},{512,640},{640,0},{1,129},{1... | collective-permute-start | bytes 196616 | tf_op jit(solution)/shard_map/ppermute | solution.py:176
  40.9 0.0 all-gather.3.cloned.1.call-update
  40.9 0.0 collective-permute-done.3
  40.9 5.8 %collective-permute-start.4 = (bf16[16,16,128]{2,1,0:T(8,128)(2,1)S(1)}, bf16[16,16,128]{2,1,0:T(8,128)(2,1)S(1)}, u32[]{:S(2)}, u32[]{:S(2)}) collective-permute-start(bf16[16,16,128]{2,1,0:T(8,128)(2,1)S(1)} %collective-permute-done.3), channel_id=1, source_target_pairs={{128,0},{256,128},{384,256},{512,384},{640,512},{0,640},{129,1},{2... | collective-permute-start | bytes 196616 | tf_op jit(solution)/shard_map/ppermute | solution.py:179
  46.8 0.0 collective-permute-done
  46.8 1.9 %collective-permute-start.1 = (bf16[16,16,128]{2,1,0:T(8,128)(2,1)S(1)}, bf16[16,16,128]{2,1,0:T(8,128)(2,1)S(1)}, u32[]{:S(2)}, u32[]{:S(2)}) collective-permute-start(bf16[16,16,128]{2,1,0:T(8,128)(2,1)S(1)} %collective-permute-done), channel_id=1, source_target_pairs={{0,128},{128,256},{256,384},{384,512},{512,640},{640,0},{1,129},{1... | collective-permute-start | bytes 196616 | tf_op jit(solution)/shard_map/ppermute | solution.py:176
  48.7 5.2 %collective-permute-done.1 = bf16[16,16,128]{2,1,0:T(8,128)(2,1)S(1)} collective-permute-done((bf16[16,16,128]{2,1,0:T(8,128)(2,1)S(1)}, bf16[16,16,128]{2,1,0:T(8,128)(2,1)S(1)}, u32[]{:S(2)}, u32[]{:S(2)}) %collective-permute-start.1) | collective-permute-done | bytes 65568 | tf_op jit(solution)/shard_map/ppermute | solution.py:176
  53.9 1.9 %collective-permute-start.2 = (bf16[16,16,128]{2,1,0:T(8,128)(2,1)S(1)}, bf16[16,16,128]{2,1,0:T(8,128)(2,1)S(1)}, u32[]{:S(2)}, u32[]{:S(2)}) collective-permute-start(bf16[16,16,128]{2,1,0:T(8,128)(2,1)S(1)} %collective-permute-done.1), channel_id=1, source_target_pairs={{0,128},{128,256},{256,384},{384,512},{512,640},{640,0},{1,129},{1... | collective-permute-start | bytes 196616 | tf_op jit(solution)/shard_map/ppermute | solution.py:176
  55.8 7.0 %collective-permute-done.2 = bf16[16,16,128]{2,1,0:T(8,128)(2,1)S(1)} collective-permute-done((bf16[16,16,128]{2,1,0:T(8,128)(2,1)S(1)}, bf16[16,16,128]{2,1,0:T(8,128)(2,1)S(1)}, u32[]{:S(2)}, u32[]{:S(2)}) %collective-permute-start.2) | collective-permute-done | bytes 65568 | tf_op jit(solution)/shard_map/ppermute | solution.py:176
  62.9 0.0 collective-permute-done.4
  62.9 4.5 %collective-permute-start.10 = (bf16[12,8,16,128]{3,2,1,0:T(8,128)(2,1)S(1)}, bf16[12,8,16,128]{3,2,1,0:T(8,128)(2,1)S(1)}, u32[]{:S(2)}, u32[]{:S(2)}) collective-permute-start(bf16[12,8,16,128]{3,2,1,0:T(8,128)(2,1)S(1)} %bitcast.40), channel_id=1, source_target_pairs={{0,48},{16,0},{32,16},{48,32},{1,49},{17,1},{33,17},{49,33},{2,50}... | collective-permute-start | bytes 1179656 | tf_op jit(solution)/shard_map/ppermute | solution.py:217
  67.5 2.3 %collective-permute-start.8 = (bf16[12,8,16,128]{3,2,1,0:T(8,128)(2,1)S(1)}, bf16[12,8,16,128]{3,2,1,0:T(8,128)(2,1)S(1)}, u32[]{:S(2)}, u32[]{:S(2)}) collective-permute-start(bf16[12,8,16,128]{3,2,1,0:T(8,128)(2,1)S(1)} %bitcast.41), channel_id=1, source_target_pairs={{0,32},{16,48},{32,0},{48,16},{1,33},{17,49},{33,1},{49,17},{2,34}... | collective-permute-start | bytes 1179656 | tf_op jit(solution)/shard_map/ppermute | solution.py:217
  69.8 2.6 %collective-permute-start.6 = (bf16[12,8,16,128]{3,2,1,0:T(8,128)(2,1)S(1)}, bf16[12,8,16,128]{3,2,1,0:T(8,128)(2,1)S(1)}, u32[]{:S(2)}, u32[]{:S(2)}) collective-permute-start(bf16[12,8,16,128]{3,2,1,0:T(8,128)(2,1)S(1)} %bitcast.42), channel_id=1, source_target_pairs={{0,16},{16,32},{32,48},{48,0},{1,17},{17,33},{33,49},{49,1},{2,18}... | collective-permute-start | bytes 1179656 | tf_op jit(solution)/shard_map/ppermute | solution.py:217
  72.4 7.3 %collective-permute-start.5 = (bf16[12,8,16,128]{3,2,1,0:T(8,128)(2,1)S(1)}, bf16[12,8,16,128]{3,2,1,0:T(8,128)(2,1)S(1)}, u32[]{:S(2)}, u32[]{:S(2)}) collective-permute-start(bf16[12,8,16,128]{3,2,1,0:T(8,128)(2,1)S(1)} %bitcast.43), channel_id=1, source_target_pairs={{0,8},{8,0},{1,9},{9,1},{2,10},{10,2},{3,11},{11,3},{4,12},{12,4},... | collective-permute-start | bytes 1179656 | tf_op jit(solution)/shard_map/ppermute | solution.py:166
  79.7 0.0 collective-permute-done.10.refs_6_
  79.7 7.4 %collective-permute-start.11 = (bf16[12,8,16,128]{3,2,1,0:T(8,128)(2,1)S(1)}, bf16[12,8,16,128]{3,2,1,0:T(8,128)(2,1)S(1)}, u32[]{:S(2)}, u32[]{:S(2)}) collective-permute-start(bf16[12,8,16,128]{3,2,1,0:T(8,128)(2,1)S(1)} %collective-permute-done.10.refs_6_), channel_id=1, source_target_pairs={{0,8},{8,0},{1,9},{9,1},{2,10},{10,2},{3,11},{11,3},{4,12},{12,4},... | collective-permute-start | bytes 1179656 | tf_op jit(solution)/shard_map/ppermute | solution.py:166
  87.1 0.0 collective-permute-done.8.refs_4_
  87.1 1.9 %collective-permute-start.9 = (bf16[12,8,16,128]{3,2,1,0:T(8,128)(2,1)S(1)}, bf16[12,8,16,128]{3,2,1,0:T(8,128)(2,1)S(1)}, u32[]{:S(2)}, u32[]{:S(2)}) collective-permute-start(bf16[12,8,16,128]{3,2,1,0:T(8,128)(2,1)S(1)} %collective-permute-done.8.refs_4_), channel_id=1, source_target_pairs={{0,8},{8,0},{1,9},{9,1},{2,10},{10,2},{3,11},{11,3},{4,12},{12,4},... | collective-permute-start | bytes 1179656 | tf_op jit(solution)/shard_map/ppermute | solution.py:166
  89.0 0.0 collective-permute-done.6.refs_2_
  89.0 3.7 %collective-permute-start.7 = (bf16[12,8,16,128]{3,2,1,0:T(8,128)(2,1)S(1)}, bf16[12,8,16,128]{3,2,1,0:T(8,128)(2,1)S(1)}, u32[]{:S(2)}, u32[]{:S(2)}) collective-permute-start(bf16[12,8,16,128]{3,2,1,0:T(8,128)(2,1)S(1)} %collective-permute-done.6.refs_2_), channel_id=1, source_target_pairs={{0,8},{8,0},{1,9},{9,1},{2,10},{10,2},{3,11},{11,3},{4,12},{12,4},... | collective-permute-start | bytes 1179656 | tf_op jit(solution)/shard_map/ppermute | solution.py:166
  92.7 0.0 collective-permute-done.5.refs_1_
  92.7 0.0 collective-permute-done.11.refs_7_
  92.7 0.0 collective-permute-done.9.refs_5_
  92.8 1.3 %collective-permute-done.7.refs_3_ = bf16[12,8,16,128]{3,2,1,0:T(8,128)(2,1)S(1)} collective-permute-done((bf16[12,8,16,128]{3,2,1,0:T(8,128)(2,1)S(1)}, bf16[12,8,16,128]{3,2,1,0:T(8,128)(2,1)S(1)}, u32[]{:S(2)}, u32[]{:S(2)}) %collective-permute-start.7) | collective-permute-done | bytes 393248 | tf_op jit(solution)/shard_map/ppermute | solution.py:166
  94.0 0.0 all-gather.3.cloned.1.call-done
  94.1 0.0 copy-start
  94.1 1.3 %copy-done = bf16[384,1536]{1,0:T(8,128)(2,1)S(1)} copy-done((bf16[384,1536]{1,0:T(8,128)(2,1)S(1)}, bf16[384,1536]{1,0:T(8,128)(2,1)}, u32[]{:S(2)}) %copy-start) | copy-done | bytes 1179672
  95.3 3.2 %grads.1 = bf16[4,96,1536]{2,1,0:T(8,128)(2,1)S(1)} custom-call(s32[1]{0:T(128)} %bitcast.core_at, s32[1]{0:T(128)} %bitcast.1.x_at, s32[1]{0:T(128)} %bitcast.2.yo_at, s32[1]{0:T(128)} %bitcast.3.zo_at, bf16[12,8,16,128]{3,2,1,0:T(8,128)(2,1)S(1)} %bitcast.44, bf16[12,8,16,128]{3,2,1,0:T(8,128)(2,1)S(1)} %collective-permute-done.5.refs_1_, ...), custom_call_target="tpu_custom_call" | custom-call | tf_op jit(solution)/shard_map/grads/pallas_call | solution.py:220
  98.5 17.4 %all_to_all.10.parts = bf16[4,96,1536]{2,1,0:T(8,128)(2,1)S(1)} all-to-all(bf16[4,96,1536]{2,1,0:T(8,128)(2,1)S(1)} %grads.1), channel_id=1, replica_groups=mesh['zo'=6,'zi'=2,'x'=4,'core'=2,'yo'=4,'yi'=2] {'zi','yi'}, dimensions={0} | all-to-all | bytes 2359296 | tf_op jit(solution)/shard_map/all_to_all | solution.py:229
  115.9 1.3 %total.1 = (bf16[30,1440]{1,0:T(8,128)(2,1)}, bf16[30,1440]{1,0:T(8,128)(2,1)}, bf16[30,1440]{1,0:T(8,128)(2,1)}) custom-call(bf16[4,96,1536]{2,1,0:T(8,128)(2,1)S(1)} %all_to_all.10.parts), custom_call_target="tpu_custom_call" | custom-call | tf_op jit(solution)/shard_map/total/pallas_call | solution.py:230
  (6 shorter events, 0.1 us)
Async XLA Ops:
  8.6 16.9 %all-to-all-start = ((bf16[16,16,128]{2,1,0:T(8,128)(2,1)}), bf16[16,16,128]{2,1,0:T(8,128)(2,1)S(1)}, u32[]{:S(2)}, u32[]{:S(2)}) async-start(bf16[16,16,128]{2,1,0:T(8,128)(2,1)} %bitcast.45), calls=%async_computation | async-start | bytes 131072 | tf_op jit(solution)/shard_map/all_to_all | solution.py:209
  18.2 75.8 %all-gather.3.cloned.1.call-start = ((), (), s32[]{:S(2)}) async-start(), calls=%async_computation.2 | async-start | bytes 1474560 | tf_op jit(solution)/shard_map/all_gather | solution.py:211
  25.6 15.4 %collective-permute-start.3 = (bf16[16,16,128]{2,1,0:T(8,128)(2,1)S(1)}, bf16[16,16,128]{2,1,0:T(8,128)(2,1)S(1)}, u32[]{:S(2)}, u32[]{:S(2)}) collective-permute-start(bf16[16,16,128]{2,1,0:T(8,128)(2,1)S(1)} %all-to-all-done), channel_id=1, source_target_pairs={{128,0},{256,128},{384,256},{512,384},{640,512},{0,640},{129,1},{2... | collective-permute-start | bytes 196616 | tf_op jit(solution)/shard_map/ppermute | solution.py:179
  39.0 7.8 %collective-permute-start = (bf16[16,16,128]{2,1,0:T(8,128)(2,1)S(1)}, bf16[16,16,128]{2,1,0:T(8,128)(2,1)S(1)}, u32[]{:S(2)}, u32[]{:S(2)}) collective-permute-start(bf16[16,16,128]{2,1,0:T(8,128)(2,1)S(1)} %all-to-all-done), channel_id=1, source_target_pairs={{0,128},{128,256},{256,384},{384,512},{512,640},{640,0},{1,129},{1... | collective-permute-start | bytes 196616 | tf_op jit(solution)/shard_map/ppermute | solution.py:176
  40.9 21.9 %collective-permute-start.4 = (bf16[16,16,128]{2,1,0:T(8,128)(2,1)S(1)}, bf16[16,16,128]{2,1,0:T(8,128)(2,1)S(1)}, u32[]{:S(2)}, u32[]{:S(2)}) collective-permute-start(bf16[16,16,128]{2,1,0:T(8,128)(2,1)S(1)} %collective-permute-done.3), channel_id=1, source_target_pairs={{128,0},{256,128},{384,256},{512,384},{640,512},{0,640},{129,1},{2... | collective-permute-start | bytes 196616 | tf_op jit(solution)/shard_map/ppermute | solution.py:179
  46.8 7.1 %collective-permute-start.1 = (bf16[16,16,128]{2,1,0:T(8,128)(2,1)S(1)}, bf16[16,16,128]{2,1,0:T(8,128)(2,1)S(1)}, u32[]{:S(2)}, u32[]{:S(2)}) collective-permute-start(bf16[16,16,128]{2,1,0:T(8,128)(2,1)S(1)} %collective-permute-done), channel_id=1, source_target_pairs={{0,128},{128,256},{256,384},{384,512},{512,640},{640,0},{1,129},{1... | collective-permute-start | bytes 196616 | tf_op jit(solution)/shard_map/ppermute | solution.py:176
  53.9 9.0 %collective-permute-start.2 = (bf16[16,16,128]{2,1,0:T(8,128)(2,1)S(1)}, bf16[16,16,128]{2,1,0:T(8,128)(2,1)S(1)}, u32[]{:S(2)}, u32[]{:S(2)}) collective-permute-start(bf16[16,16,128]{2,1,0:T(8,128)(2,1)S(1)} %collective-permute-done.1), channel_id=1, source_target_pairs={{0,128},{128,256},{256,384},{384,512},{512,640},{640,0},{1,129},{1... | collective-permute-start | bytes 196616 | tf_op jit(solution)/shard_map/ppermute | solution.py:176
  62.9 16.8 %collective-permute-start.10 = (bf16[12,8,16,128]{3,2,1,0:T(8,128)(2,1)S(1)}, bf16[12,8,16,128]{3,2,1,0:T(8,128)(2,1)S(1)}, u32[]{:S(2)}, u32[]{:S(2)}) collective-permute-start(bf16[12,8,16,128]{3,2,1,0:T(8,128)(2,1)S(1)} %bitcast.40), channel_id=1, source_target_pairs={{0,48},{16,0},{32,16},{48,32},{1,49},{17,1},{33,17},{49,33},{2,50}... | collective-permute-start | bytes 1179656 | tf_op jit(solution)/shard_map/ppermute | solution.py:217
  67.5 19.6 %collective-permute-start.8 = (bf16[12,8,16,128]{3,2,1,0:T(8,128)(2,1)S(1)}, bf16[12,8,16,128]{3,2,1,0:T(8,128)(2,1)S(1)}, u32[]{:S(2)}, u32[]{:S(2)}) collective-permute-start(bf16[12,8,16,128]{3,2,1,0:T(8,128)(2,1)S(1)} %bitcast.41), channel_id=1, source_target_pairs={{0,32},{16,48},{32,0},{48,16},{1,33},{17,49},{33,1},{49,17},{2,34}... | collective-permute-start | bytes 1179656 | tf_op jit(solution)/shard_map/ppermute | solution.py:217
  69.8 19.2 %collective-permute-start.6 = (bf16[12,8,16,128]{3,2,1,0:T(8,128)(2,1)S(1)}, bf16[12,8,16,128]{3,2,1,0:T(8,128)(2,1)S(1)}, u32[]{:S(2)}, u32[]{:S(2)}) collective-permute-start(bf16[12,8,16,128]{3,2,1,0:T(8,128)(2,1)S(1)} %bitcast.42), channel_id=1, source_target_pairs={{0,16},{16,32},{32,48},{48,0},{1,17},{17,33},{33,49},{49,1},{2,18}... | collective-permute-start | bytes 1179656 | tf_op jit(solution)/shard_map/ppermute | solution.py:217
  72.4 20.4 %collective-permute-start.5 = (bf16[12,8,16,128]{3,2,1,0:T(8,128)(2,1)S(1)}, bf16[12,8,16,128]{3,2,1,0:T(8,128)(2,1)S(1)}, u32[]{:S(2)}, u32[]{:S(2)}) collective-permute-start(bf16[12,8,16,128]{3,2,1,0:T(8,128)(2,1)S(1)} %bitcast.43), channel_id=1, source_target_pairs={{0,8},{8,0},{1,9},{9,1},{2,10},{10,2},{3,11},{11,3},{4,12},{12,4},... | collective-permute-start | bytes 1179656 | tf_op jit(solution)/shard_map/ppermute | solution.py:166
  79.7 13.0 %collective-permute-start.11 = (bf16[12,8,16,128]{3,2,1,0:T(8,128)(2,1)S(1)}, bf16[12,8,16,128]{3,2,1,0:T(8,128)(2,1)S(1)}, u32[]{:S(2)}, u32[]{:S(2)}) collective-permute-start(bf16[12,8,16,128]{3,2,1,0:T(8,128)(2,1)S(1)} %collective-permute-done.10.refs_6_), channel_id=1, source_target_pairs={{0,8},{8,0},{1,9},{9,1},{2,10},{10,2},{3,11},{11,3},{4,12},{12,4},... | collective-permute-start | bytes 1179656 | tf_op jit(solution)/shard_map/ppermute | solution.py:166
  87.1 5.6 %collective-permute-start.9 = (bf16[12,8,16,128]{3,2,1,0:T(8,128)(2,1)S(1)}, bf16[12,8,16,128]{3,2,1,0:T(8,128)(2,1)S(1)}, u32[]{:S(2)}, u32[]{:S(2)}) collective-permute-start(bf16[12,8,16,128]{3,2,1,0:T(8,128)(2,1)S(1)} %collective-permute-done.8.refs_4_), channel_id=1, source_target_pairs={{0,8},{8,0},{1,9},{9,1},{2,10},{10,2},{3,11},{11,3},{4,12},{12,4},... | collective-permute-start | bytes 1179656 | tf_op jit(solution)/shard_map/ppermute | solution.py:166
  89.0 5.0 %collective-permute-start.7 = (bf16[12,8,16,128]{3,2,1,0:T(8,128)(2,1)S(1)}, bf16[12,8,16,128]{3,2,1,0:T(8,128)(2,1)S(1)}, u32[]{:S(2)}, u32[]{:S(2)}) collective-permute-start(bf16[12,8,16,128]{3,2,1,0:T(8,128)(2,1)S(1)} %collective-permute-done.6.refs_2_), channel_id=1, source_target_pairs={{0,8},{8,0},{1,9},{9,1},{2,10},{10,2},{3,11},{11,3},{4,12},{12,4},... | collective-permute-start | bytes 1179656 | tf_op jit(solution)/shard_map/ppermute | solution.py:166
  94.1 1.3 %copy-start = (bf16[384,1536]{1,0:T(8,128)(2,1)S(1)}, bf16[384,1536]{1,0:T(8,128)(2,1)}, u32[]{:S(2)}) copy-start(bf16[384,1536]{1,0:T(8,128)(2,1)} %all-gather.3.cloned.1.call-done) | copy-start | bytes 3538948
Sparse Core Ops, SparseCore 0:
  41.1 34.4 all-gather.2

commit v6 on v4

--- a/solution.py
+++ b/solution.py
@@ -96,12 +96,19 @@
     out[...] = widen(jnp.concatenate(rows, axis=0).astype(BF16), wide)
 
 
+def regroup_kernel(gathered, out):
+    groups, stacked, wide = gathered.shape
+    hidden = stacked // 3
+    for k in range(3):
+        out[k] = gathered[:, k * hidden : (k + 1) * hidden].reshape(groups * hidden, wide)
+
+
 def grads_kernel(core_at, x_at, yo_at, *refs):
     blocks, (weights, out, inputs, cotangents) = refs[:-4], refs[-4:]
     chips_x = len(blocks) // CORES
     chips_z, tokens_y, depth, lanes = blocks[0].shape
-    groups, stacked, wide = weights.shape
-    hidden = stacked // 3
+    wide = weights.shape[2]
+    groups, hidden = out.shape[0], out.shape[1] // 3
     core, x, yo = core_at[0], x_at[0], yo_at[0]
     lower = lax.broadcasted_iota(jnp.int32, (chips_z, depth, lanes), 2) < lanes // 2
     for k, ref in enumerate(blocks):
@@ -116,12 +123,10 @@
     rows = inputs[...].reshape(wide, total)
     backs = cotangents[...].reshape(wide, total)
 
-    def part(k):
-        return weights[:, k * hidden : (k + 1) * hidden, :].reshape(groups * hidden, wide)
-
-    gate = dot(part(0), rows)
-    linear = dot(part(1), rows)
-    back = turned(dot(part(2), backs))
+    units = groups * hidden
+    both = dot(weights[:2].reshape(2 * units, wide), rows)
+    gate, linear = both[:units], both[units:]
+    back = turned(dot(weights[2], backs))
     shares = []
     for j in range(groups):
         expert = yo * PAIR + j % PAIR
@@ -134,8 +139,9 @@
     lifted = turned(gate * sigma * linear * share).astype(BF16)
     gate_term = (back * linear * sigma * (1.0 + gate * (1.0 - sigma))).astype(BF16)
     linear_term = (back * gate * sigma).astype(BF16)
-    for k, (left, right) in enumerate(((gate_term, rows), (linear_term, rows), (lifted, backs))):
-        grad = dot_t(left, right).astype(BF16)
+    upward = dot_t(jnp.concatenate([gate_term, linear_term], axis=0), rows).astype(BF16)
+    grads = (upward[:units], upward[units:], dot_t(lifted, backs).astype(BF16))
+    for k, grad in enumerate(grads):
         out[:, k * hidden : (k + 1) * hidden, :] = grad.reshape(groups, hidden, wide)
 
 
@@ -197,6 +203,15 @@
         block = lax.ppermute(along_z, "x", along) if steps else along_z
         blocks += [block, swap(block, "core")]
 
+    regrouped = pl.pallas_call(
+        regroup_kernel,
+        out_shape=jax.ShapeDtypeStruct((3, groups * hidden, wide), BF16),
+        in_specs=[VMEM],
+        out_specs=VMEM,
+        compiler_params=room(4),
+        cost_estimate=pl.CostEstimate(flops=0, bytes_accessed=2 * 3 * groups * hidden * wide * 2, transcendentals=0),
+        name="regroup",
+    )(weights)
     parts = pl.pallas_call(
         grads_kernel,
         out_shape=jax.ShapeDtypeStruct((groups, 3 * hidden, wide), BF16),
@@ -205,7 +220,7 @@
         scratch_shapes=[pltpu.VMEM((chips_z, chips_x * CORES, depth, pairs_y * LANES), BF16)] * 2,
         compiler_params=room(20),
         name="grads",
-    )(*(lax.axis_index(axis).reshape(1) for axis in ("core", "x", "yo")), *blocks, weights)
+    )(*(lax.axis_index(axis).reshape(1) for axis in ("core", "x", "yo")), *blocks, regrouped)
     met = lax.all_to_all(parts, GROUP, split_axis=0, concat_axis=0, tiled=True)
     grad_gate, grad_up, grad_down = pl.pallas_call(
         total_kernel,

time: 114 us -> 112 us (0.982)
  waiting for transfers between devices: 6.64 us -> 5.37 us
    ppermute x4, waiting for transfers between devices: 1.3 us -> 0.01 us  [swap(): return lax.ppermute(value, axis, [(0, 1), (1, 0)])]
  transfers between devices with their start and end apart: 9 -> 9, of which waited for: 2 -> 1; matrix products, arithmetic and copies ran while one was open for 0% -> 0% of each run, Pallas kernels for 2% -> 2%
where the time goes in v6:
time: 112 us; the launch traced here: 111 us
  blocking collectives  44 us (39%)
  starting transfers between devices  39.2 us (35%)
  between operations  14.2 us (13%)
  Pallas kernels  7.42 us (7%)
  waiting for transfers between devices  5.37 us (5%)
  local copies, waits for them, and re-layouts  1.26 us (1%)
    all_gather x1, blocking collectives, shards(): lax.all_gather(quarter, 'zo').reshape(chips_z, pairs_y * PAIR, depth, LANES)  26.6 us
    ppermute x4, starting transfers between devices, swap(): return lax.ppermute(value, axis, [(0, 1), (1, 0)])  20.2 us
    all_to_all x1, blocking collectives, shards(): met = lax.all_to_all(parts, GROUP, split_axis=0, concat_axis=0, tiled=True)  17.5 us
    all_to_all x1, starting transfers between devices, shards(): lax.all_to_all(sent, ('zi',) + EP, split_axis=0, concat_axis=0, tiled=True)  9.56 us
    ppermute x3, starting transfers between devices, shards(): block = lax.ppermute(along_z, 'x', along) if steps else along_z  9.32 us
    all_to_all x1, waiting for transfers between devices, shards(): lax.all_to_all(sent, ('zi',) + EP, split_axis=0, concat_axis=0, tiled=True)  5.32 us
    pallas_call x1, Pallas kernels, shards(): pl.pallas_call(grads_kernel, out_shape=jax.ShapeDtypeStruct((groups, 3 *...  2.59 us
  transfers between devices with their start and end apart: 9, of which 1 were waited for; matrix products, arithmetic and copies ran while one was open for 0% of the time, Pallas kernels for 2%

profile of v6, /device:TPU:1, one launch (start us, length us, event | category | flops | bytes accessed | tf_op | source)
XLA Modules:
  0.0 111.5 jit_solution(15695976669480034915)
XLA Ops:
  7.2 1.5 %pack.1 = bf16[2,4,2,16,128]{4,3,2,1,0:T(8,128)(2,1)} custom-call(s32[1]{0:T(128)} %bitcast.3.zone, s32[1]{0:T(128)} %bitcast.4.yi, bf16[15,256]{1,0:T(8,128)(2,1)} %bitcast.36, bf16[15,256]{1,0:T(8,128)(2,1)} %bitcast.37, s32[4,256]{1,0:T(4,128)} %bitcast.38, f32[4,256]{1,0:T(4,128)} %bitcast.39), custom_call_target="tpu_custom_call" | custom-call | tf_op jit(solution)/shard_map/pack/pallas_call | solution.py:181
  8.6 9.6 %all-to-all-start = ((bf16[16,16,128]{2,1,0:T(8,128)(2,1)}), bf16[16,16,128]{2,1,0:T(8,128)(2,1)S(1)}, u32[]{:S(2)}, u32[]{:S(2)}) async-start(bf16[16,16,128]{2,1,0:T(8,128)(2,1)} %bitcast.32), calls=%async_computation | async-start | bytes 131072 | tf_op jit(solution)/shard_map/all_to_all | solution.py:196
  18.2 0.0 all-gather.4.cloned.1.call-start
  18.3 2.0 %widen_weights.1 = bf16[96,1536]{1,0:T(8,128)(2,1)} custom-call(bf16[30,1440]{1,0:T(8,128)(2,1)} %bitcast.33, bf16[30,1440]{1,0:T(8,128)(2,1)} %bitcast.34, bf16[30,1440]{1,0:T(8,128)(2,1)} %bitcast.35), custom_call_target="tpu_custom_call" | custom-call | tf_op jit(solution)/shard_map/widen_weights/pallas_call | solution.py:188
  20.3 5.3 %all-to-all-done = bf16[16,16,128]{2,1,0:T(8,128)(2,1)S(1)} async-done(((bf16[16,16,128]{2,1,0:T(8,128)(2,1)}), bf16[16,16,128]{2,1,0:T(8,128)(2,1)S(1)}, u32[]{:S(2)}, u32[]{:S(2)}) %all-to-all-start) | async-done | bytes 65568 | tf_op jit(solution)/shard_map/all_to_all | solution.py:196
  25.6 0.0 all-gather.4.cloned.1.call-update
  25.6 26.6 %all-gather = bf16[96,16,128]{2,1,0:T(8,128)(2,1)S(1)} all-gather(bf16[16,16,128]{2,1,0:T(8,128)(2,1)S(1)} %all-to-all-done), channel_id=2, replica_groups=mesh['zo'=6,'zi'=2,'x'=4,'core'=2,'yo'=4,'yi'=2] {'zo'}, dimensions={0}, use_global_device_ids=true | all-gather | bytes 458752 | tf_op jit(solution)/shard_map/all_gather | solution.py:199
  52.2 4.4 %collective-permute-start.5 = (bf16[12,8,16,128]{3,2,1,0:T(8,128)(2,1)S(1)}, bf16[12,8,16,128]{3,2,1,0:T(8,128)(2,1)S(1)}, u32[]{:S(2)}, u32[]{:S(2)}) collective-permute-start(bf16[12,8,16,128]{3,2,1,0:T(8,128)(2,1)S(1)} %bitcast.26), channel_id=1, source_target_pairs={{0,48},{16,0},{32,16},{48,32},{1,49},{17,1},{33,17},{49,33},{2,50}... | collective-permute-start | bytes 1179656 | tf_op jit(solution)/shard_map/ppermute | solution.py:203
  56.6 2.4 %collective-permute-start.3 = (bf16[12,8,16,128]{3,2,1,0:T(8,128)(2,1)S(1)}, bf16[12,8,16,128]{3,2,1,0:T(8,128)(2,1)S(1)}, u32[]{:S(2)}, u32[]{:S(2)}) collective-permute-start(bf16[12,8,16,128]{3,2,1,0:T(8,128)(2,1)S(1)} %bitcast.27), channel_id=1, source_target_pairs={{0,32},{16,48},{32,0},{48,16},{1,33},{17,49},{33,1},{49,17},{2,34}... | collective-permute-start | bytes 1179656 | tf_op jit(solution)/shard_map/ppermute | solution.py:203
  59.0 2.5 %collective-permute-start.1 = (bf16[12,8,16,128]{3,2,1,0:T(8,128)(2,1)S(1)}, bf16[12,8,16,128]{3,2,1,0:T(8,128)(2,1)S(1)}, u32[]{:S(2)}, u32[]{:S(2)}) collective-permute-start(bf16[12,8,16,128]{3,2,1,0:T(8,128)(2,1)S(1)} %bitcast.28), channel_id=1, source_target_pairs={{0,16},{16,32},{32,48},{48,0},{1,17},{17,33},{33,49},{49,1},{2,18}... | collective-permute-start | bytes 1179656 | tf_op jit(solution)/shard_map/ppermute | solution.py:203
  61.5 8.8 %collective-permute-start = (bf16[12,8,16,128]{3,2,1,0:T(8,128)(2,1)S(1)}, bf16[12,8,16,128]{3,2,1,0:T(8,128)(2,1)S(1)}, u32[]{:S(2)}, u32[]{:S(2)}) collective-permute-start(bf16[12,8,16,128]{3,2,1,0:T(8,128)(2,1)S(1)} %bitcast.29), channel_id=1, source_target_pairs={{0,8},{8,0},{1,9},{9,1},{2,10},{10,2},{3,11},{11,3},{4,12},{12,4},... | collective-permute-start | bytes 1179656 | tf_op jit(solution)/shard_map/ppermute | solution.py:168
  70.4 0.0 collective-permute-done.5.refs_6_
  70.4 5.9 %collective-permute-start.6 = (bf16[12,8,16,128]{3,2,1,0:T(8,128)(2,1)S(1)}, bf16[12,8,16,128]{3,2,1,0:T(8,128)(2,1)S(1)}, u32[]{:S(2)}, u32[]{:S(2)}) collective-permute-start(bf16[12,8,16,128]{3,2,1,0:T(8,128)(2,1)S(1)} %collective-permute-done.5.refs_6_), channel_id=1, source_target_pairs={{0,8},{8,0},{1,9},{9,1},{2,10},{10,2},{3,11},{11,3},{4,12},{12,4},... | collective-permute-start | bytes 1179656 | tf_op jit(solution)/shard_map/ppermute | solution.py:168
  76.3 0.0 collective-permute-done.3.refs_4_
  76.3 1.9 %collective-permute-start.4 = (bf16[12,8,16,128]{3,2,1,0:T(8,128)(2,1)S(1)}, bf16[12,8,16,128]{3,2,1,0:T(8,128)(2,1)S(1)}, u32[]{:S(2)}, u32[]{:S(2)}) collective-permute-start(bf16[12,8,16,128]{3,2,1,0:T(8,128)(2,1)S(1)} %collective-permute-done.3.refs_4_), channel_id=1, source_target_pairs={{0,8},{8,0},{1,9},{9,1},{2,10},{10,2},{3,11},{11,3},{4,12},{12,4},... | collective-permute-start | bytes 1179656 | tf_op jit(solution)/shard_map/ppermute | solution.py:168
  78.2 0.0 collective-permute-done.1.refs_2_
  78.2 3.6 %collective-permute-start.2 = (bf16[12,8,16,128]{3,2,1,0:T(8,128)(2,1)S(1)}, bf16[12,8,16,128]{3,2,1,0:T(8,128)(2,1)S(1)}, u32[]{:S(2)}, u32[]{:S(2)}) collective-permute-start(bf16[12,8,16,128]{3,2,1,0:T(8,128)(2,1)S(1)} %collective-permute-done.1.refs_2_), channel_id=1, source_target_pairs={{0,8},{8,0},{1,9},{9,1},{2,10},{10,2},{3,11},{11,3},{4,12},{12,4},... | collective-permute-start | bytes 1179656 | tf_op jit(solution)/shard_map/ppermute | solution.py:168
  81.8 0.0 all-gather.4.cloned.1.call-done
  81.9 0.0 copy-start
  81.9 1.3 %copy-done = bf16[384,1536]{1,0:T(8,128)(2,1)S(1)} copy-done((bf16[384,1536]{1,0:T(8,128)(2,1)S(1)}, bf16[384,1536]{1,0:T(8,128)(2,1)}, u32[]{:S(2)}) %copy-start) | copy-done | bytes 1179672
  83.1 0.1 regroup.1.refs_8_
  83.2 0.0 collective-permute-done.refs_1_
  83.2 0.0 collective-permute-done.6.refs_7_
  83.3 0.0 collective-permute-done.4.refs_5_
  83.3 0.0 collective-permute-done.2.refs_3_
  83.3 2.6 %grads.1 = bf16[4,96,1536]{2,1,0:T(8,128)(2,1)S(1)} custom-call(s32[1]{0:T(128)} %bitcast.core_at, s32[1]{0:T(128)} %bitcast.1.x_at, s32[1]{0:T(128)} %bitcast.2.yo_at, bf16[12,8,16,128]{3,2,1,0:T(8,128)(2,1)S(1)} %bitcast.30, bf16[12,8,16,128]{3,2,1,0:T(8,128)(2,1)S(1)} %collective-permute-done.refs_1_, ...), custom_call_target="tpu_custom_call" | custom-call | tf_op jit(solution)/shard_map/grads/pallas_call | solution.py:215
  85.9 17.5 %all_to_all.10.parts = bf16[4,96,1536]{2,1,0:T(8,128)(2,1)S(1)} all-to-all(bf16[4,96,1536]{2,1,0:T(8,128)(2,1)S(1)} %grads.1), channel_id=1, replica_groups=mesh['zo'=6,'zi'=2,'x'=4,'core'=2,'yo'=4,'yi'=2] {'zi','yi'}, dimensions={0} | all-to-all | bytes 2359296 | tf_op jit(solution)/shard_map/all_to_all | solution.py:224
  103.3 1.3 %total.1 = (bf16[30,1440]{1,0:T(8,128)(2,1)}, bf16[30,1440]{1,0:T(8,128)(2,1)}, bf16[30,1440]{1,0:T(8,128)(2,1)}) custom-call(bf16[4,96,1536]{2,1,0:T(8,128)(2,1)S(1)} %all_to_all.10.parts), custom_call_target="tpu_custom_call" | custom-call | tf_op jit(solution)/shard_map/total/pallas_call | solution.py:225
Async XLA Ops:
  8.6 16.9 %all-to-all-start = ((bf16[16,16,128]{2,1,0:T(8,128)(2,1)}), bf16[16,16,128]{2,1,0:T(8,128)(2,1)S(1)}, u32[]{:S(2)}, u32[]{:S(2)}) async-start(bf16[16,16,128]{2,1,0:T(8,128)(2,1)} %bitcast.32), calls=%async_computation | async-start | bytes 131072 | tf_op jit(solution)/shard_map/all_to_all | solution.py:196
  18.2 63.7 %all-gather.4.cloned.1.call-start = ((), (), s32[]{:S(2)}) async-start(), calls=%async_computation.2 | async-start | bytes 1474560 | tf_op jit(solution)/shard_map/all_gather | solution.py:198
  52.2 18.2 %collective-permute-start.5 = (bf16[12,8,16,128]{3,2,1,0:T(8,128)(2,1)S(1)}, bf16[12,8,16,128]{3,2,1,0:T(8,128)(2,1)S(1)}, u32[]{:S(2)}, u32[]{:S(2)}) collective-permute-start(bf16[12,8,16,128]{3,2,1,0:T(8,128)(2,1)S(1)} %bitcast.26), channel_id=1, source_target_pairs={{0,48},{16,0},{32,16},{48,32},{1,49},{17,1},{33,17},{49,33},{2,50}... | collective-permute-start | bytes 1179656 | tf_op jit(solution)/shard_map/ppermute | solution.py:203
  56.6 19.7 %collective-permute-start.3 = (bf16[12,8,16,128]{3,2,1,0:T(8,128)(2,1)S(1)}, bf16[12,8,16,128]{3,2,1,0:T(8,128)(2,1)S(1)}, u32[]{:S(2)}, u32[]{:S(2)}) collective-permute-start(bf16[12,8,16,128]{3,2,1,0:T(8,128)(2,1)S(1)} %bitcast.27), channel_id=1, source_target_pairs={{0,32},{16,48},{32,0},{48,16},{1,33},{17,49},{33,1},{49,17},{2,34}... | collective-permute-start | bytes 1179656 | tf_op jit(solution)/shard_map/ppermute | solution.py:203
  59.0 19.2 %collective-permute-start.1 = (bf16[12,8,16,128]{3,2,1,0:T(8,128)(2,1)S(1)}, bf16[12,8,16,128]{3,2,1,0:T(8,128)(2,1)S(1)}, u32[]{:S(2)}, u32[]{:S(2)}) collective-permute-start(bf16[12,8,16,128]{3,2,1,0:T(8,128)(2,1)S(1)} %bitcast.28), channel_id=1, source_target_pairs={{0,16},{16,32},{32,48},{48,0},{1,17},{17,33},{33,49},{49,1},{2,18}... | collective-permute-start | bytes 1179656 | tf_op jit(solution)/shard_map/ppermute | solution.py:203
  61.5 21.7 %collective-permute-start = (bf16[12,8,16,128]{3,2,1,0:T(8,128)(2,1)S(1)}, bf16[12,8,16,128]{3,2,1,0:T(8,128)(2,1)S(1)}, u32[]{:S(2)}, u32[]{:S(2)}) collective-permute-start(bf16[12,8,16,128]{3,2,1,0:T(8,128)(2,1)S(1)} %bitcast.29), channel_id=1, source_target_pairs={{0,8},{8,0},{1,9},{9,1},{2,10},{10,2},{3,11},{11,3},{4,12},{12,4},... | collective-permute-start | bytes 1179656 | tf_op jit(solution)/shard_map/ppermute | solution.py:168
  70.4 12.9 %collective-permute-start.6 = (bf16[12,8,16,128]{3,2,1,0:T(8,128)(2,1)S(1)}, bf16[12,8,16,128]{3,2,1,0:T(8,128)(2,1)S(1)}, u32[]{:S(2)}, u32[]{:S(2)}) collective-permute-start(bf16[12,8,16,128]{3,2,1,0:T(8,128)(2,1)S(1)} %collective-permute-done.5.refs_6_), channel_id=1, source_target_pairs={{0,8},{8,0},{1,9},{9,1},{2,10},{10,2},{3,11},{11,3},{4,12},{12,4},... | collective-permute-start | bytes 1179656 | tf_op jit(solution)/shard_map/ppermute | solution.py:168
  76.3 7.0 %collective-permute-start.4 = (bf16[12,8,16,128]{3,2,1,0:T(8,128)(2,1)S(1)}, bf16[12,8,16,128]{3,2,1,0:T(8,128)(2,1)S(1)}, u32[]{:S(2)}, u32[]{:S(2)}) collective-permute-start(bf16[12,8,16,128]{3,2,1,0:T(8,128)(2,1)S(1)} %collective-permute-done.3.refs_4_), channel_id=1, source_target_pairs={{0,8},{8,0},{1,9},{9,1},{2,10},{10,2},{3,11},{11,3},{4,12},{12,4},... | collective-permute-start | bytes 1179656 | tf_op jit(solution)/shard_map/ppermute | solution.py:168
  78.2 5.1 %collective-permute-start.2 = (bf16[12,8,16,128]{3,2,1,0:T(8,128)(2,1)S(1)}, bf16[12,8,16,128]{3,2,1,0:T(8,128)(2,1)S(1)}, u32[]{:S(2)}, u32[]{:S(2)}) collective-permute-start(bf16[12,8,16,128]{3,2,1,0:T(8,128)(2,1)S(1)} %collective-permute-done.1.refs_2_), channel_id=1, source_target_pairs={{0,8},{8,0},{1,9},{9,1},{2,10},{10,2},{3,11},{11,3},{4,12},{12,4},... | collective-permute-start | bytes 1179656 | tf_op jit(solution)/shard_map/ppermute | solution.py:168
  81.9 1.3 %copy-start = (bf16[384,1536]{1,0:T(8,128)(2,1)S(1)}, bf16[384,1536]{1,0:T(8,128)(2,1)}, u32[]{:S(2)}) copy-start(bf16[384,1536]{1,0:T(8,128)(2,1)} %all-gather.4.cloned.1.call-done) | copy-start | bytes 3538948
Sparse Core Ops, SparseCore 0:
  25.7 42.1 all-gather.3

commit v7 on v6

--- a/solution.py
+++ b/solution.py
@@ -65,6 +65,22 @@
 def turned(rows):
     tiles = [half_turn(rows[:, k : k + LANES]) for k in range(0, rows.shape[1], LANES)]
     return jnp.concatenate(tiles, axis=1)
+
+
+def dense(grads, narrow, tall):
+    wide, whole = grads[0].shape[1], narrow // LANES * LANES
+    rest = narrow - whole
+    columns = [[] for _ in grads]
+    shared = 0.0
+    for k, grad in enumerate(grads):
+        main = narrowed(grad, whole)
+        columns[k] = [main[:, at : at + LANES] for at in range(0, whole, LANES)]
+        low = (whole // 15 * 16) // LANES * LANES
+        source = lax.broadcasted_iota(jnp.int32, (wide - low, LANES), 0) + low
+        target = lax.broadcasted_iota(jnp.int32, (wide - low, LANES), 1) - k * rest
+        chosen = spread(target + whole, source) & (target >= 0) & (target < rest)
+        shared = shared + dot(grad[:, low:], chosen.astype(F32).astype(BF16))
+    return columns, shared.astype(BF16)
 
 
 def pack_kernel(zone, yi, tokens, cotangent, ids, probs, out):
@@ -103,12 +119,12 @@
         out[k] = gathered[:, k * hidden : (k + 1) * hidden].reshape(groups * hidden, wide)
 
 
-def grads_kernel(core_at, x_at, yo_at, *refs):
+def grads_kernel(narrow, hidden, core_at, x_at, yo_at, *refs):
     blocks, (weights, out, inputs, cotangents) = refs[:-4], refs[-4:]
     chips_x = len(blocks) // CORES
     chips_z, tokens_y, depth, lanes = blocks[0].shape
     wide = weights.shape[2]
-    groups, hidden = out.shape[0], out.shape[1] // 3
+    groups = out.shape[0]
     core, x, yo = core_at[0], x_at[0], yo_at[0]
     lower = lax.broadcasted_iota(jnp.int32, (chips_z, depth, lanes), 2) < lanes // 2
     for k, ref in enumerate(blocks):
@@ -141,19 +157,36 @@
     linear_term = (back * gate * sigma).astype(BF16)
     upward = dot_t(jnp.concatenate([gate_term, linear_term], axis=0), rows).astype(BF16)
     grads = (upward[:units], upward[units:], dot_t(lifted, backs).astype(BF16))
-    for k, grad in enumerate(grads):
-        out[:, k * hidden : (k + 1) * hidden, :] = grad.reshape(groups, hidden, wide)
-
-
-def total_kernel(parts, gate_g, up_g, down_g):
-    hidden = parts.shape[1] // 3
+    tall = 16
+    columns, shared = dense(grads, narrow, tall)
+    halves = hidden // tall
+    for j in range(groups):
+        block = 0
+        for column in sum(columns, []) + [shared]:
+            for half in range(halves):
+                at = j * hidden + half * tall
+                out[j, block] = column[at : at + tall]
+                block += 1
+
+
+def total_kernel(parts, *refs):
     total = parts[0].astype(F32)
     for j in range(1, parts.shape[0]):
         total = total + parts[j].astype(F32)
-    units, narrow = gate_g.shape
-    slim = narrowed(total.astype(BF16), narrow).astype(F32)
-    for k, ref in enumerate((gate_g, up_g, down_g)):
-        ref[...] = slim[k * hidden : k * hidden + units].astype(BF16)
+    units, narrow = refs[0].shape
+    whole = narrow // LANES
+    rest, tall = narrow - whole * LANES, total.shape[1]
+    halves = -(-units // tall)
+    for half in range(halves):
+        at = slice(half * tall, min(units, (half + 1) * tall))
+        height = at.stop - at.start
+        shared = total[len(refs) * whole * halves + half]
+        for k, ref in enumerate(refs):
+            for tile in range(whole):
+                piece = total[(k * whole + tile) * halves + half]
+                ref[at, tile * LANES : (tile + 1) * LANES] = piece[:height].astype(BF16)
+            turn = pltpu.roll(shared, LANES - k * rest, 1) if k else shared
+            ref[at, whole * LANES :] = turn[:height, :rest].astype(BF16)
 
 
 VMEM = pl.BlockSpec(memory_space=pltpu.VMEM)
@@ -212,9 +245,10 @@
         cost_estimate=pl.CostEstimate(flops=0, bytes_accessed=2 * 3 * groups * hidden * wide * 2, transcendentals=0),
         name="regroup",
     )(weights)
+    sent_blocks = (3 * (features // LANES) + 1) * hidden // 16
     parts = pl.pallas_call(
-        grads_kernel,
-        out_shape=jax.ShapeDtypeStruct((groups, 3 * hidden, wide), BF16),
+        functools.partial(grads_kernel, features, hidden),
+        out_shape=jax.ShapeDtypeStruct((groups, sent_blocks, 16, LANES), BF16),
         in_specs=[SMEM] * 3 + [VMEM] * (len(blocks) + 1),
         out_specs=VMEM,
         scratch_shapes=[pltpu.VMEM((chips_z, chips_x * CORES, depth, pairs_y * LANES), BF16)] * 2,

time: 112 us -> 112 us (level)
  no operation moved by 1% of the time
where the time goes in v7:
time: 112 us
  blocking collectives  43.7 us (39%)
  starting transfers between devices  39.2 us (35%)
  between operations  14.2 us (13%)
  Pallas kernels  7.84 us (7%)
  waiting for transfers between devices  5.37 us (5%)
  local copies, waits for them, and re-layouts  1.26 us (1%)
    all_gather x1, blocking collectives, shards(): lax.all_gather(quarter, 'zo').reshape(chips_z, pairs_y * PAIR, depth, LANES)  26.6 us
    ppermute x4, starting transfers between devices, swap(): return lax.ppermute(value, axis, [(0, 1), (1, 0)])  20.2 us
    all_to_all x1, blocking collectives, shards(): met = lax.all_to_all(parts, GROUP, split_axis=0, concat_axis=0, tiled=True)  17.1 us
    all_to_all x1, starting transfers between devices, shards(): lax.all_to_all(sent, ('zi',) + EP, split_axis=0, concat_axis=0, tiled=True)  9.56 us
    ppermute x3, starting transfers between devices, shards(): block = lax.ppermute(along_z, 'x', along) if steps else along_z  9.32 us
    all_to_all x1, waiting for transfers between devices, shards(): lax.all_to_all(sent, ('zi',) + EP, split_axis=0, concat_axis=0, tiled=True)  5.32 us
    pallas_call x1, Pallas kernels, shards(): pl.pallas_call(functools.partial(grads_kernel, features, hidden), out_sha...  3.43 us
  transfers between devices with their start and end apart: 9, of which 1 were waited for; matrix products, arithmetic and copies ran while one was open for 0% of the time, Pallas kernels for 2%

profile of v7, /device:TPU:1, one launch (start us, length us, event | category | flops | bytes accessed | tf_op | source)
XLA Modules:
  0.0 111.6 jit_solution(5314497518781397823)
XLA Ops:
  7.2 1.5 %pack.1 = bf16[2,4,2,16,128]{4,3,2,1,0:T(8,128)(2,1)} custom-call(s32[1]{0:T(128)} %bitcast.3.zone, s32[1]{0:T(128)} %bitcast.4.yi, bf16[15,256]{1,0:T(8,128)(2,1)} %bitcast.36, bf16[15,256]{1,0:T(8,128)(2,1)} %bitcast.37, s32[4,256]{1,0:T(4,128)} %bitcast.38, f32[4,256]{1,0:T(4,128)} %bitcast.39), custom_call_target="tpu_custom_call" | custom-call | tf_op jit(solution)/shard_map/pack/pallas_call | solution.py:214
  8.6 9.6 %all-to-all-start = ((bf16[16,16,128]{2,1,0:T(8,128)(2,1)}), bf16[16,16,128]{2,1,0:T(8,128)(2,1)S(1)}, u32[]{:S(2)}, u32[]{:S(2)}) async-start(bf16[16,16,128]{2,1,0:T(8,128)(2,1)} %bitcast.32), calls=%async_computation | async-start | bytes 131072 | tf_op jit(solution)/shard_map/all_to_all | solution.py:229
  18.2 0.0 all-gather.4.cloned.1.call-start
  18.3 2.0 %widen_weights.1 = bf16[96,1536]{1,0:T(8,128)(2,1)} custom-call(bf16[30,1440]{1,0:T(8,128)(2,1)} %bitcast.33, bf16[30,1440]{1,0:T(8,128)(2,1)} %bitcast.34, bf16[30,1440]{1,0:T(8,128)(2,1)} %bitcast.35), custom_call_target="tpu_custom_call" | custom-call | tf_op jit(solution)/shard_map/widen_weights/pallas_call | solution.py:221
  20.3 5.3 %all-to-all-done = bf16[16,16,128]{2,1,0:T(8,128)(2,1)S(1)} async-done(((bf16[16,16,128]{2,1,0:T(8,128)(2,1)}), bf16[16,16,128]{2,1,0:T(8,128)(2,1)S(1)}, u32[]{:S(2)}, u32[]{:S(2)}) %all-to-all-start) | async-done | bytes 65568 | tf_op jit(solution)/shard_map/all_to_all | solution.py:229
  25.6 0.0 all-gather.4.cloned.1.call-update
  25.6 26.6 %all-gather = bf16[96,16,128]{2,1,0:T(8,128)(2,1)S(1)} all-gather(bf16[16,16,128]{2,1,0:T(8,128)(2,1)S(1)} %all-to-all-done), channel_id=2, replica_groups=mesh['zo'=6,'zi'=2,'x'=4,'core'=2,'yo'=4,'yi'=2] {'zo'}, dimensions={0}, use_global_device_ids=true | all-gather | bytes 458752 | tf_op jit(solution)/shard_map/all_gather | solution.py:232
  52.2 4.4 %collective-permute-start.5 = (bf16[12,8,16,128]{3,2,1,0:T(8,128)(2,1)S(1)}, bf16[12,8,16,128]{3,2,1,0:T(8,128)(2,1)S(1)}, u32[]{:S(2)}, u32[]{:S(2)}) collective-permute-start(bf16[12,8,16,128]{3,2,1,0:T(8,128)(2,1)S(1)} %bitcast.26), channel_id=1, source_target_pairs={{0,48},{16,0},{32,16},{48,32},{1,49},{17,1},{33,17},{49,33},{2,50}... | collective-permute-start | bytes 1179656 | tf_op jit(solution)/shard_map/ppermute | solution.py:236
  56.6 2.4 %collective-permute-start.3 = (bf16[12,8,16,128]{3,2,1,0:T(8,128)(2,1)S(1)}, bf16[12,8,16,128]{3,2,1,0:T(8,128)(2,1)S(1)}, u32[]{:S(2)}, u32[]{:S(2)}) collective-permute-start(bf16[12,8,16,128]{3,2,1,0:T(8,128)(2,1)S(1)} %bitcast.27), channel_id=1, source_target_pairs={{0,32},{16,48},{32,0},{48,16},{1,33},{17,49},{33,1},{49,17},{2,34}... | collective-permute-start | bytes 1179656 | tf_op jit(solution)/shard_map/ppermute | solution.py:236
  59.0 2.5 %collective-permute-start.1 = (bf16[12,8,16,128]{3,2,1,0:T(8,128)(2,1)S(1)}, bf16[12,8,16,128]{3,2,1,0:T(8,128)(2,1)S(1)}, u32[]{:S(2)}, u32[]{:S(2)}) collective-permute-start(bf16[12,8,16,128]{3,2,1,0:T(8,128)(2,1)S(1)} %bitcast.28), channel_id=1, source_target_pairs={{0,16},{16,32},{32,48},{48,0},{1,17},{17,33},{33,49},{49,1},{2,18}... | collective-permute-start | bytes 1179656 | tf_op jit(solution)/shard_map/ppermute | solution.py:236
  61.5 8.8 %collective-permute-start = (bf16[12,8,16,128]{3,2,1,0:T(8,128)(2,1)S(1)}, bf16[12,8,16,128]{3,2,1,0:T(8,128)(2,1)S(1)}, u32[]{:S(2)}, u32[]{:S(2)}) collective-permute-start(bf16[12,8,16,128]{3,2,1,0:T(8,128)(2,1)S(1)} %bitcast.29), channel_id=1, source_target_pairs={{0,8},{8,0},{1,9},{9,1},{2,10},{10,2},{3,11},{11,3},{4,12},{12,4},... | collective-permute-start | bytes 1179656 | tf_op jit(solution)/shard_map/ppermute | solution.py:201
  70.4 0.0 collective-permute-done.5.refs_6_
  70.4 5.9 %collective-permute-start.6 = (bf16[12,8,16,128]{3,2,1,0:T(8,128)(2,1)S(1)}, bf16[12,8,16,128]{3,2,1,0:T(8,128)(2,1)S(1)}, u32[]{:S(2)}, u32[]{:S(2)}) collective-permute-start(bf16[12,8,16,128]{3,2,1,0:T(8,128)(2,1)S(1)} %collective-permute-done.5.refs_6_), channel_id=1, source_target_pairs={{0,8},{8,0},{1,9},{9,1},{2,10},{10,2},{3,11},{11,3},{4,12},{12,4},... | collective-permute-start | bytes 1179656 | tf_op jit(solution)/shard_map/ppermute | solution.py:201
  76.3 0.0 collective-permute-done.3.refs_4_
  76.3 1.9 %collective-permute-start.4 = (bf16[12,8,16,128]{3,2,1,0:T(8,128)(2,1)S(1)}, bf16[12,8,16,128]{3,2,1,0:T(8,128)(2,1)S(1)}, u32[]{:S(2)}, u32[]{:S(2)}) collective-permute-start(bf16[12,8,16,128]{3,2,1,0:T(8,128)(2,1)S(1)} %collective-permute-done.3.refs_4_), channel_id=1, source_target_pairs={{0,8},{8,0},{1,9},{9,1},{2,10},{10,2},{3,11},{11,3},{4,12},{12,4},... | collective-permute-start | bytes 1179656 | tf_op jit(solution)/shard_map/ppermute | solution.py:201
  78.2 0.0 collective-permute-done.1.refs_2_
  78.2 3.6 %collective-permute-start.2 = (bf16[12,8,16,128]{3,2,1,0:T(8,128)(2,1)S(1)}, bf16[12,8,16,128]{3,2,1,0:T(8,128)(2,1)S(1)}, u32[]{:S(2)}, u32[]{:S(2)}) collective-permute-start(bf16[12,8,16,128]{3,2,1,0:T(8,128)(2,1)S(1)} %collective-permute-done.1.refs_2_), channel_id=1, source_target_pairs={{0,8},{8,0},{1,9},{9,1},{2,10},{10,2},{3,11},{11,3},{4,12},{12,4},... | collective-permute-start | bytes 1179656 | tf_op jit(solution)/shard_map/ppermute | solution.py:201
  81.8 0.0 all-gather.4.cloned.1.call-done
  81.9 0.0 copy-start
  81.9 1.3 %copy-done = bf16[384,1536]{1,0:T(8,128)(2,1)S(1)} copy-done((bf16[384,1536]{1,0:T(8,128)(2,1)S(1)}, bf16[384,1536]{1,0:T(8,128)(2,1)}, u32[]{:S(2)}) %copy-start) | copy-done | bytes 1179672
  83.1 0.1 regroup.1.refs_8_
  83.2 0.0 collective-permute-done.refs_1_
  83.2 0.0 collective-permute-done.6.refs_7_
  83.3 0.0 collective-permute-done.4.refs_5_
  83.3 0.0 collective-permute-done.2.refs_3_
  83.3 3.4 %grads.1 = bf16[4,68,16,128]{3,2,1,0:T(8,128)(2,1)S(1)} custom-call(s32[1]{0:T(128)} %bitcast.core_at, s32[1]{0:T(128)} %bitcast.1.x_at, s32[1]{0:T(128)} %bitcast.2.yo_at, bf16[12,8,16,128]{3,2,1,0:T(8,128)(2,1)S(1)} %bitcast.30, bf16[12,8,16,128]{3,2,1,0:T(8,128)(2,1)S(1)} %collective-permute-done.refs_1_, ...), custom_call_target="tpu_custom_call" | custom-call | tf_op jit(solution)/shard_map/grads/pallas_call | solution.py:249
  86.7 17.1 %all_to_all.10.parts = bf16[4,68,16,128]{3,2,1,0:T(8,128)(2,1)S(1)} all-to-all(bf16[4,68,16,128]{3,2,1,0:T(8,128)(2,1)S(1)} %grads.1), channel_id=1, replica_groups=mesh['zo'=6,'zi'=2,'x'=4,'core'=2,'yo'=4,'yi'=2] {'zi','yi'}, dimensions={0} | all-to-all | bytes 2228224 | tf_op jit(solution)/shard_map/all_to_all | solution.py:258
  103.8 0.9 total.1
Async XLA Ops:
  8.6 16.9 %all-to-all-start = ((bf16[16,16,128]{2,1,0:T(8,128)(2,1)}), bf16[16,16,128]{2,1,0:T(8,128)(2,1)S(1)}, u32[]{:S(2)}, u32[]{:S(2)}) async-start(bf16[16,16,128]{2,1,0:T(8,128)(2,1)} %bitcast.32), calls=%async_computation | async-start | bytes 131072 | tf_op jit(solution)/shard_map/all_to_all | solution.py:229
  18.2 63.7 %all-gather.4.cloned.1.call-start = ((), (), s32[]{:S(2)}) async-start(), calls=%async_computation.2 | async-start | bytes 1474560 | tf_op jit(solution)/shard_map/all_gather | solution.py:231
  52.2 18.2 %collective-permute-start.5 = (bf16[12,8,16,128]{3,2,1,0:T(8,128)(2,1)S(1)}, bf16[12,8,16,128]{3,2,1,0:T(8,128)(2,1)S(1)}, u32[]{:S(2)}, u32[]{:S(2)}) collective-permute-start(bf16[12,8,16,128]{3,2,1,0:T(8,128)(2,1)S(1)} %bitcast.26), channel_id=1, source_target_pairs={{0,48},{16,0},{32,16},{48,32},{1,49},{17,1},{33,17},{49,33},{2,50}... | collective-permute-start | bytes 1179656 | tf_op jit(solution)/shard_map/ppermute | solution.py:236
  56.6 19.7 %collective-permute-start.3 = (bf16[12,8,16,128]{3,2,1,0:T(8,128)(2,1)S(1)}, bf16[12,8,16,128]{3,2,1,0:T(8,128)(2,1)S(1)}, u32[]{:S(2)}, u32[]{:S(2)}) collective-permute-start(bf16[12,8,16,128]{3,2,1,0:T(8,128)(2,1)S(1)} %bitcast.27), channel_id=1, source_target_pairs={{0,32},{16,48},{32,0},{48,16},{1,33},{17,49},{33,1},{49,17},{2,34}... | collective-permute-start | bytes 1179656 | tf_op jit(solution)/shard_map/ppermute | solution.py:236
  59.0 19.2 %collective-permute-start.1 = (bf16[12,8,16,128]{3,2,1,0:T(8,128)(2,1)S(1)}, bf16[12,8,16,128]{3,2,1,0:T(8,128)(2,1)S(1)}, u32[]{:S(2)}, u32[]{:S(2)}) collective-permute-start(bf16[12,8,16,128]{3,2,1,0:T(8,128)(2,1)S(1)} %bitcast.28), channel_id=1, source_target_pairs={{0,16},{16,32},{32,48},{48,0},{1,17},{17,33},{33,49},{49,1},{2,18}... | collective-permute-start | bytes 1179656 | tf_op jit(solution)/shard_map/ppermute | solution.py:236
  61.5 21.7 %collective-permute-start = (bf16[12,8,16,128]{3,2,1,0:T(8,128)(2,1)S(1)}, bf16[12,8,16,128]{3,2,1,0:T(8,128)(2,1)S(1)}, u32[]{:S(2)}, u32[]{:S(2)}) collective-permute-start(bf16[12,8,16,128]{3,2,1,0:T(8,128)(2,1)S(1)} %bitcast.29), channel_id=1, source_target_pairs={{0,8},{8,0},{1,9},{9,1},{2,10},{10,2},{3,11},{11,3},{4,12},{12,4},... | collective-permute-start | bytes 1179656 | tf_op jit(solution)/shard_map/ppermute | solution.py:201
  70.4 12.9 %collective-permute-start.6 = (bf16[12,8,16,128]{3,2,1,0:T(8,128)(2,1)S(1)}, bf16[12,8,16,128]{3,2,1,0:T(8,128)(2,1)S(1)}, u32[]{:S(2)}, u32[]{:S(2)}) collective-permute-start(bf16[12,8,16,128]{3,2,1,0:T(8,128)(2,1)S(1)} %collective-permute-done.5.refs_6_), channel_id=1, source_target_pairs={{0,8},{8,0},{1,9},{9,1},{2,10},{10,2},{3,11},{11,3},{4,12},{12,4},... | collective-permute-start | bytes 1179656 | tf_op jit(solution)/shard_map/ppermute | solution.py:201
  76.3 7.0 %collective-permute-start.4 = (bf16[12,8,16,128]{3,2,1,0:T(8,128)(2,1)S(1)}, bf16[12,8,16,128]{3,2,1,0:T(8,128)(2,1)S(1)}, u32[]{:S(2)}, u32[]{:S(2)}) collective-permute-start(bf16[12,8,16,128]{3,2,1,0:T(8,128)(2,1)S(1)} %collective-permute-done.3.refs_4_), channel_id=1, source_target_pairs={{0,8},{8,0},{1,9},{9,1},{2,10},{10,2},{3,11},{11,3},{4,12},{12,4},... | collective-permute-start | bytes 1179656 | tf_op jit(solution)/shard_map/ppermute | solution.py:201
  78.2 5.1 %collective-permute-start.2 = (bf16[12,8,16,128]{3,2,1,0:T(8,128)(2,1)S(1)}, bf16[12,8,16,128]{3,2,1,0:T(8,128)(2,1)S(1)}, u32[]{:S(2)}, u32[]{:S(2)}) collective-permute-start(bf16[12,8,16,128]{3,2,1,0:T(8,128)(2,1)S(1)} %collective-permute-done.1.refs_2_), channel_id=1, source_target_pairs={{0,8},{8,0},{1,9},{9,1},{2,10},{10,2},{3,11},{11,3},{4,12},{12,4},... | collective-permute-start | bytes 1179656 | tf_op jit(solution)/shard_map/ppermute | solution.py:201
  81.9 1.3 %copy-start = (bf16[384,1536]{1,0:T(8,128)(2,1)S(1)}, bf16[384,1536]{1,0:T(8,128)(2,1)}, u32[]{:S(2)}) copy-start(bf16[384,1536]{1,0:T(8,128)(2,1)} %all-gather.4.cloned.1.call-done) | copy-start | bytes 3538948
Sparse Core Ops, SparseCore 0:
  25.7 42.1 all-gather.3

commit v8 on v7

--- a/solution.py
+++ b/solution.py
@@ -67,14 +67,15 @@
     return jnp.concatenate(tiles, axis=1)
 
 
-def dense(grads, narrow, tall):
+def dense(grads, narrow):
     wide, whole = grads[0].shape[1], narrow // LANES * LANES
     rest = narrow - whole
-    columns = [[] for _ in grads]
+    main = narrowed(jnp.concatenate(grads, axis=0), whole)
+    count = grads[0].shape[0]
+    columns = []
     shared = 0.0
     for k, grad in enumerate(grads):
-        main = narrowed(grad, whole)
-        columns[k] = [main[:, at : at + LANES] for at in range(0, whole, LANES)]
+        columns.append([main[k * count : (k + 1) * count, at : at + LANES] for at in range(0, whole, LANES)])
         low = (whole // 15 * 16) // LANES * LANES
         source = lax.broadcasted_iota(jnp.int32, (wide - low, LANES), 0) + low
         target = lax.broadcasted_iota(jnp.int32, (wide - low, LANES), 1) - k * rest
@@ -158,7 +159,7 @@
     upward = dot_t(jnp.concatenate([gate_term, linear_term], axis=0), rows).astype(BF16)
     grads = (upward[:units], upward[units:], dot_t(lifted, backs).astype(BF16))
     tall = 16
-    columns, shared = dense(grads, narrow, tall)
+    columns, shared = dense(grads, narrow)
     halves = hidden // tall
     for j in range(groups):
         block = 0

time: 112 us -> 112 us (level)
  no operation moved by 1% of the time
where the time goes in v8:
time: 112 us; the launch traced here: 111 us
  blocking collectives  43.7 us (39%)
  starting transfers between devices  39.2 us (35%)
  between operations  14.2 us (13%)
  Pallas kernels  7.7 us (7%)
  waiting for transfers between devices  5.37 us (5%)
  local copies, waits for them, and re-layouts  1.26 us (1%)
    all_gather x1, blocking collectives, shards(): lax.all_gather(quarter, 'zo').reshape(chips_z, pairs_y * PAIR, depth, LANES)  26.6 us
    ppermute x4, starting transfers between devices, swap(): return lax.ppermute(value, axis, [(0, 1), (1, 0)])  20.2 us
    all_to_all x1, blocking collectives, shards(): met = lax.all_to_all(parts, GROUP, split_axis=0, concat_axis=0, tiled=True)  17.1 us
    all_to_all x1, starting transfers between devices, shards(): lax.all_to_all(sent, ('zi',) + EP, split_axis=0, concat_axis=0, tiled=True)  9.56 us
    ppermute x3, starting transfers between devices, shards(): block = lax.ppermute(along_z, 'x', along) if steps else along_z  9.32 us
    all_to_all x1, waiting for transfers between devices, shards(): lax.all_to_all(sent, ('zi',) + EP, split_axis=0, concat_axis=0, tiled=True)  5.32 us
    pallas_call x1, Pallas kernels, shards(): pl.pallas_call(functools.partial(grads_kernel, features, hidden), out_sha...  3.28 us
  transfers between devices with their start and end apart: 9, of which 1 were waited for; matrix products, arithmetic and copies ran while one was open for 0% of the time, Pallas kernels for 2%

profile of v8, /device:TPU:1, one launch (start us, length us, event | category | flops | bytes accessed | tf_op | source)
XLA Modules:
  0.0 111.4 jit_solution(8366655158398183086)
XLA Ops:
  7.2 1.5 %pack.1 = bf16[2,4,2,16,128]{4,3,2,1,0:T(8,128)(2,1)} custom-call(s32[1]{0:T(128)} %bitcast.3.zone, s32[1]{0:T(128)} %bitcast.4.yi, bf16[15,256]{1,0:T(8,128)(2,1)} %bitcast.36, bf16[15,256]{1,0:T(8,128)(2,1)} %bitcast.37, s32[4,256]{1,0:T(4,128)} %bitcast.38, f32[4,256]{1,0:T(4,128)} %bitcast.39), custom_call_target="tpu_custom_call" | custom-call | tf_op jit(solution)/shard_map/pack/pallas_call | solution.py:215
  8.6 9.6 %all-to-all-start = ((bf16[16,16,128]{2,1,0:T(8,128)(2,1)}), bf16[16,16,128]{2,1,0:T(8,128)(2,1)S(1)}, u32[]{:S(2)}, u32[]{:S(2)}) async-start(bf16[16,16,128]{2,1,0:T(8,128)(2,1)} %bitcast.32), calls=%async_computation | async-start | bytes 131072 | tf_op jit(solution)/shard_map/all_to_all | solution.py:230
  18.2 0.0 all-gather.4.cloned.1.call-start
  18.3 2.0 %widen_weights.1 = bf16[96,1536]{1,0:T(8,128)(2,1)} custom-call(bf16[30,1440]{1,0:T(8,128)(2,1)} %bitcast.33, bf16[30,1440]{1,0:T(8,128)(2,1)} %bitcast.34, bf16[30,1440]{1,0:T(8,128)(2,1)} %bitcast.35), custom_call_target="tpu_custom_call" | custom-call | tf_op jit(solution)/shard_map/widen_weights/pallas_call | solution.py:222
  20.3 5.3 %all-to-all-done = bf16[16,16,128]{2,1,0:T(8,128)(2,1)S(1)} async-done(((bf16[16,16,128]{2,1,0:T(8,128)(2,1)}), bf16[16,16,128]{2,1,0:T(8,128)(2,1)S(1)}, u32[]{:S(2)}, u32[]{:S(2)}) %all-to-all-start) | async-done | bytes 65568 | tf_op jit(solution)/shard_map/all_to_all | solution.py:230
  25.6 0.0 all-gather.4.cloned.1.call-update
  25.6 26.6 %all-gather = bf16[96,16,128]{2,1,0:T(8,128)(2,1)S(1)} all-gather(bf16[16,16,128]{2,1,0:T(8,128)(2,1)S(1)} %all-to-all-done), channel_id=2, replica_groups=mesh['zo'=6,'zi'=2,'x'=4,'core'=2,'yo'=4,'yi'=2] {'zo'}, dimensions={0}, use_global_device_ids=true | all-gather | bytes 458752 | tf_op jit(solution)/shard_map/all_gather | solution.py:233
  52.2 4.4 %collective-permute-start.5 = (bf16[12,8,16,128]{3,2,1,0:T(8,128)(2,1)S(1)}, bf16[12,8,16,128]{3,2,1,0:T(8,128)(2,1)S(1)}, u32[]{:S(2)}, u32[]{:S(2)}) collective-permute-start(bf16[12,8,16,128]{3,2,1,0:T(8,128)(2,1)S(1)} %bitcast.26), channel_id=1, source_target_pairs={{0,48},{16,0},{32,16},{48,32},{1,49},{17,1},{33,17},{49,33},{2,50}... | collective-permute-start | bytes 1179656 | tf_op jit(solution)/shard_map/ppermute | solution.py:237
  56.6 2.4 %collective-permute-start.3 = (bf16[12,8,16,128]{3,2,1,0:T(8,128)(2,1)S(1)}, bf16[12,8,16,128]{3,2,1,0:T(8,128)(2,1)S(1)}, u32[]{:S(2)}, u32[]{:S(2)}) collective-permute-start(bf16[12,8,16,128]{3,2,1,0:T(8,128)(2,1)S(1)} %bitcast.27), channel_id=1, source_target_pairs={{0,32},{16,48},{32,0},{48,16},{1,33},{17,49},{33,1},{49,17},{2,34}... | collective-permute-start | bytes 1179656 | tf_op jit(solution)/shard_map/ppermute | solution.py:237
  59.0 2.5 %collective-permute-start.1 = (bf16[12,8,16,128]{3,2,1,0:T(8,128)(2,1)S(1)}, bf16[12,8,16,128]{3,2,1,0:T(8,128)(2,1)S(1)}, u32[]{:S(2)}, u32[]{:S(2)}) collective-permute-start(bf16[12,8,16,128]{3,2,1,0:T(8,128)(2,1)S(1)} %bitcast.28), channel_id=1, source_target_pairs={{0,16},{16,32},{32,48},{48,0},{1,17},{17,33},{33,49},{49,1},{2,18}... | collective-permute-start | bytes 1179656 | tf_op jit(solution)/shard_map/ppermute | solution.py:237
  61.5 8.8 %collective-permute-start = (bf16[12,8,16,128]{3,2,1,0:T(8,128)(2,1)S(1)}, bf16[12,8,16,128]{3,2,1,0:T(8,128)(2,1)S(1)}, u32[]{:S(2)}, u32[]{:S(2)}) collective-permute-start(bf16[12,8,16,128]{3,2,1,0:T(8,128)(2,1)S(1)} %bitcast.29), channel_id=1, source_target_pairs={{0,8},{8,0},{1,9},{9,1},{2,10},{10,2},{3,11},{11,3},{4,12},{12,4},... | collective-permute-start | bytes 1179656 | tf_op jit(solution)/shard_map/ppermute | solution.py:202
  70.4 0.0 collective-permute-done.5.refs_6_
  70.4 5.9 %collective-permute-start.6 = (bf16[12,8,16,128]{3,2,1,0:T(8,128)(2,1)S(1)}, bf16[12,8,16,128]{3,2,1,0:T(8,128)(2,1)S(1)}, u32[]{:S(2)}, u32[]{:S(2)}) collective-permute-start(bf16[12,8,16,128]{3,2,1,0:T(8,128)(2,1)S(1)} %collective-permute-done.5.refs_6_), channel_id=1, source_target_pairs={{0,8},{8,0},{1,9},{9,1},{2,10},{10,2},{3,11},{11,3},{4,12},{12,4},... | collective-permute-start | bytes 1179656 | tf_op jit(solution)/shard_map/ppermute | solution.py:202
  76.3 0.0 collective-permute-done.3.refs_4_
  76.3 1.9 %collective-permute-start.4 = (bf16[12,8,16,128]{3,2,1,0:T(8,128)(2,1)S(1)}, bf16[12,8,16,128]{3,2,1,0:T(8,128)(2,1)S(1)}, u32[]{:S(2)}, u32[]{:S(2)}) collective-permute-start(bf16[12,8,16,128]{3,2,1,0:T(8,128)(2,1)S(1)} %collective-permute-done.3.refs_4_), channel_id=1, source_target_pairs={{0,8},{8,0},{1,9},{9,1},{2,10},{10,2},{3,11},{11,3},{4,12},{12,4},... | collective-permute-start | bytes 1179656 | tf_op jit(solution)/shard_map/ppermute | solution.py:202
  78.2 0.0 collective-permute-done.1.refs_2_
  78.2 3.6 %collective-permute-start.2 = (bf16[12,8,16,128]{3,2,1,0:T(8,128)(2,1)S(1)}, bf16[12,8,16,128]{3,2,1,0:T(8,128)(2,1)S(1)}, u32[]{:S(2)}, u32[]{:S(2)}) collective-permute-start(bf16[12,8,16,128]{3,2,1,0:T(8,128)(2,1)S(1)} %collective-permute-done.1.refs_2_), channel_id=1, source_target_pairs={{0,8},{8,0},{1,9},{9,1},{2,10},{10,2},{3,11},{11,3},{4,12},{12,4},... | collective-permute-start | bytes 1179656 | tf_op jit(solution)/shard_map/ppermute | solution.py:202
  81.8 0.0 all-gather.4.cloned.1.call-done
  81.9 0.0 copy-start
  81.9 1.3 %copy-done = bf16[384,1536]{1,0:T(8,128)(2,1)S(1)} copy-done((bf16[384,1536]{1,0:T(8,128)(2,1)S(1)}, bf16[384,1536]{1,0:T(8,128)(2,1)}, u32[]{:S(2)}) %copy-start) | copy-done | bytes 1179672
  83.1 0.1 regroup.1.refs_8_
  83.2 0.0 collective-permute-done.refs_1_
  83.2 0.0 collective-permute-done.6.refs_7_
  83.3 0.0 collective-permute-done.4.refs_5_
  83.3 0.0 collective-permute-done.2.refs_3_
  83.3 3.3 %grads.1 = bf16[4,68,16,128]{3,2,1,0:T(8,128)(2,1)S(1)} custom-call(s32[1]{0:T(128)} %bitcast.core_at, s32[1]{0:T(128)} %bitcast.1.x_at, s32[1]{0:T(128)} %bitcast.2.yo_at, bf16[12,8,16,128]{3,2,1,0:T(8,128)(2,1)S(1)} %bitcast.30, bf16[12,8,16,128]{3,2,1,0:T(8,128)(2,1)S(1)} %collective-permute-done.refs_1_, ...), custom_call_target="tpu_custom_call" | custom-call | tf_op jit(solution)/shard_map/grads/pallas_call | solution.py:250
  86.6 17.1 %all_to_all.10.parts = bf16[4,68,16,128]{3,2,1,0:T(8,128)(2,1)S(1)} all-to-all(bf16[4,68,16,128]{3,2,1,0:T(8,128)(2,1)S(1)} %grads.1), channel_id=1, replica_groups=mesh['zo'=6,'zi'=2,'x'=4,'core'=2,'yo'=4,'yi'=2] {'zi','yi'}, dimensions={0} | all-to-all | bytes 2228224 | tf_op jit(solution)/shard_map/all_to_all | solution.py:259
  103.7 0.9 total.1
Async XLA Ops:
  8.6 16.9 %all-to-all-start = ((bf16[16,16,128]{2,1,0:T(8,128)(2,1)}), bf16[16,16,128]{2,1,0:T(8,128)(2,1)S(1)}, u32[]{:S(2)}, u32[]{:S(2)}) async-start(bf16[16,16,128]{2,1,0:T(8,128)(2,1)} %bitcast.32), calls=%async_computation | async-start | bytes 131072 | tf_op jit(solution)/shard_map/all_to_all | solution.py:230
  18.2 63.7 %all-gather.4.cloned.1.call-start = ((), (), s32[]{:S(2)}) async-start(), calls=%async_computation.2 | async-start | bytes 1474560 | tf_op jit(solution)/shard_map/all_gather | solution.py:232
  52.2 18.2 %collective-permute-start.5 = (bf16[12,8,16,128]{3,2,1,0:T(8,128)(2,1)S(1)}, bf16[12,8,16,128]{3,2,1,0:T(8,128)(2,1)S(1)}, u32[]{:S(2)}, u32[]{:S(2)}) collective-permute-start(bf16[12,8,16,128]{3,2,1,0:T(8,128)(2,1)S(1)} %bitcast.26), channel_id=1, source_target_pairs={{0,48},{16,0},{32,16},{48,32},{1,49},{17,1},{33,17},{49,33},{2,50}... | collective-permute-start | bytes 1179656 | tf_op jit(solution)/shard_map/ppermute | solution.py:237
  56.6 19.7 %collective-permute-start.3 = (bf16[12,8,16,128]{3,2,1,0:T(8,128)(2,1)S(1)}, bf16[12,8,16,128]{3,2,1,0:T(8,128)(2,1)S(1)}, u32[]{:S(2)}, u32[]{:S(2)}) collective-permute-start(bf16[12,8,16,128]{3,2,1,0:T(8,128)(2,1)S(1)} %bitcast.27), channel_id=1, source_target_pairs={{0,32},{16,48},{32,0},{48,16},{1,33},{17,49},{33,1},{49,17},{2,34}... | collective-permute-start | bytes 1179656 | tf_op jit(solution)/shard_map/ppermute | solution.py:237
  59.0 19.2 %collective-permute-start.1 = (bf16[12,8,16,128]{3,2,1,0:T(8,128)(2,1)S(1)}, bf16[12,8,16,128]{3,2,1,0:T(8,128)(2,1)S(1)}, u32[]{:S(2)}, u32[]{:S(2)}) collective-permute-start(bf16[12,8,16,128]{3,2,1,0:T(8,128)(2,1)S(1)} %bitcast.28), channel_id=1, source_target_pairs={{0,16},{16,32},{32,48},{48,0},{1,17},{17,33},{33,49},{49,1},{2,18}... | collective-permute-start | bytes 1179656 | tf_op jit(solution)/shard_map/ppermute | solution.py:237
  61.5 21.7 %collective-permute-start = (bf16[12,8,16,128]{3,2,1,0:T(8,128)(2,1)S(1)}, bf16[12,8,16,128]{3,2,1,0:T(8,128)(2,1)S(1)}, u32[]{:S(2)}, u32[]{:S(2)}) collective-permute-start(bf16[12,8,16,128]{3,2,1,0:T(8,128)(2,1)S(1)} %bitcast.29), channel_id=1, source_target_pairs={{0,8},{8,0},{1,9},{9,1},{2,10},{10,2},{3,11},{11,3},{4,12},{12,4},... | collective-permute-start | bytes 1179656 | tf_op jit(solution)/shard_map/ppermute | solution.py:202
  70.4 12.9 %collective-permute-start.6 = (bf16[12,8,16,128]{3,2,1,0:T(8,128)(2,1)S(1)}, bf16[12,8,16,128]{3,2,1,0:T(8,128)(2,1)S(1)}, u32[]{:S(2)}, u32[]{:S(2)}) collective-permute-start(bf16[12,8,16,128]{3,2,1,0:T(8,128)(2,1)S(1)} %collective-permute-done.5.refs_6_), channel_id=1, source_target_pairs={{0,8},{8,0},{1,9},{9,1},{2,10},{10,2},{3,11},{11,3},{4,12},{12,4},... | collective-permute-start | bytes 1179656 | tf_op jit(solution)/shard_map/ppermute | solution.py:202
  76.3 7.0 %collective-permute-start.4 = (bf16[12,8,16,128]{3,2,1,0:T(8,128)(2,1)S(1)}, bf16[12,8,16,128]{3,2,1,0:T(8,128)(2,1)S(1)}, u32[]{:S(2)}, u32[]{:S(2)}) collective-permute-start(bf16[12,8,16,128]{3,2,1,0:T(8,128)(2,1)S(1)} %collective-permute-done.3.refs_4_), channel_id=1, source_target_pairs={{0,8},{8,0},{1,9},{9,1},{2,10},{10,2},{3,11},{11,3},{4,12},{12,4},... | collective-permute-start | bytes 1179656 | tf_op jit(solution)/shard_map/ppermute | solution.py:202
  78.2 5.1 %collective-permute-start.2 = (bf16[12,8,16,128]{3,2,1,0:T(8,128)(2,1)S(1)}, bf16[12,8,16,128]{3,2,1,0:T(8,128)(2,1)S(1)}, u32[]{:S(2)}, u32[]{:S(2)}) collective-permute-start(bf16[12,8,16,128]{3,2,1,0:T(8,128)(2,1)S(1)} %collective-permute-done.1.refs_2_), channel_id=1, source_target_pairs={{0,8},{8,0},{1,9},{9,1},{2,10},{10,2},{3,11},{11,3},{4,12},{12,4},... | collective-permute-start | bytes 1179656 | tf_op jit(solution)/shard_map/ppermute | solution.py:202
  81.9 1.3 %copy-start = (bf16[384,1536]{1,0:T(8,128)(2,1)S(1)}, bf16[384,1536]{1,0:T(8,128)(2,1)}, u32[]{:S(2)}) copy-start(bf16[384,1536]{1,0:T(8,128)(2,1)} %all-gather.4.cloned.1.call-done) | copy-start | bytes 3538948
Sparse Core Ops, SparseCore 0:
  25.7 42.1 all-gather.3

commit v9 on v6

--- a/solution.py
+++ b/solution.py
@@ -67,7 +67,14 @@
     return jnp.concatenate(tiles, axis=1)
 
 
-def pack_kernel(zone, yi, tokens, cotangent, ids, probs, out):
+def pack_kernel(zone, yi, *refs):
+    sources, out, held, sems = refs[:4], refs[4], refs[5:9], refs[9]
+    copies = [pltpu.make_async_copy(a, b, sems.at[k]) for k, (a, b) in enumerate(zip(sources, held))]
+    for copy in copies:
+        copy.start()
+    for copy in copies:
+        copy.wait()
+    tokens, cotangent, ids, probs = held
     count = tokens.shape[1]
     mine = ids[...] == zone[0]
     weight = jnp.sum(jnp.where(mine, probs[...], 0.0), axis=0, keepdims=True)
@@ -178,13 +185,15 @@
     hidden = -(-units // 16) * 16
     zone = lax.axis_index(("zo", "zi"))
 
+    sources = (tokens.T, grad_out.T, expert_ids.T, probs.T)
     packed = pl.pallas_call(
         pack_kernel,
         out_shape=jax.ShapeDtypeStruct((PAIR, pairs_y, PAIR, depth, LANES), BF16),
-        in_specs=[SMEM, SMEM, VMEM, VMEM, VMEM, VMEM],
-        out_specs=VMEM,
+        in_specs=[SMEM] * 2 + [pl.BlockSpec(memory_space=pl.ANY)] * 4,
+        out_specs=VMEM,
+        scratch_shapes=[pltpu.VMEM(source.shape, source.dtype) for source in sources] + [pltpu.SemaphoreType.DMA((4,))],
         name="pack",
-    )(zone.reshape(1), lax.axis_index("yi").reshape(1), tokens.T, grad_out.T, expert_ids.T, probs.T)
+    )(zone.reshape(1), lax.axis_index("yi").reshape(1), *sources)
     stacked = pl.pallas_call(
         weights_kernel,
         out_shape=jax.ShapeDtypeStruct((3 * hidden, wide), BF16),

time: 112 us -> 112 us (level)
  no operation moved by 1% of the time
where the time goes in v9:
time: 112 us
  blocking collectives  44 us (39%)
  starting transfers between devices  39.2 us (35%)
  between operations  14.2 us (13%)
  Pallas kernels  7.46 us (7%)
  waiting for transfers between devices  5.37 us (5%)
  local copies, waits for them, and re-layouts  1.26 us (1%)
    all_gather x1, blocking collectives, shards(): lax.all_gather(quarter, 'zo').reshape(chips_z, pairs_y * PAIR, depth, LANES)  26.6 us
    ppermute x4, starting transfers between devices, swap(): return lax.ppermute(value, axis, [(0, 1), (1, 0)])  20.2 us
    all_to_all x1, blocking collectives, shards(): met = lax.all_to_all(parts, GROUP, split_axis=0, concat_axis=0, tiled=True)  17.4 us
    all_to_all x1, starting transfers between devices, shards(): lax.all_to_all(sent, ('zi',) + EP, split_axis=0, concat_axis=0, tiled=True)  9.58 us
    ppermute x3, starting transfers between devices, shards(): block = lax.ppermute(along_z, 'x', along) if steps else along_z  9.32 us
    all_to_all x1, waiting for transfers between devices, shards(): lax.all_to_all(sent, ('zi',) + EP, split_axis=0, concat_axis=0, tiled=True)  5.32 us
    pallas_call x1, Pallas kernels, shards(): pl.pallas_call(grads_kernel, out_shape=jax.ShapeDtypeStruct((groups, 3 *...  2.59 us
  transfers between devices with their start and end apart: 9, of which 1 were waited for; matrix products, arithmetic and copies ran while one was open for 0% of the time, Pallas kernels for 2%

profile of v9, /device:TPU:1, one launch (start us, length us, event | category | flops | bytes accessed | tf_op | source)
XLA Modules:
  0.0 111.5 jit_solution(1033288921193079094)
XLA Ops:
  7.2 1.5 %pack.1 = bf16[2,4,2,16,128]{4,3,2,1,0:T(8,128)(2,1)} custom-call(s32[1]{0:T(128)} %bitcast.3.zone, s32[1]{0:T(128)} %bitcast.4.yi, bf16[15,256]{1,0:T(8,128)(2,1)} %bitcast.36, bf16[15,256]{1,0:T(8,128)(2,1)} %bitcast.37, s32[4,256]{1,0:T(4,128)} %bitcast.38, f32[4,256]{1,0:T(4,128)} %bitcast.39), custom_call_target="tpu_custom_call" | custom-call | tf_op jit(solution)/shard_map/pack/pallas_call | solution.py:189
  8.7 9.6 %all-to-all-start = ((bf16[16,16,128]{2,1,0:T(8,128)(2,1)}), bf16[16,16,128]{2,1,0:T(8,128)(2,1)S(1)}, u32[]{:S(2)}, u32[]{:S(2)}) async-start(bf16[16,16,128]{2,1,0:T(8,128)(2,1)} %bitcast.32), calls=%async_computation | async-start | bytes 131072 | tf_op jit(solution)/shard_map/all_to_all | solution.py:205
  18.3 0.0 all-gather.4.cloned.1.call-start
  18.3 2.0 %widen_weights.1 = bf16[96,1536]{1,0:T(8,128)(2,1)} custom-call(bf16[30,1440]{1,0:T(8,128)(2,1)} %bitcast.33, bf16[30,1440]{1,0:T(8,128)(2,1)} %bitcast.34, bf16[30,1440]{1,0:T(8,128)(2,1)} %bitcast.35), custom_call_target="tpu_custom_call" | custom-call | tf_op jit(solution)/shard_map/widen_weights/pallas_call | solution.py:197
  20.3 5.3 %all-to-all-done = bf16[16,16,128]{2,1,0:T(8,128)(2,1)S(1)} async-done(((bf16[16,16,128]{2,1,0:T(8,128)(2,1)}), bf16[16,16,128]{2,1,0:T(8,128)(2,1)S(1)}, u32[]{:S(2)}, u32[]{:S(2)}) %all-to-all-start) | async-done | bytes 65568 | tf_op jit(solution)/shard_map/all_to_all | solution.py:205
  25.6 0.0 all-gather.4.cloned.1.call-update
  25.7 26.6 %all-gather = bf16[96,16,128]{2,1,0:T(8,128)(2,1)S(1)} all-gather(bf16[16,16,128]{2,1,0:T(8,128)(2,1)S(1)} %all-to-all-done), channel_id=2, replica_groups=mesh['zo'=6,'zi'=2,'x'=4,'core'=2,'yo'=4,'yi'=2] {'zo'}, dimensions={0}, use_global_device_ids=true | all-gather | bytes 458752 | tf_op jit(solution)/shard_map/all_gather | solution.py:208
  52.2 4.4 %collective-permute-start.5 = (bf16[12,8,16,128]{3,2,1,0:T(8,128)(2,1)S(1)}, bf16[12,8,16,128]{3,2,1,0:T(8,128)(2,1)S(1)}, u32[]{:S(2)}, u32[]{:S(2)}) collective-permute-start(bf16[12,8,16,128]{3,2,1,0:T(8,128)(2,1)S(1)} %bitcast.26), channel_id=1, source_target_pairs={{0,48},{16,0},{32,16},{48,32},{1,49},{17,1},{33,17},{49,33},{2,50}... | collective-permute-start | bytes 1179656 | tf_op jit(solution)/shard_map/ppermute | solution.py:212
  56.6 2.4 %collective-permute-start.3 = (bf16[12,8,16,128]{3,2,1,0:T(8,128)(2,1)S(1)}, bf16[12,8,16,128]{3,2,1,0:T(8,128)(2,1)S(1)}, u32[]{:S(2)}, u32[]{:S(2)}) collective-permute-start(bf16[12,8,16,128]{3,2,1,0:T(8,128)(2,1)S(1)} %bitcast.27), channel_id=1, source_target_pairs={{0,32},{16,48},{32,0},{48,16},{1,33},{17,49},{33,1},{49,17},{2,34}... | collective-permute-start | bytes 1179656 | tf_op jit(solution)/shard_map/ppermute | solution.py:212
  59.1 2.5 %collective-permute-start.1 = (bf16[12,8,16,128]{3,2,1,0:T(8,128)(2,1)S(1)}, bf16[12,8,16,128]{3,2,1,0:T(8,128)(2,1)S(1)}, u32[]{:S(2)}, u32[]{:S(2)}) collective-permute-start(bf16[12,8,16,128]{3,2,1,0:T(8,128)(2,1)S(1)} %bitcast.28), channel_id=1, source_target_pairs={{0,16},{16,32},{32,48},{48,0},{1,17},{17,33},{33,49},{49,1},{2,18}... | collective-permute-start | bytes 1179656 | tf_op jit(solution)/shard_map/ppermute | solution.py:212
  61.6 8.8 %collective-permute-start = (bf16[12,8,16,128]{3,2,1,0:T(8,128)(2,1)S(1)}, bf16[12,8,16,128]{3,2,1,0:T(8,128)(2,1)S(1)}, u32[]{:S(2)}, u32[]{:S(2)}) collective-permute-start(bf16[12,8,16,128]{3,2,1,0:T(8,128)(2,1)S(1)} %bitcast.29), channel_id=1, source_target_pairs={{0,8},{8,0},{1,9},{9,1},{2,10},{10,2},{3,11},{11,3},{4,12},{12,4},... | collective-permute-start | bytes 1179656 | tf_op jit(solution)/shard_map/ppermute | solution.py:175
  70.4 0.0 collective-permute-done.5.refs_6_
  70.4 5.9 %collective-permute-start.6 = (bf16[12,8,16,128]{3,2,1,0:T(8,128)(2,1)S(1)}, bf16[12,8,16,128]{3,2,1,0:T(8,128)(2,1)S(1)}, u32[]{:S(2)}, u32[]{:S(2)}) collective-permute-start(bf16[12,8,16,128]{3,2,1,0:T(8,128)(2,1)S(1)} %collective-permute-done.5.refs_6_), channel_id=1, source_target_pairs={{0,8},{8,0},{1,9},{9,1},{2,10},{10,2},{3,11},{11,3},{4,12},{12,4},... | collective-permute-start | bytes 1179656 | tf_op jit(solution)/shard_map/ppermute | solution.py:175
  76.3 0.0 collective-permute-done.3.refs_4_
  76.3 1.9 %collective-permute-start.4 = (bf16[12,8,16,128]{3,2,1,0:T(8,128)(2,1)S(1)}, bf16[12,8,16,128]{3,2,1,0:T(8,128)(2,1)S(1)}, u32[]{:S(2)}, u32[]{:S(2)}) collective-permute-start(bf16[12,8,16,128]{3,2,1,0:T(8,128)(2,1)S(1)} %collective-permute-done.3.refs_4_), channel_id=1, source_target_pairs={{0,8},{8,0},{1,9},{9,1},{2,10},{10,2},{3,11},{11,3},{4,12},{12,4},... | collective-permute-start | bytes 1179656 | tf_op jit(solution)/shard_map/ppermute | solution.py:175
  78.2 0.0 collective-permute-done.1.refs_2_
  78.3 3.6 %collective-permute-start.2 = (bf16[12,8,16,128]{3,2,1,0:T(8,128)(2,1)S(1)}, bf16[12,8,16,128]{3,2,1,0:T(8,128)(2,1)S(1)}, u32[]{:S(2)}, u32[]{:S(2)}) collective-permute-start(bf16[12,8,16,128]{3,2,1,0:T(8,128)(2,1)S(1)} %collective-permute-done.1.refs_2_), channel_id=1, source_target_pairs={{0,8},{8,0},{1,9},{9,1},{2,10},{10,2},{3,11},{11,3},{4,12},{12,4},... | collective-permute-start | bytes 1179656 | tf_op jit(solution)/shard_map/ppermute | solution.py:175
  81.9 0.0 all-gather.4.cloned.1.call-done
  81.9 0.0 copy-start
  81.9 1.3 %copy-done = bf16[384,1536]{1,0:T(8,128)(2,1)S(1)} copy-done((bf16[384,1536]{1,0:T(8,128)(2,1)S(1)}, bf16[384,1536]{1,0:T(8,128)(2,1)}, u32[]{:S(2)}) %copy-start) | copy-done | bytes 1179672
  83.2 0.1 regroup.1.refs_8_
  83.3 0.0 collective-permute-done.refs_1_
  83.3 0.0 collective-permute-done.6.refs_7_
  83.3 0.0 collective-permute-done.4.refs_5_
  83.3 0.0 collective-permute-done.2.refs_3_
  83.3 2.6 %grads.1 = bf16[4,96,1536]{2,1,0:T(8,128)(2,1)S(1)} custom-call(s32[1]{0:T(128)} %bitcast.core_at, s32[1]{0:T(128)} %bitcast.1.x_at, s32[1]{0:T(128)} %bitcast.2.yo_at, bf16[12,8,16,128]{3,2,1,0:T(8,128)(2,1)S(1)} %bitcast.30, bf16[12,8,16,128]{3,2,1,0:T(8,128)(2,1)S(1)} %collective-permute-done.refs_1_, ...), custom_call_target="tpu_custom_call" | custom-call | tf_op jit(solution)/shard_map/grads/pallas_call | solution.py:224
  85.9 17.4 %all_to_all.10.parts = bf16[4,96,1536]{2,1,0:T(8,128)(2,1)S(1)} all-to-all(bf16[4,96,1536]{2,1,0:T(8,128)(2,1)S(1)} %grads.1), channel_id=1, replica_groups=mesh['zo'=6,'zi'=2,'x'=4,'core'=2,'yo'=4,'yi'=2] {'zi','yi'}, dimensions={0} | all-to-all | bytes 2359296 | tf_op jit(solution)/shard_map/all_to_all | solution.py:233
  103.4 1.3 %total.1 = (bf16[30,1440]{1,0:T(8,128)(2,1)}, bf16[30,1440]{1,0:T(8,128)(2,1)}, bf16[30,1440]{1,0:T(8,128)(2,1)}) custom-call(bf16[4,96,1536]{2,1,0:T(8,128)(2,1)S(1)} %all_to_all.10.parts), custom_call_target="tpu_custom_call" | custom-call | tf_op jit(solution)/shard_map/total/pallas_call | solution.py:234
Async XLA Ops:
  8.7 17.0 %all-to-all-start = ((bf16[16,16,128]{2,1,0:T(8,128)(2,1)}), bf16[16,16,128]{2,1,0:T(8,128)(2,1)S(1)}, u32[]{:S(2)}, u32[]{:S(2)}) async-start(bf16[16,16,128]{2,1,0:T(8,128)(2,1)} %bitcast.32), calls=%async_computation | async-start | bytes 131072 | tf_op jit(solution)/shard_map/all_to_all | solution.py:205
  18.3 63.7 %all-gather.4.cloned.1.call-start = ((), (), s32[]{:S(2)}) async-start(), calls=%async_computation.2 | async-start | bytes 1474560 | tf_op jit(solution)/shard_map/all_gather | solution.py:207
  52.2 18.2 %collective-permute-start.5 = (bf16[12,8,16,128]{3,2,1,0:T(8,128)(2,1)S(1)}, bf16[12,8,16,128]{3,2,1,0:T(8,128)(2,1)S(1)}, u32[]{:S(2)}, u32[]{:S(2)}) collective-permute-start(bf16[12,8,16,128]{3,2,1,0:T(8,128)(2,1)S(1)} %bitcast.26), channel_id=1, source_target_pairs={{0,48},{16,0},{32,16},{48,32},{1,49},{17,1},{33,17},{49,33},{2,50}... | collective-permute-start | bytes 1179656 | tf_op jit(solution)/shard_map/ppermute | solution.py:212
  56.6 19.7 %collective-permute-start.3 = (bf16[12,8,16,128]{3,2,1,0:T(8,128)(2,1)S(1)}, bf16[12,8,16,128]{3,2,1,0:T(8,128)(2,1)S(1)}, u32[]{:S(2)}, u32[]{:S(2)}) collective-permute-start(bf16[12,8,16,128]{3,2,1,0:T(8,128)(2,1)S(1)} %bitcast.27), channel_id=1, source_target_pairs={{0,32},{16,48},{32,0},{48,16},{1,33},{17,49},{33,1},{49,17},{2,34}... | collective-permute-start | bytes 1179656 | tf_op jit(solution)/shard_map/ppermute | solution.py:212
  59.1 19.2 %collective-permute-start.1 = (bf16[12,8,16,128]{3,2,1,0:T(8,128)(2,1)S(1)}, bf16[12,8,16,128]{3,2,1,0:T(8,128)(2,1)S(1)}, u32[]{:S(2)}, u32[]{:S(2)}) collective-permute-start(bf16[12,8,16,128]{3,2,1,0:T(8,128)(2,1)S(1)} %bitcast.28), channel_id=1, source_target_pairs={{0,16},{16,32},{32,48},{48,0},{1,17},{17,33},{33,49},{49,1},{2,18}... | collective-permute-start | bytes 1179656 | tf_op jit(solution)/shard_map/ppermute | solution.py:212
  61.6 21.7 %collective-permute-start = (bf16[12,8,16,128]{3,2,1,0:T(8,128)(2,1)S(1)}, bf16[12,8,16,128]{3,2,1,0:T(8,128)(2,1)S(1)}, u32[]{:S(2)}, u32[]{:S(2)}) collective-permute-start(bf16[12,8,16,128]{3,2,1,0:T(8,128)(2,1)S(1)} %bitcast.29), channel_id=1, source_target_pairs={{0,8},{8,0},{1,9},{9,1},{2,10},{10,2},{3,11},{11,3},{4,12},{12,4},... | collective-permute-start | bytes 1179656 | tf_op jit(solution)/shard_map/ppermute | solution.py:175
  70.4 12.9 %collective-permute-start.6 = (bf16[12,8,16,128]{3,2,1,0:T(8,128)(2,1)S(1)}, bf16[12,8,16,128]{3,2,1,0:T(8,128)(2,1)S(1)}, u32[]{:S(2)}, u32[]{:S(2)}) collective-permute-start(bf16[12,8,16,128]{3,2,1,0:T(8,128)(2,1)S(1)} %collective-permute-done.5.refs_6_), channel_id=1, source_target_pairs={{0,8},{8,0},{1,9},{9,1},{2,10},{10,2},{3,11},{11,3},{4,12},{12,4},... | collective-permute-start | bytes 1179656 | tf_op jit(solution)/shard_map/ppermute | solution.py:175
  76.3 7.0 %collective-permute-start.4 = (bf16[12,8,16,128]{3,2,1,0:T(8,128)(2,1)S(1)}, bf16[12,8,16,128]{3,2,1,0:T(8,128)(2,1)S(1)}, u32[]{:S(2)}, u32[]{:S(2)}) collective-permute-start(bf16[12,8,16,128]{3,2,1,0:T(8,128)(2,1)S(1)} %collective-permute-done.3.refs_4_), channel_id=1, source_target_pairs={{0,8},{8,0},{1,9},{9,1},{2,10},{10,2},{3,11},{11,3},{4,12},{12,4},... | collective-permute-start | bytes 1179656 | tf_op jit(solution)/shard_map/ppermute | solution.py:175
  78.3 5.1 %collective-permute-start.2 = (bf16[12,8,16,128]{3,2,1,0:T(8,128)(2,1)S(1)}, bf16[12,8,16,128]{3,2,1,0:T(8,128)(2,1)S(1)}, u32[]{:S(2)}, u32[]{:S(2)}) collective-permute-start(bf16[12,8,16,128]{3,2,1,0:T(8,128)(2,1)S(1)} %collective-permute-done.1.refs_2_), channel_id=1, source_target_pairs={{0,8},{8,0},{1,9},{9,1},{2,10},{10,2},{3,11},{11,3},{4,12},{12,4},... | collective-permute-start | bytes 1179656 | tf_op jit(solution)/shard_map/ppermute | solution.py:175
  81.9 1.3 %copy-start = (bf16[384,1536]{1,0:T(8,128)(2,1)S(1)}, bf16[384,1536]{1,0:T(8,128)(2,1)}, u32[]{:S(2)}) copy-start(bf16[384,1536]{1,0:T(8,128)(2,1)} %all-gather.4.cloned.1.call-done) | copy-start | bytes 3538948
Sparse Core Ops, SparseCore 0:
  25.8 42.1 all-gather.3

commit v10 on v6

--- a/solution.py
+++ b/solution.py
@@ -104,11 +104,11 @@
 
 
 def grads_kernel(core_at, x_at, yo_at, *refs):
-    blocks, (weights, out, inputs, cotangents) = refs[:-4], refs[-4:]
+    blocks, (weights, out, down, inputs, cotangents) = refs[:-5], refs[-5:]
     chips_x = len(blocks) // CORES
     chips_z, tokens_y, depth, lanes = blocks[0].shape
     wide = weights.shape[2]
-    groups, hidden = out.shape[0], out.shape[1] // 3
+    groups, hidden = down.shape[0], down.shape[1]
     core, x, yo = core_at[0], x_at[0], yo_at[0]
     lower = lax.broadcasted_iota(jnp.int32, (chips_z, depth, lanes), 2) < lanes // 2
     for k, ref in enumerate(blocks):
@@ -142,14 +142,19 @@
     upward = dot_t(jnp.concatenate([gate_term, linear_term], axis=0), rows).astype(BF16)
     grads = (upward[:units], upward[units:], dot_t(lifted, backs).astype(BF16))
     for k, grad in enumerate(grads):
-        out[:, k * hidden : (k + 1) * hidden, :] = grad.reshape(groups, hidden, wide)
-
-
-def total_kernel(parts, gate_g, up_g, down_g):
-    hidden = parts.shape[1] // 3
-    total = parts[0].astype(F32)
-    for j in range(1, parts.shape[0]):
-        total = total + parts[j].astype(F32)
+        target = down if k == 2 else out
+        target[:, k % 2 * hidden : (k % 2 + 1) * hidden, :] = grad.reshape(groups, hidden, wide)
+
+
+def total_kernel(first, second, gate_g, up_g, down_g):
+    hidden = second.shape[1]
+    totals = []
+    for parts in (first, second):
+        total = parts[0].astype(F32)
+        for j in range(1, parts.shape[0]):
+            total = total + parts[j].astype(F32)
+        totals.append(total)
+    total = jnp.concatenate(totals, axis=0)
     units, narrow = gate_g.shape
     slim = narrowed(total.astype(BF16), narrow).astype(F32)
     for k, ref in enumerate((gate_g, up_g, down_g)):
@@ -214,22 +219,22 @@
     )(weights)
     parts = pl.pallas_call(
         grads_kernel,
-        out_shape=jax.ShapeDtypeStruct((groups, 3 * hidden, wide), BF16),
+        out_shape=[jax.ShapeDtypeStruct((groups, k * hidden, wide), BF16) for k in (2, 1)],
         in_specs=[SMEM] * 3 + [VMEM] * (len(blocks) + 1),
-        out_specs=VMEM,
+        out_specs=[VMEM] * 2,
         scratch_shapes=[pltpu.VMEM((chips_z, chips_x * CORES, depth, pairs_y * LANES), BF16)] * 2,
         compiler_params=room(20),
         name="grads",
     )(*(lax.axis_index(axis).reshape(1) for axis in ("core", "x", "yo")), *blocks, regrouped)
-    met = lax.all_to_all(parts, GROUP, split_axis=0, concat_axis=0, tiled=True)
+    met = [lax.all_to_all(part, GROUP, split_axis=0, concat_axis=0, tiled=True) for part in parts]
     grad_gate, grad_up, grad_down = pl.pallas_call(
         total_kernel,
         out_shape=[jax.ShapeDtypeStruct((units, features), BF16)] * 3,
-        in_specs=[VMEM],
+        in_specs=[VMEM] * 2,
         out_specs=[VMEM] * 3,
         compiler_params=room(8),
         name="total",
-    )(met)
+    )(*met)
     return grad_gate.T[None], grad_up.T[None], grad_down[None]
 
 

time: 112 us -> 116 us (1.036)
  blocking collectives: 44 us -> 47.3 us
    all_to_all x1 -> x2, blocking collectives: 17.5 us -> 20.7 us  [shards(): lax.all_to_all(part, GROUP, split_axis=0, concat_axis=0, tiled=True)]
where the time goes in v10:
time: 116 us; the launch traced here: 115 us
  blocking collectives  47.3 us (41%)
  starting transfers between devices  39.2 us (34%)
  between operations  14.2 us (12%)
  Pallas kernels  7.44 us (6%)
  waiting for transfers between devices  5.36 us (5%)
  local copies, waits for them, and re-layouts  1.26 us (1%)
    all_gather x1, blocking collectives, shards(): lax.all_gather(quarter, 'zo').reshape(chips_z, pairs_y * PAIR, depth, LANES)  26.6 us
    all_to_all x2, blocking collectives, shards(): lax.all_to_all(part, GROUP, split_axis=0, concat_axis=0, tiled=True)  20.7 us
    ppermute x4, starting transfers between devices, swap(): return lax.ppermute(value, axis, [(0, 1), (1, 0)])  20.2 us
    all_to_all x1, starting transfers between devices, shards(): lax.all_to_all(sent, ('zi',) + EP, split_axis=0, concat_axis=0, tiled=True)  9.56 us
    ppermute x3, starting transfers between devices, shards(): block = lax.ppermute(along_z, 'x', along) if steps else along_z  9.32 us
    all_to_all x1, waiting for transfers between devices, shards(): lax.all_to_all(sent, ('zi',) + EP, split_axis=0, concat_axis=0, tiled=True)  5.31 us
    pallas_call x1, Pallas kernels, shards(): pl.pallas_call(grads_kernel, out_shape=[jax.ShapeDtypeStruct((groups, k *...  2.6 us
  transfers between devices with their start and end apart: 9, of which 1 were waited for; matrix products, arithmetic and copies ran while one was open for 0% of the time, Pallas kernels for 2%

profile of v10, /device:TPU:1, one launch (start us, length us, event | category | flops | bytes accessed | tf_op | source)
XLA Modules:
  0.0 114.7 jit_solution(11398791612841585219)
XLA Ops:
  7.2 1.5 %pack.1 = bf16[2,4,2,16,128]{4,3,2,1,0:T(8,128)(2,1)} custom-call(s32[1]{0:T(128)} %bitcast.3.zone, s32[1]{0:T(128)} %bitcast.4.yi, bf16[15,256]{1,0:T(8,128)(2,1)} %bitcast.36, bf16[15,256]{1,0:T(8,128)(2,1)} %bitcast.37, s32[4,256]{1,0:T(4,128)} %bitcast.38, f32[4,256]{1,0:T(4,128)} %bitcast.39), custom_call_target="tpu_custom_call" | custom-call | tf_op jit(solution)/shard_map/pack/pallas_call | solution.py:186
  8.6 9.6 %all-to-all-start = ((bf16[16,16,128]{2,1,0:T(8,128)(2,1)}), bf16[16,16,128]{2,1,0:T(8,128)(2,1)S(1)}, u32[]{:S(2)}, u32[]{:S(2)}) async-start(bf16[16,16,128]{2,1,0:T(8,128)(2,1)} %bitcast.32), calls=%async_computation | async-start | bytes 131072 | tf_op jit(solution)/shard_map/all_to_all | solution.py:201
  18.2 0.0 all-gather.4.cloned.1.call-start
  18.3 2.0 %widen_weights.1 = bf16[96,1536]{1,0:T(8,128)(2,1)} custom-call(bf16[30,1440]{1,0:T(8,128)(2,1)} %bitcast.33, bf16[30,1440]{1,0:T(8,128)(2,1)} %bitcast.34, bf16[30,1440]{1,0:T(8,128)(2,1)} %bitcast.35), custom_call_target="tpu_custom_call" | custom-call | tf_op jit(solution)/shard_map/widen_weights/pallas_call | solution.py:193
  20.3 5.3 %all-to-all-done = bf16[16,16,128]{2,1,0:T(8,128)(2,1)S(1)} async-done(((bf16[16,16,128]{2,1,0:T(8,128)(2,1)}), bf16[16,16,128]{2,1,0:T(8,128)(2,1)S(1)}, u32[]{:S(2)}, u32[]{:S(2)}) %all-to-all-start) | async-done | bytes 65568 | tf_op jit(solution)/shard_map/all_to_all | solution.py:201
  25.6 0.0 all-gather.4.cloned.1.call-update
  25.6 26.6 %all-gather = bf16[96,16,128]{2,1,0:T(8,128)(2,1)S(1)} all-gather(bf16[16,16,128]{2,1,0:T(8,128)(2,1)S(1)} %all-to-all-done), channel_id=2, replica_groups=mesh['zo'=6,'zi'=2,'x'=4,'core'=2,'yo'=4,'yi'=2] {'zo'}, dimensions={0}, use_global_device_ids=true | all-gather | bytes 458752 | tf_op jit(solution)/shard_map/all_gather | solution.py:204
  52.2 4.4 %collective-permute-start.5 = (bf16[12,8,16,128]{3,2,1,0:T(8,128)(2,1)S(1)}, bf16[12,8,16,128]{3,2,1,0:T(8,128)(2,1)S(1)}, u32[]{:S(2)}, u32[]{:S(2)}) collective-permute-start(bf16[12,8,16,128]{3,2,1,0:T(8,128)(2,1)S(1)} %bitcast.26), channel_id=1, source_target_pairs={{0,48},{16,0},{32,16},{48,32},{1,49},{17,1},{33,17},{49,33},{2,50}... | collective-permute-start | bytes 1179656 | tf_op jit(solution)/shard_map/ppermute | solution.py:208
  56.6 2.4 %collective-permute-start.3 = (bf16[12,8,16,128]{3,2,1,0:T(8,128)(2,1)S(1)}, bf16[12,8,16,128]{3,2,1,0:T(8,128)(2,1)S(1)}, u32[]{:S(2)}, u32[]{:S(2)}) collective-permute-start(bf16[12,8,16,128]{3,2,1,0:T(8,128)(2,1)S(1)} %bitcast.27), channel_id=1, source_target_pairs={{0,32},{16,48},{32,0},{48,16},{1,33},{17,49},{33,1},{49,17},{2,34}... | collective-permute-start | bytes 1179656 | tf_op jit(solution)/shard_map/ppermute | solution.py:208
  59.0 2.5 %collective-permute-start.1 = (bf16[12,8,16,128]{3,2,1,0:T(8,128)(2,1)S(1)}, bf16[12,8,16,128]{3,2,1,0:T(8,128)(2,1)S(1)}, u32[]{:S(2)}, u32[]{:S(2)}) collective-permute-start(bf16[12,8,16,128]{3,2,1,0:T(8,128)(2,1)S(1)} %bitcast.28), channel_id=1, source_target_pairs={{0,16},{16,32},{32,48},{48,0},{1,17},{17,33},{33,49},{49,1},{2,18}... | collective-permute-start | bytes 1179656 | tf_op jit(solution)/shard_map/ppermute | solution.py:208
  61.5 8.8 %collective-permute-start = (bf16[12,8,16,128]{3,2,1,0:T(8,128)(2,1)S(1)}, bf16[12,8,16,128]{3,2,1,0:T(8,128)(2,1)S(1)}, u32[]{:S(2)}, u32[]{:S(2)}) collective-permute-start(bf16[12,8,16,128]{3,2,1,0:T(8,128)(2,1)S(1)} %bitcast.29), channel_id=1, source_target_pairs={{0,8},{8,0},{1,9},{9,1},{2,10},{10,2},{3,11},{11,3},{4,12},{12,4},... | collective-permute-start | bytes 1179656 | tf_op jit(solution)/shard_map/ppermute | solution.py:173
  70.4 0.0 collective-permute-done.5.refs_6_
  70.4 5.9 %collective-permute-start.6 = (bf16[12,8,16,128]{3,2,1,0:T(8,128)(2,1)S(1)}, bf16[12,8,16,128]{3,2,1,0:T(8,128)(2,1)S(1)}, u32[]{:S(2)}, u32[]{:S(2)}) collective-permute-start(bf16[12,8,16,128]{3,2,1,0:T(8,128)(2,1)S(1)} %collective-permute-done.5.refs_6_), channel_id=1, source_target_pairs={{0,8},{8,0},{1,9},{9,1},{2,10},{10,2},{3,11},{11,3},{4,12},{12,4},... | collective-permute-start | bytes 1179656 | tf_op jit(solution)/shard_map/ppermute | solution.py:173
  76.3 0.0 collective-permute-done.3.refs_4_
  76.3 1.9 %collective-permute-start.4 = (bf16[12,8,16,128]{3,2,1,0:T(8,128)(2,1)S(1)}, bf16[12,8,16,128]{3,2,1,0:T(8,128)(2,1)S(1)}, u32[]{:S(2)}, u32[]{:S(2)}) collective-permute-start(bf16[12,8,16,128]{3,2,1,0:T(8,128)(2,1)S(1)} %collective-permute-done.3.refs_4_), channel_id=1, source_target_pairs={{0,8},{8,0},{1,9},{9,1},{2,10},{10,2},{3,11},{11,3},{4,12},{12,4},... | collective-permute-start | bytes 1179656 | tf_op jit(solution)/shard_map/ppermute | solution.py:173
  78.2 0.0 collective-permute-done.1.refs_2_
  78.2 3.6 %collective-permute-start.2 = (bf16[12,8,16,128]{3,2,1,0:T(8,128)(2,1)S(1)}, bf16[12,8,16,128]{3,2,1,0:T(8,128)(2,1)S(1)}, u32[]{:S(2)}, u32[]{:S(2)}) collective-permute-start(bf16[12,8,16,128]{3,2,1,0:T(8,128)(2,1)S(1)} %collective-permute-done.1.refs_2_), channel_id=1, source_target_pairs={{0,8},{8,0},{1,9},{9,1},{2,10},{10,2},{3,11},{11,3},{4,12},{12,4},... | collective-permute-start | bytes 1179656 | tf_op jit(solution)/shard_map/ppermute | solution.py:173
  81.8 0.0 all-gather.4.cloned.1.call-done
  81.9 0.0 copy-start
  81.9 1.3 %copy-done = bf16[384,1536]{1,0:T(8,128)(2,1)S(1)} copy-done((bf16[384,1536]{1,0:T(8,128)(2,1)S(1)}, bf16[384,1536]{1,0:T(8,128)(2,1)}, u32[]{:S(2)}) %copy-start) | copy-done | bytes 1179672
  83.1 0.1 regroup.1.refs_8_
  83.2 0.0 collective-permute-done.refs_1_
  83.2 0.0 collective-permute-done.6.refs_7_
  83.3 0.0 collective-permute-done.4.refs_5_
  83.3 0.0 collective-permute-done.2.refs_3_
  83.3 2.6 %grads.1 = (bf16[4,64,1536]{2,1,0:T(8,128)(2,1)S(1)}, bf16[4,32,1536]{2,1,0:T(8,128)(2,1)S(1)}) custom-call(s32[1]{0:T(128)} %bitcast.core_at, s32[1]{0:T(128)} %bitcast.1.x_at, s32[1]{0:T(128)} %bitcast.2.yo_at, bf16[12,8,16,128]{3,2,1,0:T(8,128)(2,1)S(1)} %bitcast.30, bf16[12,8,16,128]{3,2,1,0:T(8,128)(2,1)S(1)} %collective-permute-done.refs_1_, ...), custom_call_target="tpu_custom_call" | custom-call | tf_op jit(solution)/shard_map/grads/pallas_call | solution.py:220
  85.9 9.0 %all_to_all.15.second = bf16[4,32,1536]{2,1,0:T(8,128)(2,1)S(1)} all-to-all(bf16[4,32,1536]{2,1,0:T(8,128)(2,1)S(1)} %get-tuple-element.13), channel_id=1, replica_groups=mesh['zo'=6,'zi'=2,'x'=4,'core'=2,'yo'=4,'yi'=2] {'zi','yi'}, dimensions={0} | all-to-all | bytes 786432 | tf_op jit(solution)/shard_map/all_to_all | solution.py:229
  94.9 11.7 %all_to_all.16.first = bf16[4,64,1536]{2,1,0:T(8,128)(2,1)S(1)} all-to-all(bf16[4,64,1536]{2,1,0:T(8,128)(2,1)S(1)} %get-tuple-element.12), channel_id=1, replica_groups=mesh['zo'=6,'zi'=2,'x'=4,'core'=2,'yo'=4,'yi'=2] {'zi','yi'}, dimensions={0} | all-to-all | bytes 1572864 | tf_op jit(solution)/shard_map/all_to_all | solution.py:229
  106.6 1.3 %total.1 = (bf16[30,1440]{1,0:T(8,128)(2,1)}, bf16[30,1440]{1,0:T(8,128)(2,1)}, bf16[30,1440]{1,0:T(8,128)(2,1)}) custom-call(bf16[4,64,1536]{2,1,0:T(8,128)(2,1)S(1)} %all_to_all.16.first, bf16[4,32,1536]{2,1,0:T(8,128)(2,1)S(1)} %all_to_all.15.second), custom_call_target="tpu_custom_call" | custom-call | tf_op jit(solution)/shard_map/total/pallas_call | solution.py:230
Async XLA Ops:
  8.6 16.9 %all-to-all-start = ((bf16[16,16,128]{2,1,0:T(8,128)(2,1)}), bf16[16,16,128]{2,1,0:T(8,128)(2,1)S(1)}, u32[]{:S(2)}, u32[]{:S(2)}) async-start(bf16[16,16,128]{2,1,0:T(8,128)(2,1)} %bitcast.32), calls=%async_computation | async-start | bytes 131072 | tf_op jit(solution)/shard_map/all_to_all | solution.py:201
  18.2 63.7 %all-gather.4.cloned.1.call-start = ((), (), s32[]{:S(2)}) async-start(), calls=%async_computation.3 | async-start | bytes 1474560 | tf_op jit(solution)/shard_map/all_gather | solution.py:203
  52.2 18.2 %collective-permute-start.5 = (bf16[12,8,16,128]{3,2,1,0:T(8,128)(2,1)S(1)}, bf16[12,8,16,128]{3,2,1,0:T(8,128)(2,1)S(1)}, u32[]{:S(2)}, u32[]{:S(2)}) collective-permute-start(bf16[12,8,16,128]{3,2,1,0:T(8,128)(2,1)S(1)} %bitcast.26), channel_id=1, source_target_pairs={{0,48},{16,0},{32,16},{48,32},{1,49},{17,1},{33,17},{49,33},{2,50}... | collective-permute-start | bytes 1179656 | tf_op jit(solution)/shard_map/ppermute | solution.py:208
  56.6 19.7 %collective-permute-start.3 = (bf16[12,8,16,128]{3,2,1,0:T(8,128)(2,1)S(1)}, bf16[12,8,16,128]{3,2,1,0:T(8,128)(2,1)S(1)}, u32[]{:S(2)}, u32[]{:S(2)}) collective-permute-start(bf16[12,8,16,128]{3,2,1,0:T(8,128)(2,1)S(1)} %bitcast.27), channel_id=1, source_target_pairs={{0,32},{16,48},{32,0},{48,16},{1,33},{17,49},{33,1},{49,17},{2,34}... | collective-permute-start | bytes 1179656 | tf_op jit(solution)/shard_map/ppermute | solution.py:208
  59.0 19.2 %collective-permute-start.1 = (bf16[12,8,16,128]{3,2,1,0:T(8,128)(2,1)S(1)}, bf16[12,8,16,128]{3,2,1,0:T(8,128)(2,1)S(1)}, u32[]{:S(2)}, u32[]{:S(2)}) collective-permute-start(bf16[12,8,16,128]{3,2,1,0:T(8,128)(2,1)S(1)} %bitcast.28), channel_id=1, source_target_pairs={{0,16},{16,32},{32,48},{48,0},{1,17},{17,33},{33,49},{49,1},{2,18}... | collective-permute-start | bytes 1179656 | tf_op jit(solution)/shard_map/ppermute | solution.py:208
  61.5 21.7 %collective-permute-start = (bf16[12,8,16,128]{3,2,1,0:T(8,128)(2,1)S(1)}, bf16[12,8,16,128]{3,2,1,0:T(8,128)(2,1)S(1)}, u32[]{:S(2)}, u32[]{:S(2)}) collective-permute-start(bf16[12,8,16,128]{3,2,1,0:T(8,128)(2,1)S(1)} %bitcast.29), channel_id=1, source_target_pairs={{0,8},{8,0},{1,9},{9,1},{2,10},{10,2},{3,11},{11,3},{4,12},{12,4},... | collective-permute-start | bytes 1179656 | tf_op jit(solution)/shard_map/ppermute | solution.py:173
  70.4 12.9 %collective-permute-start.6 = (bf16[12,8,16,128]{3,2,1,0:T(8,128)(2,1)S(1)}, bf16[12,8,16,128]{3,2,1,0:T(8,128)(2,1)S(1)}, u32[]{:S(2)}, u32[]{:S(2)}) collective-permute-start(bf16[12,8,16,128]{3,2,1,0:T(8,128)(2,1)S(1)} %collective-permute-done.5.refs_6_), channel_id=1, source_target_pairs={{0,8},{8,0},{1,9},{9,1},{2,10},{10,2},{3,11},{11,3},{4,12},{12,4},... | collective-permute-start | bytes 1179656 | tf_op jit(solution)/shard_map/ppermute | solution.py:173
  76.3 7.0 %collective-permute-start.4 = (bf16[12,8,16,128]{3,2,1,0:T(8,128)(2,1)S(1)}, bf16[12,8,16,128]{3,2,1,0:T(8,128)(2,1)S(1)}, u32[]{:S(2)}, u32[]{:S(2)}) collective-permute-start(bf16[12,8,16,128]{3,2,1,0:T(8,128)(2,1)S(1)} %collective-permute-done.3.refs_4_), channel_id=1, source_target_pairs={{0,8},{8,0},{1,9},{9,1},{2,10},{10,2},{3,11},{11,3},{4,12},{12,4},... | collective-permute-start | bytes 1179656 | tf_op jit(solution)/shard_map/ppermute | solution.py:173
  78.2 5.1 %collective-permute-start.2 = (bf16[12,8,16,128]{3,2,1,0:T(8,128)(2,1)S(1)}, bf16[12,8,16,128]{3,2,1,0:T(8,128)(2,1)S(1)}, u32[]{:S(2)}, u32[]{:S(2)}) collective-permute-start(bf16[12,8,16,128]{3,2,1,0:T(8,128)(2,1)S(1)} %collective-permute-done.1.refs_2_), channel_id=1, source_target_pairs={{0,8},{8,0},{1,9},{9,1},{2,10},{10,2},{3,11},{11,3},{4,12},{12,4},... | collective-permute-start | bytes 1179656 | tf_op jit(solution)/shard_map/ppermute | solution.py:173
  81.9 1.3 %copy-start = (bf16[384,1536]{1,0:T(8,128)(2,1)S(1)}, bf16[384,1536]{1,0:T(8,128)(2,1)}, u32[]{:S(2)}) copy-start(bf16[384,1536]{1,0:T(8,128)(2,1)} %all-gather.4.cloned.1.call-done) | copy-start | bytes 3538948
Sparse Core Ops, SparseCore 0:
  25.7 42.1 all-gather.3
